TPU v7x, 32 devices: a whole 2x2x4 slice. The times are simulated.
32 devices in a mesh: groups: 2 (over y), pts: 4 (over z), mem: 4 (over x, core).
Axes of the slice: x: 2, y: 2, z: 4, core: 2. Of those that a mesh axis runs over, the one named last changes fastest.
Arguments:
- latents: bfloat16 [16, 8192, 512], P('mem', ('groups', 'pts')), parts along dimension 1, may hold values from -6 to 6
- member_seeds: int32 [32], P(('groups', 'mem')), parts along dimension 0, may hold values from 1 to 65520
- targets: float32 [8192, 128], P(('groups', 'pts')), parts along dimension 0, may hold values from -12 to 12
- lat_row: int32 [8192], P(('groups', 'pts')), parts along dimension 0, may hold values from 0 to 639
- weight_in: bfloat16 [512, 512], replicated, may hold values from -0.25 to 0.25
- bias_in: float32 [512], replicated, may hold values from -3 to 3
- weight_out: bfloat16 [512, 128], replicated, may hold values from -0.25 to 0.25
Outputs:
- grad_w_in: float32 [1024, 512], P(('groups', 'pts', 'mem')), parts along dimension 0
- grad_w_out: float32 [1024, 128], P(('groups', 'pts', 'mem')), parts along dimension 0
- grad_b_in: float32 [1024], P(('groups', 'pts', 'mem')), parts along dimension 0
There are 2 independent parts, one for each index of `groups`. A program takes and returns all parts, laid end to end along the dimension named above; an argument that names none is the same for every part. Nothing has to cross between parts.
All inputs are finite; a program needn't handle non-finite values.
Results may differ from a plain program's by a relative error of at most 0.0019.
Values may be sent and summed in bfloat16 or wider, within the bound.
No kernel may reach another device: no remote copies, remote signals or barrier semaphores. Data moves between devices by JAX's collectives and lax.ppermute only.
A program may use at most 64 MiB of HBM per device.

v0:
```python
from functools import partial
import math

import jax
import jax.numpy as jnp
from jax import lax
from jax.sharding import PartitionSpec as P

LAT_ROWS = 640
LOSS_SCALE = 256


EPSILON = 0.0001


def member_noise_of(member_seeds, width):
    channel = jnp.arange(width, dtype=jnp.int32)
    mixed_int = member_seeds[:, None] * (37 * channel[None, :] + 11) + 7 * channel[None, :]
    return ((mixed_int % 65521).astype(jnp.float32) / 65521.0 - 0.5) * 2.0


def area_of(lat_row, rows_total):
    return jnp.cos(jnp.pi * (lat_row.astype(jnp.float32) + 0.5) / rows_total - jnp.pi / 2)


def finish_gradient(values, targets, area_weight, pair_term, loss_coef, count):
    to_target = values - targets[None]
    spread = jnp.sqrt(jnp.sum(to_target * to_target, axis=-1) + EPSILON)
    member_grad = (
        loss_coef
        * area_weight[None, :, None]
        * (to_target / (count * spread[..., None]) - pair_term / (count * (count - 1)))
    )
    return member_grad.astype(jnp.bfloat16)


def pair_weights(values, others, values_low, others_low, off_diag):
    own_sq = jnp.sum(values * values, axis=-1)
    other_sq = jnp.sum(others * others, axis=-1)
    gram = jnp.einsum("mpv,kpv->mkp", values_low, others_low, preferred_element_type=jnp.float32)
    dist_sq = jnp.maximum(own_sq[:, None, :] + other_sq[None, :, :] - 2.0 * gram, 0.0)
    pair_dist = jnp.sqrt(dist_sq + EPSILON)
    return off_diag[:, :, None] / pair_dist


def pair_sum(values, others, pair_weight):
    weighted = jnp.einsum("mkp,kpv->mpv", pair_weight, others, precision=lax.Precision.HIGHEST)
    return values * jnp.sum(pair_weight, axis=1)[..., None] - weighted


def block_gradient(outputs, targets, area_weight, loss_coef, count):
    values = outputs.astype(jnp.float32)
    off_diag = 1.0 - jnp.eye(count, dtype=jnp.float32)
    pair_weight = pair_weights(values, values, outputs, outputs, off_diag)
    pair_term = pair_sum(values, values, pair_weight)
    return finish_gradient(values, targets, area_weight, pair_term, loss_coef, count)


def local(latents, member_seeds, targets, lat_row, weight_in, bias_in, weight_out):
    local_members = latents.shape[0]
    local_points = latents.shape[1]
    members = local_members * lax.axis_size("mem")
    points_total = local_points * lax.axis_size("pts")
    loss_coef = LOSS_SCALE / math.sqrt(points_total)
    member_noise = member_noise_of(member_seeds, weight_in.shape[1])
    area_weight = area_of(lat_row, LAT_ROWS)
    preact = jnp.einsum("mpd,dh->mph", latents, weight_in, preferred_element_type=jnp.float32)
    preact = preact + bias_in[None, None, :] + member_noise[:, None, :]
    hidden = jax.nn.gelu(preact, approximate=True).astype(jnp.bfloat16)
    outputs = jnp.einsum(
        "mph,hv->mpv", hidden, weight_out, preferred_element_type=jnp.float32
    ).astype(jnp.bfloat16)
    grouped = lax.all_to_all(outputs, "mem", split_axis=1, concat_axis=0, tiled=True)
    part_rows = grouped.shape[1]
    first_row = lax.axis_index("mem") * part_rows
    target_part = lax.dynamic_slice_in_dim(targets, first_row, part_rows, 0)
    area_part = lax.dynamic_slice_in_dim(area_weight, first_row, part_rows, 0)
    grouped_grad = block_gradient(grouped, target_part, area_part, loss_coef, members)
    member_grad = lax.all_to_all(grouped_grad, "mem", split_axis=0, concat_axis=1, tiled=True)
    grad_out = jnp.einsum("mph,mpv->hv", hidden, member_grad, preferred_element_type=jnp.float32)
    hidden_grad = jnp.einsum(
        "mpv,hv->mph", member_grad, weight_out, preferred_element_type=jnp.float32
    )
    pre_grad = jax.vjp(partial(jax.nn.gelu, approximate=True), preact)[1](hidden_grad)[0]
    grad_bias = jnp.sum(pre_grad, axis=(0, 1))
    pre_grad_low = pre_grad.astype(jnp.bfloat16)
    out_share = lax.psum_scatter(grad_out, ("pts", "mem"), scatter_dimension=0, tiled=True)
    grad_in = jnp.einsum("mpd,mph->dh", latents, pre_grad_low, preferred_element_type=jnp.float32)
    in_share, bias_share = (
        lax.psum_scatter(grad_in, ("pts", "mem"), scatter_dimension=0, tiled=True),
        lax.psum_scatter(grad_bias, ("pts", "mem"), scatter_dimension=0, tiled=True),
    )
    return (in_share, out_share, bias_share)


def solution(mesh):
    return jax.shard_map(
        local,
        mesh=mesh,
        in_specs=(
            P("mem", ("groups", "pts"), None),
            P(("groups", "mem")),
            P(("groups", "pts"), None),
            P(("groups", "pts")),
            P(),
            P(),
            P(),
        ),
        out_specs=(
            P(("groups", "pts", "mem"), None),
            P(("groups", "pts", "mem"), None),
            P(("groups", "pts", "mem")),
        ),
        check_vma=False,
    )
```

profile of v0, /device:TPU:0, one launch (start us, length us, event | category | flops | bytes accessed | tf_op | source)
XLA Modules:
  0.0 196.9 jit_solution(1724625529899960064)
XLA Ops:
  7.2 0.0 copy-start
  7.2 0.8 fusion.31
  8.0 0.2 copy-done
  8.2 0.0 copy-start.4
  8.2 8.1 %multiply_convert_fusion = (bf16[4,1024,512]{2,1,0:T(8,128)(2,1)S(1)}, f32[4,1024,512]{2,1,0:T(8,128)}) fusion(f32[4,512]{1,0:T(4,128)S(1)} %fusion.31, f32[512]{0:T(512)} %param.12, bf16[4,1024,512]{2,1,0:T(8,128)(2,1)} %param.7, bf16[512,512]{1,0:T(8,128)(2,1)S(1)} %copy-done), kind=kOutput, calls=%fused_computation.8 | convolution fusion | flops 2170552320 | bytes 17311744 | tf_op jit(solution)/shard_map/mpd,dh->mph/dot_general | solution.py:67
  16.4 0.0 copy-start.1
  16.4 2.0 copy-done.1
  18.4 0.0 copy-done.4
  18.4 1.3 convolution_convert_fusion
  19.6 1.8 copy.52
  21.5 4.2 %all-to-all-start = ((bf16[4,1024,128]{2,0,1:T(4,128)(2,1)}), bf16[4,1024,128]{2,0,1:T(4,128)(2,1)S(1)}, u32[]{:S(2)}, u32[]{:S(2)}) async-start(bf16[4,1024,128]{2,0,1:T(4,128)(2,1)} %copy.52), calls=%async_computation | async-start | bytes 2097152 | tf_op jit(solution)/shard_map/all_to_all | solution.py:73
  25.7 0.0 reduce-scatter.5.cloned.1.call-start
  25.7 0.0 copy-done.5
  25.7 0.1 dynamic-slice_multiply_fusion
  25.8 0.9 constant_dynamic-slice_fusion
  26.7 13.4 %all-to-all-done = bf16[4,1024,128]{2,0,1:T(4,128)(2,1)S(1)} async-done(((bf16[4,1024,128]{2,0,1:T(4,128)(2,1)}), bf16[4,1024,128]{2,0,1:T(4,128)(2,1)S(1)}, u32[]{:S(2)}, u32[]{:S(2)}) %all-to-all-start) | async-done | bytes 1048608 | tf_op jit(solution)/shard_map/all_to_all | solution.py:73
  40.1 0.2 copy.75
  40.3 1.2 fusion.14
  41.5 0.8 copy.54
  42.3 2.0 %fusion.38 = f32[256,16,16]{2,1,0:T(8,128)} fusion(bf16[16,256,128]{2,0,1:T(8,128)(2,1)S(1)} %bitcast.61), kind=kOutput, calls=%fused_computation.57 | convolution fusion | flops 16777216 | bytes 1310720 | tf_op jit(solution)/shard_map/mpv,kpv->mkp/dot_general | solution.py:40
  44.4 2.6 %copy.58 = f32[256,16,16]{0,1,2:T(8,128)S(1)} copy(f32[256,16,16]{2,1,0:T(8,128)} %fusion.38) | data formatting | bytes 524288 | tf_op jit(solution)/shard_map/mpv,kpv->mkp/dot_general | solution.py:40
  46.9 0.1 fusion.35
  47.1 2.5 %copy.60 = f32[16,16,256]{1,0,2:T(8,128)} copy(f32[16,16,256]{2,1,0:T(8,128)S(1)} %get-tuple-element.21) | data formatting | bytes 524288 | tf_op jit(solution)/shard_map/div | solution.py:43
  49.5 0.1 copy.59
  49.7 0.1 copy.56
  49.8 3.8 %fusion.16 = bf16[16,256,128]{2,0,1:T(8,128)(2,1)S(1)} fusion(bf16[16,256,128]{2,0,1:T(8,128)(2,1)S(1)} %bitcast.62, f32[16,16,256]{1,0,2:T(8,128)} %copy.60, f32[16,256]{0,1:T(8,128)S(1)} %copy.59, f32[16,256]{0,1:T(8,128)S(1)} %copy.56, f32[256,128]{1,0:T(8,128)S(1)} %constant_dynamic-slice_fusion, f32[256]{0:T(256)S(1)} %dynamic-slice_multiply_fusion), kind=kOutput, calls=%fused_computation.24 | convolution fusion | flops 105381888 | bytes 2524160 | tf_op jit(solution)/shard_map/mkp,kpv->mpv/dot_general | solution.py:47
  53.7 0.0 copy-start.6
  53.7 0.3 copy.61
  53.9 16.9 %all_to_all.36 = bf16[16,256,128]{2,1,0:T(8,128)(2,1)S(1)} all-to-all(bf16[16,256,128]{2,1,0:T(8,128)(2,1)S(1)} %copy.61), channel_id=1, replica_groups=mesh['groups'=2,'pts'=4,'mem'=4] {'mem'}, dimensions={0} | all-to-all | bytes 2097152 | tf_op jit(solution)/shard_map/all_to_all | solution.py:79
  70.8 0.1 copy.62
  70.9 0.0 copy-done.2
  70.9 2.0 %convolution_bitcast_fusion = f32[512,128]{1,0:T(8,128)} fusion(bf16[4,1024,512]{2,1,0:T(8,128)(2,1)S(1)} %copy-done.2, bf16[4,1024,128]{2,1,0:T(8,128)(2,1)S(1)} %bitcast.65), kind=kOutput, calls=%fused_computation.27 | convolution fusion | flops 536870912 | bytes 5505024 | tf_op jit(solution)/shard_map/mph,mpv->hv/dot_general | solution.py:80
  73.0 0.0 reduce-scatter.5.cloned.1.call-update
  73.0 0.0 reduce-scatter.7.cloned.1.call-start
  73.0 0.0 copy-done.6
  73.0 0.0 copy-start.3
  73.1 9.1 %fusion.37 = (f32[512]{0:T(512)S(1)}, bf16[4,1024,512]{2,1,0:T(8,128)(2,1)S(1)}) fusion(f32[4,512]{1,0:T(4,128)S(1)} %fusion.31, f32[4,1024,512]{2,1,0:T(8,128)} %get-tuple-element.23, f32[512]{0:T(512)S(1)} %copy-done.6, bf16[4,1024,128]{2,1,0:T(8,128)(2,1)S(1)} %bitcast.66, bf16[512,128]{1,0:T(8,128)(2,1)S(1)} %copy-done.4), kind=kOutput, calls=%fused_computation.56 | convolution fusion | flops 585104896 | bytes 13774848 | tf_op jit(solution)/shard_map/mpv,hv->mph/dot_general | solution.py:81
  82.2 0.0 copy-start.7
  82.2 0.0 copy-done.3
  82.2 2.3 %fusion.17 = f32[512,512]{0,1:T(8,128)S(1)} fusion(bf16[4,1024,512]{2,1,0:T(8,128)(2,1)S(1)} %copy-done.3, bf16[4,1024,512]{2,1,0:T(8,128)(2,1)S(1)} %get-tuple-element.25), kind=kOutput, calls=%fused_computation.26 | convolution fusion | flops 2147483648 | bytes 9437184 | tf_op jit(solution)/shard_map/mpd,mph->dh/dot_general | solution.py:88
  84.5 1.3 copy.68
  85.9 0.0 reduce-scatter.7.cloned.1.call-update
  85.9 0.0 copy-done.7
  85.9 0.6 dynamic-slice
  87.1 33.1 %all-reduce = f32[512]{0:T(512)S(1)} all-reduce(f32[512]{0:T(512)S(1)} %get-tuple-element.24), channel_id=4, replica_groups=mesh['groups'=2,'pts'=4,'mem'=4] {'pts','mem'}, use_global_device_ids=true, to_apply=%region_6.7.clone | all-reduce | flops 512 | bytes 4096
  120.2 0.6 dynamic-slice.1
  120.8 8.7 %reduce-scatter.5.cloned.1.call-done = f32[32,128]{1,0:T(8,128)} async-done(((f32[512,128]{1,0:T(8,128)}), f32[32,128]{1,0:T(8,128)}) %reduce-scatter.5.cloned.1.call-update) | async-done | bytes 16400 | tf_op jit(solution)/shard_map/reduce_scatter | solution.py:87
  129.5 60.6 %reduce-scatter.7.cloned.1.call-done = f32[32,512]{1,0:T(8,128)} async-done(((f32[512,512]{1,0:T(8,128)}), f32[32,512]{1,0:T(8,128)}) %reduce-scatter.7.cloned.1.call-update) | async-done | bytes 65552
  (10 shorter events, 0.1 us)
Async XLA Ops:
  7.2 1.1 copy-start
  8.2 10.1 %copy-start.4 = (bf16[512,128]{1,0:T(8,128)(2,1)S(1)}, bf16[512,128]{1,0:T(8,128)(2,1)}, u32[]{:S(2)}) copy-start(bf16[512,128]{1,0:T(8,128)(2,1)} %param.13) | copy-start | bytes 393220
  16.4 2.0 %copy-start.1 = (bf16[4,1024,512]{2,1,0:T(8,128)(2,1)}, bf16[4,1024,512]{2,1,0:T(8,128)(2,1)S(1)}, u32[]{:S(2)}) copy-start(bf16[4,1024,512]{2,1,0:T(8,128)(2,1)S(1)} %get-tuple-element.22) | copy-start | bytes 12582916
  16.4 9.3 %copy-start.5 = (s32[1024]{0:T(1024)S(1)}, s32[1024]{0:T(1024)}, u32[]{:S(2)}) copy-start(s32[1024]{0:T(1024)} %param.10) | copy-start | bytes 12292
  21.5 18.7 %all-to-all-start = ((bf16[4,1024,128]{2,0,1:T(4,128)(2,1)}), bf16[4,1024,128]{2,0,1:T(4,128)(2,1)S(1)}, u32[]{:S(2)}, u32[]{:S(2)}) async-start(bf16[4,1024,128]{2,0,1:T(4,128)(2,1)} %copy.52), calls=%async_computation | async-start | bytes 2097152 | tf_op jit(solution)/shard_map/all_to_all | solution.py:73
  25.7 103.9 %reduce-scatter.5.cloned.1.call-start = ((), (), s32[]{:S(2)}) async-start(), calls=%async_computation.4 | async-start | bytes 278528 | tf_op jit(solution)/shard_map/reduce_scatter | solution.py:87
  49.8 21.1 %copy-start.2 = (bf16[4,1024,512]{2,1,0:T(8,128)(2,1)S(1)}, bf16[4,1024,512]{2,1,0:T(8,128)(2,1)}, u32[]{:S(2)}) copy-start(bf16[4,1024,512]{2,1,0:T(8,128)(2,1)} %copy-done.1) | copy-start | bytes 12582916
  53.7 19.4 %copy-start.6 = (f32[512]{0:T(512)S(1)}, f32[512]{0:T(512)}, u32[]{:S(2)}) copy-start(f32[512]{0:T(512)} %param.12) | copy-start | bytes 6148
  73.0 117.1 %reduce-scatter.7.cloned.1.call-start = ((), (), s32[]{:S(2)}) async-start(), calls=%async_computation.5 | async-start | bytes 1114112
  73.0 9.1 %copy-start.3 = (bf16[4,1024,512]{2,1,0:T(8,128)(2,1)S(1)}, bf16[4,1024,512]{2,1,0:T(8,128)(2,1)}, u32[]{:S(2)}) copy-start(bf16[4,1024,512]{2,1,0:T(8,128)(2,1)} %param.7) | copy-start | bytes 12582916
  82.2 3.7 %copy-start.7 = (u32[32]{0:T(128)S(1)}, u32[32]{0:T(128)}, u32[]{:S(2)}) copy-start(u32[32]{0:T(128)} %constant.74) | copy-start | bytes 388
Sparse Core Ops, SparseCore 0:
  73.1 56.3 reduce-scatter.4
  133.7 56.3 reduce-scatter.6
where the time goes:
time: 197 us
  waiting for transfers between devices  82.8 us (42%)
  blocking collectives  49.9 us (25%)
  matrix products  28.7 us (15%)
  between operations  14.9 us (8%)
  local copies, waits for them, and re-layouts  14.1 us (7%)
  starting transfers between devices  4.25 us (2%)
  other arithmetic  2.25 us (1%)
    unnamed x3, waiting for transfers between devices  60.6 us
    unnamed x1, blocking collectives  33.1 us
    all_to_all x1, blocking collectives, local(): lax.all_to_all(grouped_grad, 'mem', split_axis=0, concat_axis=1, tiled=True)  16.9 us
    all_to_all x1, waiting for transfers between devices, local(): lax.all_to_all(outputs, 'mem', split_axis=1, concat_axis=0, tiled=True)  13.4 us
    dot_general x1, matrix products, local(): jnp.einsum('mpv,hv->mph', member_grad, weight_out, preferred_element_type...  9.1 us
    reduce_scatter x1, waiting for transfers between devices, local(): lax.psum_scatter(grad_out, ('pts', 'mem'), scatter_dimension=0, tiled=True)  8.74 us
    dot_general x1, matrix products, local(): jnp.einsum('mpd,dh->mph', latents, weight_in, preferred_element_type=jnp....  8.15 us
    unnamed x19, local copies, waits for them, and re-layouts  4.74 us
  transfers between devices with their start and end apart: 3, of which 3 were waited for; matrix products, arithmetic and copies ran while one was open for 8% of the time, Pallas kernels for 0%

commit v1 on v0

v1 whole, which is shorter than its diff:
```python
from functools import partial
import math

import jax
import jax.numpy as jnp
from jax import lax
from jax.experimental import pallas as pl
from jax.experimental.pallas import tpu as pltpu
from jax.sharding import PartitionSpec as P

LAT_ROWS = 640
LOSS_SCALE = 256
EPSILON = 0.0001
TILE = 16
F32 = jnp.float32
BF16 = jnp.bfloat16
VMEM_LIMIT = 32 * 1024 * 1024
SMALL_LIMIT = 16 * 1024 * 1024
LINK = BF16
GELU_A = math.sqrt(2.0 / math.pi)
GELU_B = GELU_A * 0.044715


def nt(a, b):
    return lax.dot_general(a, b, (((1,), (1,)), ((), ())), preferred_element_type=F32)


def tn(a, b):
    return lax.dot_general(a, b, (((0,), (0,)), ((), ())), preferred_element_type=F32)


def noise_row(seed, width):
    channel = lax.broadcasted_iota(jnp.int32, (1, width), 1)
    mixed = seed * (37 * channel + 11) + 7 * channel
    quotient = (mixed.astype(F32) * (1.0 / 65521.0)).astype(jnp.int32)
    rest = mixed - quotient * 65521
    rest = jnp.where(rest < 0, rest + 65521, rest)
    rest = jnp.where(rest >= 65521, rest - 65521, rest)
    return (rest.astype(F32) / 65521.0 - 0.5) * 2.0


def forward_body(sub, seeds, bias, latents, weight_in, weight_out, outputs, hidden, slope):
    group, block, depth = latents.shape
    width = bias.shape[1]
    first = pl.program_id(0) * group
    parts = []
    for k in range(group):
        shift = bias[...] + noise_row(seeds[first + k], width)
        for r in range(block // sub):
            parts.append((k, r, shift))
    w_in = weight_in[...]
    w_out = weight_out[...]
    ahead = None
    behind = None

    def activate(k, rows, x):
        x2 = x * x
        half = 0.5 * jnp.tanh(x * (GELU_A + GELU_B * x2)) + 0.5
        h = x * half
        low = h.astype(BF16)
        hidden[k, rows, :] = low
        slope[k, rows, :] = half + (h - h * half) * (2.0 * GELU_A + 6.0 * GELU_B * x2)
        return k, rows, low

    def finish(k, rows, low):
        outputs[k, rows, :] = jnp.dot(low, w_out, preferred_element_type=F32).astype(BF16)

    for k, r, shift in parts:
        rows = pl.ds(r * sub, sub)
        x = jnp.dot(latents[k, rows, :], w_in, preferred_element_type=F32) + shift
        if behind is not None:
            finish(*behind)
        behind = activate(*ahead) if ahead is not None else None
        ahead = (k, rows, x)
    if behind is not None:
        finish(*behind)
    finish(*activate(*ahead))


def forward(seeds, bias, latents, weight_in, weight_out, first, size, sub=256, group=2, most=256):
    members, _, depth = latents.shape
    width, variables = weight_out.shape
    block = min(most, math.gcd(first, size) if first else size)
    steps = size // block
    base = first // block
    whole = pl.BlockSpec(memory_space=pltpu.VMEM)
    return pl.pallas_call(
        partial(forward_body, min(sub, block)),
        grid=(members // group, steps),
        in_specs=[
            pl.BlockSpec(memory_space=pltpu.SMEM),
            whole,
            pl.BlockSpec((group, block, depth), lambda m, s: (m, base + s, 0)),
            whole,
            whole,
        ],
        out_specs=[
            pl.BlockSpec((group, block, variables), lambda m, s: (m, s, 0)),
            pl.BlockSpec((group, block, width), lambda m, s: (m, s, 0)),
            pl.BlockSpec((group, block, width), lambda m, s: (m, s, 0)),
        ],
        out_shape=[
            jax.ShapeDtypeStruct((members, size, variables), BF16),
            jax.ShapeDtypeStruct((members, size, width), BF16),
            jax.ShapeDtypeStruct((members, size, width), F32),
        ],
        compiler_params=pltpu.CompilerParams(vmem_limit_bytes=VMEM_LIMIT),
        cost_estimate=pl.CostEstimate(
            flops=2 * members * size * width * (depth + variables),
            bytes_accessed=members * size * (2 * depth + 6 * width + 2 * variables),
            transcendentals=members * size * width,
        ),
        name="forward",
    )(seeds, bias, latents, weight_in, weight_out)


def pair_tiles(own, others, targets, area, grad, start, unroll, first, loss_coef):
    members = own.shape[0]
    variables = own.shape[2]
    count = members * (1 + len(others))
    mine = members * TILE
    spots = [pl.multiple_of(start + u * TILE, TILE) for u in range(unroll)]
    ones = jnp.ones((8, 2 * variables), BF16)
    i = lax.broadcasted_iota(jnp.int32, (mine, count * TILE), 0)
    j = lax.broadcasted_iota(jnp.int32, (mine, count * TILE), 1)
    pair = jnp.logical_and(jnp.bitwise_and(i ^ j, TILE - 1) == 0, i != j)
    fulls, dists, weights = [], [], []
    for row in spots:
        rows = pl.ds(row, TILE)
        low = own[:, rows, :].reshape(mine, variables)
        full = jnp.concatenate(
            [low] + [o[:, rows, :].reshape(mine, variables) for o in others], axis=0
        )
        wide = full.astype(F32)
        square = wide * wide
        square_high = square.astype(BF16)
        square_low = (square - square_high.astype(F32)).astype(BF16)
        norms = nt(ones, jnp.concatenate([square_high, square_low], axis=1))[0:1, :] + EPSILON
        own_norms = jnp.sum(square[:mine], axis=1, keepdims=True)
        fulls.append(full)
        dists.append(jnp.maximum((own_norms + norms) - nt(low + low, full), EPSILON))
    for dist in dists:
        weight = jnp.where(pair, lax.rsqrt(dist), 0.0)
        total = jnp.sum(weight, axis=1, keepdims=True)
        weight_high = weight.astype(BF16)
        weight_low = (weight - weight_high.astype(F32)).astype(BF16)
        weights.append((total, jnp.concatenate([weight_high, weight_low], axis=0)))
    boths = [
        jnp.dot(weight, full, preferred_element_type=F32)
        for (_, weight), full in zip(weights, fulls)
    ]
    for row, full, both, (total, _) in zip(spots, fulls, boths, weights):
        mine_wide = full[:mine].astype(F32)
        weighted = both[:mine] + both[mine:]
        place = pl.ds(first + row, TILE)
        target = jnp.concatenate([targets[place, :]] * members, axis=0)
        scale = jnp.concatenate([area[place, :]] * members, axis=0)
        to_target = mine_wide - target
        spread = lax.rsqrt(jnp.sum(to_target * to_target, axis=1, keepdims=True) + EPSILON)
        pair_term = mine_wide * total - weighted
        value = scale * (
            to_target * (spread * (loss_coef / count)) - pair_term * (loss_coef / (count * (count - 1)))
        )
        grad[:, pl.ds(row, TILE), :] = value.astype(BF16).reshape(members, TILE, variables)


def backward_body(n_others, first, loss_coef, has_total, unroll, sub, dests, *refs):
    if dests:
        where, *refs = refs
    own, *refs = refs
    others, refs = refs[:n_others], refs[n_others:]
    targets, area, hidden_in, slope_in, latents_in, weight_out, *refs = refs
    if has_total:
        in_prior, out_prior, bias_prior, *refs = refs
    if dests:
        keep, send, *refs = refs
    else:
        in_total, out_total, bias_total, *refs = refs
    grad, hidden, slope, latents, low, sems = refs
    members, size, variables = own.shape
    copies = [
        pltpu.make_async_copy(slope_in, slope, sems.at[0]),
        pltpu.make_async_copy(hidden_in, hidden, sems.at[1]),
        pltpu.make_async_copy(latents_in.at[:, pl.ds(first, size), :], latents, sems.at[2]),
    ]
    for copy in copies:
        copy.start()

    @pl.loop(0, size // TILE // unroll)
    def _(t):
        pair_tiles(own, others, targets, area, grad, t * (unroll * TILE), unroll, first, loss_coef)

    w_out = weight_out[...]
    width = w_out.shape[0]
    bias_sum = bias_prior[...] if has_total else jnp.zeros((TILE, width), F32)
    copies[0].wait()
    for m in range(members):
        for r in range(size // sub):
            rows = pl.ds(r * sub, sub)
            pre = nt(grad[m, rows, :], w_out) * slope[m, rows, :]
            bias_sum += jnp.sum(pre.reshape(sub // TILE, TILE, width), axis=0)
            low[m, rows, :] = pre.astype(BF16)
    copies[1].wait()
    copies[2].wait()
    flat = lambda ref: ref[...].reshape(members * size, ref.shape[2])
    out_sum = tn(flat(hidden), flat(grad))
    in_sum = tn(flat(latents), flat(low))
    if has_total:
        out_sum += out_prior[...]
        in_sum += in_prior[...]
    if not dests:
        in_total[...] = in_sum
        out_total[...] = out_sum
        bias_total[...] = bias_sum
        return
    core = where[0]
    share = in_sum.shape[0] // dests
    lanes = out_sum.shape[1]
    groups = width // lanes
    for half in range(2):
        for place in range(dests // 2):
            dest = 2 * place + half
            rows = slice(dest * share, (dest + 1) * share)
            block = jnp.concatenate(
                [in_sum[rows, q * lanes : (q + 1) * lanes] for q in range(groups)]
                + [out_sum[rows, :]]
                + [bias_sum[:, dest * share // lanes * lanes : (dest * share // lanes + 1) * lanes]],
                axis=0,
            )

            @pl.when(core == half)
            def _():
                keep[place] = block

            @pl.when(core != half)
            def _():
                send[place] = block


def backward(own, others, targets, area, hidden, slope, latents, weight_out, prior, first, loss_coef, core=None, dests=0, unroll=8, sub=256):
    members, size, variables = own.shape
    depth = latents.shape[2]
    width = weight_out.shape[0]
    whole = pl.BlockSpec(memory_space=pltpu.VMEM)
    anywhere = pl.BlockSpec(memory_space=pl.ANY)
    count = members * (1 + len(others))
    if dests:
        rows = depth // dests * (width // variables + 1) + TILE
        shapes = [jax.ShapeDtypeStruct((dests // 2, rows, variables), F32)] * 2
    else:
        shapes = [
            jax.ShapeDtypeStruct((depth, width), F32),
            jax.ShapeDtypeStruct((width, variables), F32),
            jax.ShapeDtypeStruct((TILE, width), F32),
        ]
    return pl.pallas_call(
        partial(backward_body, len(others), first, loss_coef, prior is not None, min(unroll, size // TILE), min(sub, size), dests),
        in_specs=([pl.BlockSpec(memory_space=pltpu.SMEM)] if dests else [])
        + [whole] * (3 + len(others))
        + [anywhere] * 3 + [whole]
        + ([whole] * 3 if prior is not None else []),
        out_specs=[whole] * len(shapes),
        out_shape=shapes,
        scratch_shapes=[
            pltpu.VMEM((members, size, variables), BF16),
            pltpu.VMEM((members, size, width), BF16),
            pltpu.VMEM((members, size, width), F32),
            pltpu.VMEM((members, size, depth), BF16),
            pltpu.VMEM((members, size, width), BF16),
            pltpu.SemaphoreType.DMA((3,)),
        ],
        compiler_params=pltpu.CompilerParams(vmem_limit_bytes=VMEM_LIMIT),
        cost_estimate=pl.CostEstimate(
            flops=2 * members * size * (width * (depth + 2 * variables) + count * TILE * variables * 3),
            bytes_accessed=members * size * (2 * depth + 6 * width + 2 * variables),
            transcendentals=0,
        ),
        name="backward",
    )(*([core] if dests else []), own, *others, targets, area, hidden, slope, latents, weight_out, *(prior or ()))


OFFSETS = ((2, 1), (3, 1), (2, 0), (3, 0), (1, 1), (1, 0), (0, 1))


def spread_body(where, keep, arrived, mine, *parts):
    z, x = where[0], where[1]
    here = z * 2 + x
    mine[...] = keep[here] + arrived[here]
    for part, (dz, dx) in zip(parts, OFFSETS):
        there = (z ^ dz) * 2 + (x ^ dx)
        part[...] = (keep[there] + arrived[there]).astype(part.dtype)


def spread_out(where, keep, arrived, dtype):
    _, rows, lanes = keep.shape
    whole = pl.BlockSpec(memory_space=pltpu.VMEM)
    return pl.pallas_call(
        spread_body,
        in_specs=[pl.BlockSpec(memory_space=pltpu.SMEM), whole, whole],
        out_specs=[whole] * (1 + len(OFFSETS)),
        out_shape=[jax.ShapeDtypeStruct((rows, lanes), F32)]
        + [jax.ShapeDtypeStruct((rows, lanes), dtype)] * len(OFFSETS),
        compiler_params=pltpu.CompilerParams(vmem_limit_bytes=SMALL_LIMIT),
        name="spread_out",
    )(where, keep, arrived)


def finish_body(share, where, mine, *refs):
    parts, (in_share, out_share, bias_share) = refs[:-3], refs[-3:]
    total = mine[...]
    for part in parts:
        total += part[...].astype(F32)
    lanes = total.shape[1]
    groups = in_share.shape[1] // lanes
    for q in range(groups):
        in_share[:, q * lanes : (q + 1) * lanes] = total[q * share : (q + 1) * share]
    out_share[...] = total[groups * share : (groups + 1) * share]
    row = jnp.sum(total[(groups + 1) * share :], axis=0, keepdims=True)
    place = where[2]
    picked = row[:, :share]
    for k in range(1, lanes // share):
        picked = jnp.where(place == k, row[:, k * share : (k + 1) * share], picked)
    bias_share[...] = picked


def finish(where, mine, parts, share, width):
    lanes = mine.shape[1]
    whole = pl.BlockSpec(memory_space=pltpu.VMEM)
    return pl.pallas_call(
        partial(finish_body, share),
        in_specs=[pl.BlockSpec(memory_space=pltpu.SMEM)] + [whole] * (1 + len(parts)),
        out_specs=[whole] * 3,
        out_shape=[
            jax.ShapeDtypeStruct((share, width), F32),
            jax.ShapeDtypeStruct((share, lanes), F32),
            jax.ShapeDtypeStruct((1, share), F32),
        ],
        compiler_params=pltpu.CompilerParams(vmem_limit_bytes=SMALL_LIMIT),
        name="finish",
    )(where, mine, *parts)


def area_of(lat_row, rows_total):
    return jnp.cos(jnp.pi * (lat_row.astype(F32) + 0.5) / rows_total - jnp.pi / 2)


def swap_members(block, bit):
    size = lax.axis_size("mem")
    return lax.ppermute(block, "mem", [(i, i ^ bit) for i in range(size)])


def swap_points(block, dz, dx):
    points, members = lax.axis_size("pts"), lax.axis_size("mem")
    pairs = [
        (z * members + m, (z ^ dz) * members + (m ^ (2 * dx)))
        for z in range(points)
        for m in range(members)
    ]
    return lax.ppermute(block, ("pts", "mem"), pairs)


def gather_members(block):
    held = [block]
    bit = lax.axis_size("mem") // 2
    while bit:
        held += [swap_members(b, bit) for b in held]
        bit //= 2
    return held


CHUNKS = (256, 256, 256, 256)


def chunks_of(points):
    scale = points // sum(CHUNKS)
    first = 0
    for size in CHUNKS:
        yield first, size * scale
        first += size * scale


def local(latents, member_seeds, targets, lat_row, weight_in, bias_in, weight_out):
    points = latents.shape[1]
    depth = latents.shape[2]
    width, variables = weight_out.shape
    devices_pts, devices_mem = lax.axis_size("pts"), lax.axis_size("mem")
    dests = devices_pts * devices_mem
    loss_coef = LOSS_SCALE / math.sqrt(points * devices_pts)
    area = jnp.broadcast_to(area_of(lat_row, LAT_ROWS)[:, None], (points, variables))
    bias_row = bias_in[None, :]
    packed = dests == 16 and devices_mem == 4
    mem = lax.axis_index("mem")
    pts = lax.axis_index("pts")
    plan = list(chunks_of(points))
    done = []
    for first, size in plan:
        out, hidden, slope = forward(
            member_seeds, bias_row, latents, weight_in, weight_out, first, size
        )
        done.append((gather_members(out), hidden, slope))
    total = None
    core = (mem & 1).astype(jnp.int32).reshape(1)
    for (first, size), (held, hidden, slope) in zip(plan, done):
        last = first + size == points
        total = backward(
            held[0], held[1:], targets, area, hidden, slope, latents, weight_out, total,
            first, loss_coef, core, dests if last and packed else 0,
        )
    if not packed:
        scatter = lambda v: lax.psum_scatter(v, ("pts", "mem"), scatter_dimension=0, tiled=True)
        return scatter(total[0]), scatter(total[1]), scatter(jnp.sum(total[2], axis=0))
    keep, send = total
    arrived = swap_members(send, 1)
    where = jnp.stack([pts, mem >> 1, mem]).astype(jnp.int32)
    mine, *parts = spread_out(where, keep, arrived, LINK)
    parts = [swap_points(part, dz, dx) for part, (dz, dx) in zip(parts, OFFSETS)]
    in_share, out_share, bias_share = finish(where, mine, parts, depth // dests, width)
    return in_share, out_share, bias_share.reshape(depth // dests)


def solution(mesh):
    return jax.shard_map(
        local,
        mesh=mesh,
        in_specs=(
            P("mem", ("groups", "pts"), None),
            P(("groups", "mem")),
            P(("groups", "pts"), None),
            P(("groups", "pts")),
            P(),
            P(),
            P(),
        ),
        out_specs=(
            P(("groups", "pts", "mem"), None),
            P(("groups", "pts", "mem"), None),
            P(("groups", "pts", "mem")),
        ),
        check_vma=False,
    )
```

time: 197 us -> 83.2 us (0.42)
  waiting for transfers between devices: 82.8 us -> 13.3 us
  blocking collectives: 49.9 us -> 0 us
  Pallas kernels: 0 us -> 30.1 us
  matrix products: 28.7 us -> 0 us
  between operations: 14.9 us -> 1.02 us
  starting transfers between devices: 4.25 us -> 17.6 us
  local copies, waits for them, and re-layouts: 14.1 us -> 20.7 us
  other arithmetic: 2.25 us -> 0.12 us
    unnamed x3 -> x0, waiting for transfers between devices: 60.6 us -> none
    unnamed x1 -> x0, blocking collectives: 33.1 us -> none
    pallas_call x0 -> x10, Pallas kernels: none -> 30.1 us  [the longest x4 17.7 us: backward(): pl.pallas_call(partial(backward_body, len(others), first, loss_coef, prio...]
    dot_general x7 -> x0, matrix products: 28.7 us -> none  [the longest x1 9.1 us: local(): jnp.einsum('mpv,hv->mph', member_grad, weight_out, preferred_element_type...]
    ppermute x0 -> x20, starting transfers between devices: none -> 17.6 us  [the longest x7 10.9 us: swap_points(): return lax.ppermute(block, ('pts', 'mem'), pairs)]
    all_to_all x1 -> x0, blocking collectives: 16.9 us -> none  [local(): lax.all_to_all(grouped_grad, 'mem', split_axis=0, concat_axis=1, tiled=True)]
    unnamed x19 -> x70, local copies, waits for them, and re-layouts: 4.74 us -> 20.5 us
    all_to_all x1 -> x0, waiting for transfers between devices: 13.4 us -> none  [local(): lax.all_to_all(outputs, 'mem', split_axis=1, concat_axis=0, tiled=True)]
  transfers between devices with their start and end apart: 3 -> 20, of which waited for: 3 -> 7; matrix products, arithmetic and copies ran while one was open for 8% -> 0% of each run, Pallas kernels for 0% -> 25%
where the time goes in v1:
time: 83.2 us; the launch traced here: 82.8 us
  Pallas kernels  30.1 us (36%)
  local copies, waits for them, and re-layouts  20.7 us (25%)
  starting transfers between devices  17.6 us (21%)
  waiting for transfers between devices  13.3 us (16%)
  between operations  1.02 us (1%)
    unnamed x70, local copies, waits for them, and re-layouts  20.5 us
    pallas_call x4, Pallas kernels, backward(): pl.pallas_call(partial(backward_body, len(others), first, loss_coef, prio...  17.7 us
    ppermute x7, starting transfers between devices, swap_points(): return lax.ppermute(block, ('pts', 'mem'), pairs)  10.9 us
    ppermute x13, waiting for transfers between devices, swap_members(): return lax.ppermute(block, 'mem', [(i, i ^ bit) for i in range(size)])  10.4 us
    pallas_call x4, Pallas kernels, forward(): pl.pallas_call(partial(forward_body, min(sub, block)), grid=(members // g...  10.3 us
    ppermute x13, starting transfers between devices, swap_members(): return lax.ppermute(block, 'mem', [(i, i ^ bit) for i in range(size)])  6.69 us
    ppermute x7, waiting for transfers between devices, swap_points(): return lax.ppermute(block, ('pts', 'mem'), pairs)  2.94 us
  transfers between devices with their start and end apart: 20, of which 7 were waited for; matrix products, arithmetic and copies ran while one was open for 0% of the time, Pallas kernels for 25%

profile of v1, /device:TPU:0, one launch (start us, length us, event | category | flops | bytes accessed | tf_op | source)
XLA Modules:
  0.0 82.8 jit_solution(13294850726562878466)
XLA Ops:
  0.6 2.2 %copy-done = bf16[4,1024,512]{2,1,0:T(8,128)(2,1)S(1)} copy-done((bf16[4,1024,512]{2,1,0:T(8,128)(2,1)S(1)}, bf16[4,1024,512]{2,1,0:T(8,128)(2,1)}, u32[]{:S(2)}) %copy-start) | copy-done | bytes 4194328
  2.8 0.9 %copy-done.2 = bf16[512,128]{1,0:T(8,128)(2,1)S(1)} copy-done((bf16[512,128]{1,0:T(8,128)(2,1)S(1)}, bf16[512,128]{1,0:T(8,128)(2,1)}, u32[]{:S(2)}) %copy-start.2) | copy-done | bytes 131096
  3.7 1.0 %copy-done.4 = bf16[512,512]{1,0:T(8,128)(2,1)S(1)} copy-done((bf16[512,512]{1,0:T(8,128)(2,1)S(1)}, bf16[512,512]{1,0:T(8,128)(2,1)}, u32[]{:S(2)}) %copy-start.4) | copy-done | bytes 524312
  4.8 0.7 copy-done.32
  5.5 0.7 copy-done.33
  6.1 2.6 %forward.7 = (bf16[4,256,128]{2,1,0:T(8,128)(2,1)S(1)}, bf16[4,256,512]{2,1,0:T(8,128)(2,1)S(1)}, f32[4,256,512]{2,1,0:T(8,128)S(1)}) custom-call(s32[4]{0:T(128)S(1)} %copy-done.33, f32[1,512]{1,0:T(1,128)S(1)} %bitcast.6, bf16[4,1024,512]{2,1,0:T(8,128)(2,1)S(1)} %copy-done, bf16[512,512]{1,0:T(8,128)(2,1)S(1)} %copy-done.4, bf16[512,128]{1,0:T(8,128)(2,1)S(1)} %copy-done.2), custom_call_target="tpu_custom_call" | custom-call | flops 671088640 | bytes 4456448 | tf_op jit(solution)/shard_map/forward/pallas_call | solution.py:87
  8.7 1.4 %copy-done.10 = f32[4,256,512]{2,1,0:T(8,128)} copy-done((f32[4,256,512]{2,1,0:T(8,128)}, f32[4,256,512]{2,1,0:T(8,128)S(1)}, u32[]{:S(2)}) %copy-start.10) | copy-done | bytes 2097176
  10.1 1.0 %copy-done.12 = bf16[4,256,512]{2,1,0:T(8,128)(2,1)} copy-done((bf16[4,256,512]{2,1,0:T(8,128)(2,1)}, bf16[4,256,512]{2,1,0:T(8,128)(2,1)S(1)}, u32[]{:S(2)}) %copy-start.12) | copy-done | bytes 1048600
  11.0 0.5 collective-permute-start.10
  11.5 2.5 %collective-permute-start.9 = (bf16[4,256,128]{2,1,0:T(8,128)(2,1)S(1)}, bf16[4,256,128]{2,1,0:T(8,128)(2,1)}, u32[]{:S(2)}, u32[]{:S(2)}) collective-permute-start(bf16[4,256,128]{2,1,0:T(8,128)(2,1)S(1)} %get-tuple-element.46.refs_0_), channel_id=1, source_target_pairs={{0,2},{1,3},{2,0},{3,1},{4,6},{5,7},{6,4},{7,5},{8,10},{9,11},{10,... | collective-permute-start | bytes 786440 | tf_op jit(solution)/shard_map/ppermute | solution.py:349
  14.0 2.6 %forward.6 = (bf16[4,256,128]{2,1,0:T(8,128)(2,1)S(1)}, bf16[4,256,512]{2,1,0:T(8,128)(2,1)S(1)}, f32[4,256,512]{2,1,0:T(8,128)S(1)}) custom-call(s32[4]{0:T(128)S(1)} %copy-done.33, f32[1,512]{1,0:T(1,128)S(1)} %bitcast.7, bf16[4,1024,512]{2,1,0:T(8,128)(2,1)S(1)} %copy-done, bf16[512,512]{1,0:T(8,128)(2,1)S(1)} %copy-done.4, bf16[512,128]{1,0:T(8,128)(2,1)S(1)} %copy-done.2), custom_call_target="tpu_custom_call" | custom-call | flops 671088640 | bytes 4456448 | tf_op jit(solution)/shard_map/forward/pallas_call | solution.py:87
  16.6 1.4 %copy-done.8 = f32[4,256,512]{2,1,0:T(8,128)} copy-done((f32[4,256,512]{2,1,0:T(8,128)}, f32[4,256,512]{2,1,0:T(8,128)S(1)}, u32[]{:S(2)}) %copy-start.8) | copy-done | bytes 2097176
  17.9 1.0 %copy-done.18 = bf16[4,256,512]{2,1,0:T(8,128)(2,1)} copy-done((bf16[4,256,512]{2,1,0:T(8,128)(2,1)}, bf16[4,256,512]{2,1,0:T(8,128)(2,1)S(1)}, u32[]{:S(2)}) %copy-start.18) | copy-done | bytes 1048600
  19.4 2.6 %forward.5 = (bf16[4,256,128]{2,1,0:T(8,128)(2,1)S(1)}, bf16[4,256,512]{2,1,0:T(8,128)(2,1)S(1)}, f32[4,256,512]{2,1,0:T(8,128)S(1)}) custom-call(s32[4]{0:T(128)S(1)} %copy-done.33, f32[1,512]{1,0:T(1,128)S(1)} %bitcast.8, bf16[4,1024,512]{2,1,0:T(8,128)(2,1)S(1)} %copy-done, bf16[512,512]{1,0:T(8,128)(2,1)S(1)} %copy-done.4, bf16[512,128]{1,0:T(8,128)(2,1)S(1)} %copy-done.2), custom_call_target="tpu_custom_call" | custom-call | flops 671088640 | bytes 4456448 | tf_op jit(solution)/shard_map/forward/pallas_call | solution.py:87
  22.0 1.1 %copy-done.16 = bf16[4,256,512]{2,1,0:T(8,128)(2,1)} copy-done((bf16[4,256,512]{2,1,0:T(8,128)(2,1)}, bf16[4,256,512]{2,1,0:T(8,128)(2,1)S(1)}, u32[]{:S(2)}) %copy-start.16) | copy-done | bytes 1048600
  23.1 1.8 %collective-permute-start.3 = (bf16[4,256,128]{2,1,0:T(8,128)(2,1)S(1)}, bf16[4,256,128]{2,1,0:T(8,128)(2,1)}, u32[]{:S(2)}, u32[]{:S(2)}) collective-permute-start(bf16[4,256,128]{2,1,0:T(8,128)(2,1)S(1)} %get-tuple-element.40.refs_0_), channel_id=1, source_target_pairs={{0,2},{1,3},{2,0},{3,1},{4,6},{5,7},{6,4},{7,5},{8,10},{9,11},{10,... | collective-permute-start | bytes 786440 | tf_op jit(solution)/shard_map/ppermute | solution.py:349
  24.9 2.6 %forward.4 = (bf16[4,256,128]{2,1,0:T(8,128)(2,1)S(1)}, bf16[4,256,512]{2,1,0:T(8,128)(2,1)S(1)}, f32[4,256,512]{2,1,0:T(8,128)S(1)}) custom-call(s32[4]{0:T(128)S(1)} %copy-done.33, f32[1,512]{1,0:T(1,128)S(1)} %bitcast.9, bf16[4,1024,512]{2,1,0:T(8,128)(2,1)S(1)} %copy-done, bf16[512,512]{1,0:T(8,128)(2,1)S(1)} %copy-done.4, bf16[512,128]{1,0:T(8,128)(2,1)S(1)} %copy-done.2), custom_call_target="tpu_custom_call" | custom-call | flops 671088640 | bytes 4456448 | tf_op jit(solution)/shard_map/forward/pallas_call | solution.py:87
  27.5 1.0 %copy-done.14 = bf16[4,256,512]{2,1,0:T(8,128)(2,1)} copy-done((bf16[4,256,512]{2,1,0:T(8,128)(2,1)}, bf16[4,256,512]{2,1,0:T(8,128)(2,1)S(1)}, u32[]{:S(2)}) %copy-start.14) | copy-done | bytes 1048600
  28.5 0.7 copy-done.30
  29.3 0.3 collective-permute-start
  29.6 0.7 copy-done.28
  30.2 0.5 collective-permute-start.4
  30.7 3.3 %collective-permute-done.3.refs_1_ = bf16[4,256,128]{2,1,0:T(8,128)(2,1)} collective-permute-done((bf16[4,256,128]{2,1,0:T(8,128)(2,1)S(1)}, bf16[4,256,128]{2,1,0:T(8,128)(2,1)}, u32[]{:S(2)}, u32[]{:S(2)}) %collective-permute-start.3) | collective-permute-done | bytes 262176 | tf_op jit(solution)/shard_map/ppermute | solution.py:349
  34.1 4.8 %collective-permute-done.refs_2_ = bf16[4,256,128]{2,1,0:T(8,128)(2,1)S(1)} collective-permute-done((bf16[4,256,128]{2,1,0:T(8,128)(2,1)S(1)}, bf16[4,256,128]{2,1,0:T(8,128)(2,1)S(1)}, u32[]{:S(2)}, u32[]{:S(2)}) %collective-permute-start) | collective-permute-done | bytes 262176 | tf_op jit(solution)/shard_map/ppermute | solution.py:349
  38.9 0.5 collective-permute-start.2
  39.6 2.2 %copy-done.1 = bf16[4,1024,512]{2,1,0:T(8,128)(2,1)S(1)} copy-done((bf16[4,1024,512]{2,1,0:T(8,128)(2,1)S(1)}, bf16[4,1024,512]{2,1,0:T(8,128)(2,1)}, u32[]{:S(2)}) %copy-start.1) | copy-done | bytes 4194328
  41.8 1.6 %copy-done.11 = f32[4,256,512]{2,1,0:T(8,128)S(1)} copy-done((f32[4,256,512]{2,1,0:T(8,128)S(1)}, f32[4,256,512]{2,1,0:T(8,128)}, u32[]{:S(2)}) %copy-start.11) | copy-done | bytes 2097176
  43.4 1.2 %copy-done.13 = bf16[4,256,512]{2,1,0:T(8,128)(2,1)S(1)} copy-done((bf16[4,256,512]{2,1,0:T(8,128)(2,1)S(1)}, bf16[4,256,512]{2,1,0:T(8,128)(2,1)}, u32[]{:S(2)}) %copy-start.13) | copy-done | bytes 1048600
  44.6 0.9 %copy-done.27 = bf16[4,256,128]{2,1,0:T(8,128)(2,1)S(1)} copy-done((bf16[4,256,128]{2,1,0:T(8,128)(2,1)S(1)}, bf16[4,256,128]{2,1,0:T(8,128)(2,1)}, u32[]{:S(2)}) %copy-start.27) | copy-done | bytes 262168
  45.6 0.9 %copy-done.31 = bf16[4,256,128]{2,1,0:T(8,128)(2,1)S(1)} copy-done((bf16[4,256,128]{2,1,0:T(8,128)(2,1)S(1)}, bf16[4,256,128]{2,1,0:T(8,128)(2,1)}, u32[]{:S(2)}) %copy-start.31) | copy-done | bytes 262168
  46.5 4.4 %backward.4 = (f32[512,512]{1,0:T(8,128)S(1)}, f32[512,128]{1,0:T(8,128)S(1)}, f32[16,512]{1,0:T(8,128)S(1)}) custom-call(bf16[4,256,128]{2,1,0:T(8,128)(2,1)S(1)} %copy-done.27, bf16[4,256,128]{2,1,0:T(8,128)(2,1)} %collective-permute-done.9.refs_1_, bf16[4,256,128]{2,1,0:T(8,128)(2,1)S(1)} %copy-done.31, ...), custom_call_target="tpu_custom_call" | custom-call | flops 1006632960 | bytes 4456448 | tf_op jit(solution)/shard_map/backward/pallas_call | solution.py:256
  51.1 4.4 %backward.5 = (f32[512,512]{1,0:T(8,128)S(1)}, f32[512,128]{1,0:T(8,128)S(1)}, f32[16,512]{1,0:T(8,128)S(1)}) custom-call(bf16[4,256,128]{2,1,0:T(8,128)(2,1)S(1)} %copy-done.25, bf16[4,256,128]{2,1,0:T(8,128)(2,1)} %collective-permute-done.6.refs_1_, bf16[4,256,128]{2,1,0:T(8,128)(2,1)S(1)} %copy-done.29, ...), custom_call_target="tpu_custom_call" | custom-call | flops 1006632960 | bytes 4456448 | tf_op jit(solution)/shard_map/backward/pallas_call | solution.py:256
  55.6 4.5 %backward.6 = (f32[512,512]{1,0:T(8,128)S(1)}, f32[512,128]{1,0:T(8,128)S(1)}, f32[16,512]{1,0:T(8,128)S(1)}) custom-call(bf16[4,256,128]{2,1,0:T(8,128)(2,1)S(1)} %get-tuple-element.40.refs_0_, bf16[4,256,128]{2,1,0:T(8,128)(2,1)} %collective-permute-done.3.refs_1_, bf16[4,256,128]{2,1,0:T(8,128)(2,1)} %collective-permute-done.4.refs_2_, ...), custom_call_target="tpu_custom_call" | custom-call | flops 1006632960 | bytes 4456448 | tf_op jit(solution)/shard_map/backward/pallas_call | solution.py:256
  60.1 4.3 %backward.7 = (f32[8,176,128]{2,1,0:T(8,128)S(1)}, f32[8,176,128]{2,1,0:T(8,128)}) custom-call(s32[1]{0:T(128)} %bitcast.3.refs_0_, bf16[4,256,128]{2,1,0:T(8,128)(2,1)S(1)} %copy-done.21, bf16[4,256,128]{2,1,0:T(8,128)(2,1)S(1)} %copy-done.23, bf16[4,256,128]{2,1,0:T(8,128)(2,1)S(1)} %collective-permute-done.1.refs_3_, ...), custom_call_target="tpu_custom_call" | custom-call | flops 1006632960 | bytes 4456448 | tf_op jit(solution)/shard_map/backward/pallas_call | solution.py:256
  64.7 2.3 %collective-permute-done.12.arrived = f32[8,176,128]{2,1,0:T(8,128)S(1)} collective-permute-done((f32[8,176,128]{2,1,0:T(8,128)}, f32[8,176,128]{2,1,0:T(8,128)S(1)}, u32[]{:S(2)}, u32[]{:S(2)}) %collective-permute-start.12) | collective-permute-done | bytes 720928 | tf_op jit(solution)/shard_map/ppermute | solution.py:349
  66.9 0.6 spread_out.1
  67.6 2.8 %collective-permute-start.13 = (bf16[176,128]{1,0:T(8,128)(2,1)S(1)}, bf16[176,128]{1,0:T(8,128)(2,1)S(1)}, u32[]{:S(2)}, u32[]{:S(2)}) collective-permute-start(bf16[176,128]{1,0:T(8,128)(2,1)S(1)} %get-tuple-element.61), channel_id=1, source_target_pairs={{0,10},{1,11},{2,8},{3,9},{4,14},{5,15},{6,12},{7,13},{8,2},{9,3},... | collective-permute-start | bytes 135176 | tf_op jit(solution)/shard_map/ppermute | solution.py:359
  70.3 2.1 %collective-permute-start.14 = (bf16[176,128]{1,0:T(8,128)(2,1)S(1)}, bf16[176,128]{1,0:T(8,128)(2,1)S(1)}, u32[]{:S(2)}, u32[]{:S(2)}) collective-permute-start(bf16[176,128]{1,0:T(8,128)(2,1)S(1)} %get-tuple-element.62), channel_id=1, source_target_pairs={{0,14},{1,15},{2,12},{3,13},{4,10},{5,11},{6,8},{7,9},{8,6},{9,7},... | collective-permute-start | bytes 135176 | tf_op jit(solution)/shard_map/ppermute | solution.py:359
  72.5 1.7 %collective-permute-start.15 = (bf16[176,128]{1,0:T(8,128)(2,1)S(1)}, bf16[176,128]{1,0:T(8,128)(2,1)S(1)}, u32[]{:S(2)}, u32[]{:S(2)}) collective-permute-start(bf16[176,128]{1,0:T(8,128)(2,1)S(1)} %get-tuple-element.63), channel_id=1, source_target_pairs={{0,8},{1,9},{2,10},{3,11},{4,12},{5,13},{6,14},{7,15},{8,0},{9,1},... | collective-permute-start | bytes 135176 | tf_op jit(solution)/shard_map/ppermute | solution.py:359
  74.2 0.8 collective-permute-start.16
  74.9 1.1 %collective-permute-start.17 = (bf16[176,128]{1,0:T(8,128)(2,1)S(1)}, bf16[176,128]{1,0:T(8,128)(2,1)S(1)}, u32[]{:S(2)}, u32[]{:S(2)}) collective-permute-start(bf16[176,128]{1,0:T(8,128)(2,1)S(1)} %get-tuple-element.65), channel_id=1, source_target_pairs={{0,6},{1,7},{2,4},{3,5},{4,2},{5,3},{6,0},{7,1},{8,14},{9,15},{10,... | collective-permute-start | bytes 135176 | tf_op jit(solution)/shard_map/ppermute | solution.py:359
  76.1 1.0 %collective-permute-start.18 = (bf16[176,128]{1,0:T(8,128)(2,1)S(1)}, bf16[176,128]{1,0:T(8,128)(2,1)S(1)}, u32[]{:S(2)}, u32[]{:S(2)}) collective-permute-start(bf16[176,128]{1,0:T(8,128)(2,1)S(1)} %get-tuple-element.66), channel_id=1, source_target_pairs={{0,4},{1,5},{2,6},{3,7},{4,0},{5,1},{6,2},{7,3},{8,12},{9,13},{10,... | collective-permute-start | bytes 135176 | tf_op jit(solution)/shard_map/ppermute | solution.py:359
  77.1 1.3 %collective-permute-start.19 = (bf16[176,128]{1,0:T(8,128)(2,1)S(1)}, bf16[176,128]{1,0:T(8,128)(2,1)S(1)}, u32[]{:S(2)}, u32[]{:S(2)}) collective-permute-start(bf16[176,128]{1,0:T(8,128)(2,1)S(1)} %get-tuple-element.67), channel_id=1, source_target_pairs={{0,2},{1,3},{2,0},{3,1},{4,6},{5,7},{6,4},{7,5},{8,10},{9,11},{10,... | collective-permute-start | bytes 135176 | tf_op jit(solution)/shard_map/ppermute | solution.py:359
  78.4 1.5 %collective-permute-done.15.refs_2_ = bf16[176,128]{1,0:T(8,128)(2,1)S(1)} collective-permute-done((bf16[176,128]{1,0:T(8,128)(2,1)S(1)}, bf16[176,128]{1,0:T(8,128)(2,1)S(1)}, u32[]{:S(2)}, u32[]{:S(2)}) %collective-permute-start.15) | collective-permute-done | bytes 45088 | tf_op jit(solution)/shard_map/ppermute | solution.py:359
  79.9 0.6 collective-permute-done.16.refs_3_
  80.5 0.6 collective-permute-done.17.refs_4_
  81.1 0.3 collective-permute-done.19.refs_6_
  81.4 1.4 %finish.1 = (f32[32,512]{1,0:T(8,128)}, f32[32,128]{1,0:T(8,128)}, f32[1,32]{1,0:T(1,128)}) custom-call(s32[3]{0:T(128)S(1)} %pad_add_fusion.where, f32[176,128]{1,0:T(8,128)S(1)} %get-tuple-element.60.mine, bf16[176,128]{1,0:T(8,128)(2,1)S(1)} %collective-permute-done.13.refs_0_, bf16[176,128]{1,0:T(8,128)(2,1)S(1)} %collective-permute-done.14.refs_1_, ...), custom_call_target="tpu_custom_call" | custom-call | tf_op jit(solution)/shard_map/finish/pallas_call | solution.py:329
  (75 shorter events, 1.1 us)
Async XLA Ops:
  0.6 2.2 %copy-start = (bf16[4,1024,512]{2,1,0:T(8,128)(2,1)S(1)}, bf16[4,1024,512]{2,1,0:T(8,128)(2,1)}, u32[]{:S(2)}) copy-start(bf16[4,1024,512]{2,1,0:T(8,128)(2,1)} %refs_9_.7) | copy-start | bytes 12582916
  3.7 1.0 %copy-start.4 = (bf16[512,512]{1,0:T(8,128)(2,1)S(1)}, bf16[512,512]{1,0:T(8,128)(2,1)}, u32[]{:S(2)}) copy-start(bf16[512,512]{1,0:T(8,128)(2,1)} %weight_in.7) | copy-start | bytes 1572868
  8.7 1.4 %copy-start.10 = (f32[4,256,512]{2,1,0:T(8,128)}, f32[4,256,512]{2,1,0:T(8,128)S(1)}, u32[]{:S(2)}) copy-start(f32[4,256,512]{2,1,0:T(8,128)S(1)} %get-tuple-element.48.refs_7_) | copy-start | bytes 6291460
  10.1 1.0 %copy-start.12 = (bf16[4,256,512]{2,1,0:T(8,128)(2,1)}, bf16[4,256,512]{2,1,0:T(8,128)(2,1)S(1)}, u32[]{:S(2)}) copy-start(bf16[4,256,512]{2,1,0:T(8,128)(2,1)S(1)} %get-tuple-element.47.refs_6_) | copy-start | bytes 3145732
  11.0 5.5 %copy-start.26 = (bf16[4,256,128]{2,1,0:T(8,128)(2,1)}, bf16[4,256,128]{2,1,0:T(8,128)(2,1)S(1)}, u32[]{:S(2)}) copy-start(bf16[4,256,128]{2,1,0:T(8,128)(2,1)S(1)} %get-tuple-element.46.refs_0_) | copy-start | bytes 786436
  11.0 17.5 %collective-permute-start.10 = (bf16[4,256,128]{2,1,0:T(8,128)(2,1)S(1)}, bf16[4,256,128]{2,1,0:T(8,128)(2,1)S(1)}, u32[]{:S(2)}, u32[]{:S(2)}) collective-permute-start(bf16[4,256,128]{2,1,0:T(8,128)(2,1)S(1)} %get-tuple-element.46.refs_0_), channel_id=1, source_target_pairs={{0,1},{1,0},{2,3},{3,2},{4,5},{5,4},{6,7},{7,6},{8,9},{9,8},{10,11... | collective-permute-start | bytes 786440 | tf_op jit(solution)/shard_map/ppermute | solution.py:349
  11.5 18.1 %collective-permute-start.9 = (bf16[4,256,128]{2,1,0:T(8,128)(2,1)S(1)}, bf16[4,256,128]{2,1,0:T(8,128)(2,1)}, u32[]{:S(2)}, u32[]{:S(2)}) collective-permute-start(bf16[4,256,128]{2,1,0:T(8,128)(2,1)S(1)} %get-tuple-element.46.refs_0_), channel_id=1, source_target_pairs={{0,2},{1,3},{2,0},{3,1},{4,6},{5,7},{6,4},{7,5},{8,10},{9,11},{10,... | collective-permute-start | bytes 786440 | tf_op jit(solution)/shard_map/ppermute | solution.py:349
  16.6 1.4 %copy-start.8 = (f32[4,256,512]{2,1,0:T(8,128)}, f32[4,256,512]{2,1,0:T(8,128)S(1)}, u32[]{:S(2)}) copy-start(f32[4,256,512]{2,1,0:T(8,128)S(1)} %get-tuple-element.45.refs_7_) | copy-start | bytes 6291460
  17.9 1.0 %copy-start.18 = (bf16[4,256,512]{2,1,0:T(8,128)(2,1)}, bf16[4,256,512]{2,1,0:T(8,128)(2,1)S(1)}, u32[]{:S(2)}) copy-start(bf16[4,256,512]{2,1,0:T(8,128)(2,1)S(1)} %get-tuple-element.44.refs_6_) | copy-start | bytes 3145732
  18.9 3.1 %copy-start.24 = (bf16[4,256,128]{2,1,0:T(8,128)(2,1)}, bf16[4,256,128]{2,1,0:T(8,128)(2,1)S(1)}, u32[]{:S(2)}) copy-start(bf16[4,256,128]{2,1,0:T(8,128)(2,1)S(1)} %get-tuple-element.43.refs_0_) | copy-start | bytes 786436
  18.9 10.6 %collective-permute-start.7 = (bf16[4,256,128]{2,1,0:T(8,128)(2,1)S(1)}, bf16[4,256,128]{2,1,0:T(8,128)(2,1)S(1)}, u32[]{:S(2)}, u32[]{:S(2)}) collective-permute-start(bf16[4,256,128]{2,1,0:T(8,128)(2,1)S(1)} %get-tuple-element.43.refs_0_), channel_id=1, source_target_pairs={{0,1},{1,0},{2,3},{3,2},{4,5},{5,4},{6,7},{7,6},{8,9},{9,8},{10,11... | collective-permute-start | bytes 786440 | tf_op jit(solution)/shard_map/ppermute | solution.py:349
  19.1 11.6 %collective-permute-start.6 = (bf16[4,256,128]{2,1,0:T(8,128)(2,1)S(1)}, bf16[4,256,128]{2,1,0:T(8,128)(2,1)}, u32[]{:S(2)}, u32[]{:S(2)}) collective-permute-start(bf16[4,256,128]{2,1,0:T(8,128)(2,1)S(1)} %get-tuple-element.43.refs_0_), channel_id=1, source_target_pairs={{0,2},{1,3},{2,0},{3,1},{4,6},{5,7},{6,4},{7,5},{8,10},{9,11},{10,... | collective-permute-start | bytes 786440 | tf_op jit(solution)/shard_map/ppermute | solution.py:349
  22.0 1.1 %copy-start.16 = (bf16[4,256,512]{2,1,0:T(8,128)(2,1)}, bf16[4,256,512]{2,1,0:T(8,128)(2,1)S(1)}, u32[]{:S(2)}) copy-start(bf16[4,256,512]{2,1,0:T(8,128)(2,1)S(1)} %get-tuple-element.41.refs_6_) | copy-start | bytes 3145732
  23.1 4.4 %copy-start.6 = (f32[4,256,512]{2,1,0:T(8,128)}, f32[4,256,512]{2,1,0:T(8,128)S(1)}, u32[]{:S(2)}) copy-start(f32[4,256,512]{2,1,0:T(8,128)S(1)} %get-tuple-element.42.refs_7_) | copy-start | bytes 6291460
  23.1 10.9 %copy-start.34 = (s32[1024]{0:T(1024)S(1)}, s32[1024]{0:T(1024)}, u32[]{:S(2)}) copy-start(s32[1024]{0:T(1024)} %param.10) | copy-start | bytes 12292
  23.1 16.5 %copy-start.3 = (bf16[512,128]{1,0:T(8,128)(2,1)S(1)}, bf16[512,128]{1,0:T(8,128)(2,1)}, u32[]{:S(2)}) copy-start(bf16[512,128]{1,0:T(8,128)(2,1)} %refs_10_.1) | copy-start | bytes 393220
  23.1 16.5 %copy-start.5 = (f32[1024,128]{1,0:T(8,128)S(1)}, f32[1024,128]{1,0:T(8,128)}, u32[]{:S(2)}) copy-start(f32[1024,128]{1,0:T(8,128)} %refs_5_.1) | copy-start | bytes 1572868
  23.1 10.9 %collective-permute-start.3 = (bf16[4,256,128]{2,1,0:T(8,128)(2,1)S(1)}, bf16[4,256,128]{2,1,0:T(8,128)(2,1)}, u32[]{:S(2)}, u32[]{:S(2)}) collective-permute-start(bf16[4,256,128]{2,1,0:T(8,128)(2,1)S(1)} %get-tuple-element.40.refs_0_), channel_id=1, source_target_pairs={{0,2},{1,3},{2,0},{3,1},{4,6},{5,7},{6,4},{7,5},{8,10},{9,11},{10,... | collective-permute-start | bytes 786440 | tf_op jit(solution)/shard_map/ppermute | solution.py:349
  27.5 1.0 %copy-start.14 = (bf16[4,256,512]{2,1,0:T(8,128)(2,1)}, bf16[4,256,512]{2,1,0:T(8,128)(2,1)S(1)}, u32[]{:S(2)}) copy-start(bf16[4,256,512]{2,1,0:T(8,128)(2,1)S(1)} %get-tuple-element.38.refs_7_) | copy-start | bytes 3145732
  28.5 22.5 %copy-start.20 = (bf16[4,256,128]{2,1,0:T(8,128)(2,1)}, bf16[4,256,128]{2,1,0:T(8,128)(2,1)S(1)}, u32[]{:S(2)}) copy-start(bf16[4,256,128]{2,1,0:T(8,128)(2,1)S(1)} %get-tuple-element.37.refs_1_) | copy-start | bytes 786436
  29.3 9.6 %collective-permute-start = (bf16[4,256,128]{2,1,0:T(8,128)(2,1)S(1)}, bf16[4,256,128]{2,1,0:T(8,128)(2,1)S(1)}, u32[]{:S(2)}, u32[]{:S(2)}) collective-permute-start(bf16[4,256,128]{2,1,0:T(8,128)(2,1)S(1)} %get-tuple-element.37.refs_1_), channel_id=1, source_target_pairs={{0,2},{1,3},{2,0},{3,1},{4,6},{5,7},{6,4},{7,5},{8,10},{9,11},{10,... | collective-permute-start | bytes 786440 | tf_op jit(solution)/shard_map/ppermute | solution.py:349
  29.5 9.3 %collective-permute-start.11 = (bf16[4,256,128]{2,1,0:T(8,128)(2,1)}, bf16[4,256,128]{2,1,0:T(8,128)(2,1)}, u32[]{:S(2)}, u32[]{:S(2)}) collective-permute-start(bf16[4,256,128]{2,1,0:T(8,128)(2,1)} %collective-permute-done.9.refs_1_), channel_id=1, source_target_pairs={{0,1},{1,0},{2,3},{3,2},{4,5},{5,4},{6,7},{7,6},{8,9},{9,8},{10,11... | collective-permute-start | bytes 786440 | tf_op jit(solution)/shard_map/ppermute | solution.py:349
  30.2 25.3 %collective-permute-start.4 = (bf16[4,256,128]{2,1,0:T(8,128)(2,1)S(1)}, bf16[4,256,128]{2,1,0:T(8,128)(2,1)}, u32[]{:S(2)}, u32[]{:S(2)}) collective-permute-start(bf16[4,256,128]{2,1,0:T(8,128)(2,1)S(1)} %get-tuple-element.40.refs_0_), channel_id=1, source_target_pairs={{0,1},{1,0},{2,3},{3,2},{4,5},{5,4},{6,7},{7,6},{8,9},{9,8},{10,11... | collective-permute-start | bytes 786440 | tf_op jit(solution)/shard_map/ppermute | solution.py:349
  30.7 20.2 %collective-permute-start.8 = (bf16[4,256,128]{2,1,0:T(8,128)(2,1)}, bf16[4,256,128]{2,1,0:T(8,128)(2,1)}, u32[]{:S(2)}, u32[]{:S(2)}) collective-permute-start(bf16[4,256,128]{2,1,0:T(8,128)(2,1)} %collective-permute-done.6.refs_1_), channel_id=1, source_target_pairs={{0,1},{1,0},{2,3},{3,2},{4,5},{5,4},{6,7},{7,6},{8,9},{9,8},{10,11... | collective-permute-start | bytes 786440 | tf_op jit(solution)/shard_map/ppermute | solution.py:349
  34.0 21.5 %collective-permute-start.5 = (bf16[4,256,128]{2,1,0:T(8,128)(2,1)}, bf16[4,256,128]{2,1,0:T(8,128)(2,1)}, u32[]{:S(2)}, u32[]{:S(2)}) collective-permute-start(bf16[4,256,128]{2,1,0:T(8,128)(2,1)} %collective-permute-done.3.refs_1_), channel_id=1, source_target_pairs={{0,1},{1,0},{2,3},{3,2},{4,5},{5,4},{6,7},{7,6},{8,9},{9,8},{10,11... | collective-permute-start | bytes 786440 | tf_op jit(solution)/shard_map/ppermute | solution.py:349
  38.9 12.1 %copy-start.22 = (bf16[4,256,128]{2,1,0:T(8,128)(2,1)}, bf16[4,256,128]{2,1,0:T(8,128)(2,1)S(1)}, u32[]{:S(2)}) copy-start(bf16[4,256,128]{2,1,0:T(8,128)(2,1)S(1)} %collective-permute-done.refs_2_) | copy-start | bytes 786436
  38.9 21.2 %collective-permute-start.1 = (bf16[4,256,128]{2,1,0:T(8,128)(2,1)S(1)}, bf16[4,256,128]{2,1,0:T(8,128)(2,1)S(1)}, u32[]{:S(2)}, u32[]{:S(2)}) collective-permute-start(bf16[4,256,128]{2,1,0:T(8,128)(2,1)S(1)} %get-tuple-element.37.refs_1_), channel_id=1, source_target_pairs={{0,1},{1,0},{2,3},{3,2},{4,5},{5,4},{6,7},{7,6},{8,9},{9,8},{10,11... | collective-permute-start | bytes 786440 | tf_op jit(solution)/shard_map/ppermute | solution.py:349
  38.9 21.2 %collective-permute-start.2 = (bf16[4,256,128]{2,1,0:T(8,128)(2,1)S(1)}, bf16[4,256,128]{2,1,0:T(8,128)(2,1)S(1)}, u32[]{:S(2)}, u32[]{:S(2)}) collective-permute-start(bf16[4,256,128]{2,1,0:T(8,128)(2,1)S(1)} %collective-permute-done.refs_2_), channel_id=1, source_target_pairs={{0,1},{1,0},{2,3},{3,2},{4,5},{5,4},{6,7},{7,6},{8,9},{9,8},{10,11... | collective-permute-start | bytes 786440 | tf_op jit(solution)/shard_map/ppermute | solution.py:349
  39.6 2.2 %copy-start.1 = (bf16[4,1024,512]{2,1,0:T(8,128)(2,1)S(1)}, bf16[4,1024,512]{2,1,0:T(8,128)(2,1)}, u32[]{:S(2)}) copy-start(bf16[4,1024,512]{2,1,0:T(8,128)(2,1)} %refs_9_.7) | copy-start | bytes 12582916
  41.8 1.6 %copy-start.11 = (f32[4,256,512]{2,1,0:T(8,128)S(1)}, f32[4,256,512]{2,1,0:T(8,128)}, u32[]{:S(2)}) copy-start(f32[4,256,512]{2,1,0:T(8,128)} %copy-done.10) | copy-start | bytes 6291460
  43.4 1.2 %copy-start.13 = (bf16[4,256,512]{2,1,0:T(8,128)(2,1)S(1)}, bf16[4,256,512]{2,1,0:T(8,128)(2,1)}, u32[]{:S(2)}) copy-start(bf16[4,256,512]{2,1,0:T(8,128)(2,1)} %copy-done.12) | copy-start | bytes 3145732
  46.5 4.5 %copy-start.9 = (f32[4,256,512]{2,1,0:T(8,128)S(1)}, f32[4,256,512]{2,1,0:T(8,128)}, u32[]{:S(2)}) copy-start(f32[4,256,512]{2,1,0:T(8,128)} %copy-done.8) | copy-start | bytes 6291460
  46.5 4.5 %copy-start.19 = (bf16[4,256,512]{2,1,0:T(8,128)(2,1)S(1)}, bf16[4,256,512]{2,1,0:T(8,128)(2,1)}, u32[]{:S(2)}) copy-start(bf16[4,256,512]{2,1,0:T(8,128)(2,1)} %copy-done.18) | copy-start | bytes 3145732
  46.5 4.5 %copy-start.25 = (bf16[4,256,128]{2,1,0:T(8,128)(2,1)S(1)}, bf16[4,256,128]{2,1,0:T(8,128)(2,1)}, u32[]{:S(2)}) copy-start(bf16[4,256,128]{2,1,0:T(8,128)(2,1)} %copy-done.24) | copy-start | bytes 786436
  46.5 4.5 %copy-start.29 = (bf16[4,256,128]{2,1,0:T(8,128)(2,1)S(1)}, bf16[4,256,128]{2,1,0:T(8,128)(2,1)}, u32[]{:S(2)}) copy-start(bf16[4,256,128]{2,1,0:T(8,128)(2,1)} %copy-done.28) | copy-start | bytes 786436
  51.0 4.5 %copy-start.7 = (f32[4,256,512]{2,1,0:T(8,128)S(1)}, f32[4,256,512]{2,1,0:T(8,128)}, u32[]{:S(2)}) copy-start(f32[4,256,512]{2,1,0:T(8,128)} %copy-done.6) | copy-start | bytes 6291460
  51.0 4.5 %copy-start.17 = (bf16[4,256,512]{2,1,0:T(8,128)(2,1)S(1)}, bf16[4,256,512]{2,1,0:T(8,128)(2,1)}, u32[]{:S(2)}) copy-start(bf16[4,256,512]{2,1,0:T(8,128)(2,1)} %copy-done.16) | copy-start | bytes 3145732
  55.5 4.5 %copy-start.15 = (bf16[4,256,512]{2,1,0:T(8,128)(2,1)S(1)}, bf16[4,256,512]{2,1,0:T(8,128)(2,1)}, u32[]{:S(2)}) copy-start(bf16[4,256,512]{2,1,0:T(8,128)(2,1)} %copy-done.14) | copy-start | bytes 3145732
  55.6 4.5 %copy-start.21 = (bf16[4,256,128]{2,1,0:T(8,128)(2,1)S(1)}, bf16[4,256,128]{2,1,0:T(8,128)(2,1)}, u32[]{:S(2)}) copy-start(bf16[4,256,128]{2,1,0:T(8,128)(2,1)} %copy-done.20) | copy-start | bytes 786436
  55.6 4.5 %copy-start.23 = (bf16[4,256,128]{2,1,0:T(8,128)(2,1)S(1)}, bf16[4,256,128]{2,1,0:T(8,128)(2,1)}, u32[]{:S(2)}) copy-start(bf16[4,256,128]{2,1,0:T(8,128)(2,1)} %copy-done.22) | copy-start | bytes 786436
  64.5 2.5 %collective-permute-start.12 = (f32[8,176,128]{2,1,0:T(8,128)}, f32[8,176,128]{2,1,0:T(8,128)S(1)}, u32[]{:S(2)}, u32[]{:S(2)}) collective-permute-start(f32[8,176,128]{2,1,0:T(8,128)} %get-tuple-element.59), channel_id=1, source_target_pairs={{0,1},{1,0},{2,3},{3,2},{4,5},{5,4},{6,7},{7,6},{8,9},{9,8},{10,11... | collective-permute-start | bytes 2162696 | tf_op jit(solution)/shard_map/ppermute | solution.py:349
  67.6 8.5 %collective-permute-start.13 = (bf16[176,128]{1,0:T(8,128)(2,1)S(1)}, bf16[176,128]{1,0:T(8,128)(2,1)S(1)}, u32[]{:S(2)}, u32[]{:S(2)}) collective-permute-start(bf16[176,128]{1,0:T(8,128)(2,1)S(1)} %get-tuple-element.61), channel_id=1, source_target_pairs={{0,10},{1,11},{2,8},{3,9},{4,14},{5,15},{6,12},{7,13},{8,2},{9,3},... | collective-permute-start | bytes 135176 | tf_op jit(solution)/shard_map/ppermute | solution.py:359
  70.3 6.8 %collective-permute-start.14 = (bf16[176,128]{1,0:T(8,128)(2,1)S(1)}, bf16[176,128]{1,0:T(8,128)(2,1)S(1)}, u32[]{:S(2)}, u32[]{:S(2)}) collective-permute-start(bf16[176,128]{1,0:T(8,128)(2,1)S(1)} %get-tuple-element.62), channel_id=1, source_target_pairs={{0,14},{1,15},{2,12},{3,13},{4,10},{5,11},{6,8},{7,9},{8,6},{9,7},... | collective-permute-start | bytes 135176 | tf_op jit(solution)/shard_map/ppermute | solution.py:359
  72.5 7.4 %collective-permute-start.15 = (bf16[176,128]{1,0:T(8,128)(2,1)S(1)}, bf16[176,128]{1,0:T(8,128)(2,1)S(1)}, u32[]{:S(2)}, u32[]{:S(2)}) collective-permute-start(bf16[176,128]{1,0:T(8,128)(2,1)S(1)} %get-tuple-element.63), channel_id=1, source_target_pairs={{0,8},{1,9},{2,10},{3,11},{4,12},{5,13},{6,14},{7,15},{8,0},{9,1},... | collective-permute-start | bytes 135176 | tf_op jit(solution)/shard_map/ppermute | solution.py:359
  74.2 6.3 %collective-permute-start.16 = (bf16[176,128]{1,0:T(8,128)(2,1)S(1)}, bf16[176,128]{1,0:T(8,128)(2,1)S(1)}, u32[]{:S(2)}, u32[]{:S(2)}) collective-permute-start(bf16[176,128]{1,0:T(8,128)(2,1)S(1)} %get-tuple-element.64), channel_id=1, source_target_pairs={{0,12},{1,13},{2,14},{3,15},{4,8},{5,9},{6,10},{7,11},{8,4},{9,5},... | collective-permute-start | bytes 135176 | tf_op jit(solution)/shard_map/ppermute | solution.py:359
  74.9 6.1 %collective-permute-start.17 = (bf16[176,128]{1,0:T(8,128)(2,1)S(1)}, bf16[176,128]{1,0:T(8,128)(2,1)S(1)}, u32[]{:S(2)}, u32[]{:S(2)}) collective-permute-start(bf16[176,128]{1,0:T(8,128)(2,1)S(1)} %get-tuple-element.65), channel_id=1, source_target_pairs={{0,6},{1,7},{2,4},{3,5},{4,2},{5,3},{6,0},{7,1},{8,14},{9,15},{10,... | collective-permute-start | bytes 135176 | tf_op jit(solution)/shard_map/ppermute | solution.py:359
  76.1 5.0 %collective-permute-start.18 = (bf16[176,128]{1,0:T(8,128)(2,1)S(1)}, bf16[176,128]{1,0:T(8,128)(2,1)S(1)}, u32[]{:S(2)}, u32[]{:S(2)}) collective-permute-start(bf16[176,128]{1,0:T(8,128)(2,1)S(1)} %get-tuple-element.66), channel_id=1, source_target_pairs={{0,4},{1,5},{2,6},{3,7},{4,0},{5,1},{6,2},{7,3},{8,12},{9,13},{10,... | collective-permute-start | bytes 135176 | tf_op jit(solution)/shard_map/ppermute | solution.py:359
  77.1 4.3 %collective-permute-start.19 = (bf16[176,128]{1,0:T(8,128)(2,1)S(1)}, bf16[176,128]{1,0:T(8,128)(2,1)S(1)}, u32[]{:S(2)}, u32[]{:S(2)}) collective-permute-start(bf16[176,128]{1,0:T(8,128)(2,1)S(1)} %get-tuple-element.67), channel_id=1, source_target_pairs={{0,2},{1,3},{2,0},{3,1},{4,6},{5,7},{6,4},{7,5},{8,10},{9,11},{10,... | collective-permute-start | bytes 135176 | tf_op jit(solution)/shard_map/ppermute | solution.py:359
  (7 other events, 5.6 us)

commit v2 on v1

--- a/solution.py
+++ b/solution.py
@@ -14,7 +14,7 @@
 TILE = 16
 F32 = jnp.float32
 BF16 = jnp.bfloat16
-VMEM_LIMIT = 32 * 1024 * 1024
+VMEM_LIMIT = 16 * 1024 * 1024
 SMALL_LIMIT = 16 * 1024 * 1024
 LINK = BF16
 GELU_A = math.sqrt(2.0 / math.pi)
@@ -27,6 +27,10 @@
 
 def tn(a, b):
     return lax.dot_general(a, b, (((0,), (0,)), ((), ())), preferred_element_type=F32)
+
+
+def in_hbm(v):
+    return pltpu.with_memory_space_constraint(v, pltpu.HBM)
 
 
 def noise_row(seed, width):
@@ -39,17 +43,46 @@
     return (rest.astype(F32) / 65521.0 - 0.5) * 2.0
 
 
-def forward_body(sub, seeds, bias, latents, weight_in, weight_out, outputs, hidden, slope):
-    group, block, depth = latents.shape
-    width = bias.shape[1]
-    first = pl.program_id(0) * group
-    parts = []
-    for k in range(group):
-        shift = bias[...] + noise_row(seeds[first + k], width)
-        for r in range(block // sub):
-            parts.append((k, r, shift))
-    w_in = weight_in[...]
-    w_out = weight_out[...]
+def forward_body(first, sub, stage, *refs):
+    seeds_in, bias_in, latents_in, w_in_ref, w_out_ref, *refs = refs
+    if stage:
+        outputs, hidden, slope, bias_ref, w_in_kept, w_out_kept, *refs = refs
+    else:
+        outputs, hidden, slope, *refs = refs
+    latents, seeds, sems = refs
+    members, size, depth = latents.shape
+    copies = [
+        pltpu.make_async_copy(latents_in.at[m, pl.ds(first, size), :], latents.at[m], sems.at[m])
+        for m in range(members)
+    ]
+    seed_copy = pltpu.make_async_copy(seeds_in, seeds, sems.at[members])
+    seed_copy.start()
+    if stage:
+        loads = [
+            pltpu.make_async_copy(w_in_ref, w_in_kept, sems.at[members + 1]),
+            pltpu.make_async_copy(bias_in, bias_ref, sems.at[members + 2]),
+            pltpu.make_async_copy(w_out_ref, w_out_kept, sems.at[members + 3]),
+        ]
+        w_in_ref, bias_in, w_out_ref = w_in_kept, bias_ref, w_out_kept
+        loads[0].start()
+        copies[0].start()
+        loads[1].start()
+        loads[2].start()
+        for copy in copies[1:]:
+            copy.start()
+    else:
+        for copy in copies:
+            copy.start()
+    seed_copy.wait()
+    if stage:
+        for load in loads[1:]:
+            load.wait()
+    width = bias_in.shape[1]
+    shifts = [bias_in[...] + noise_row(seeds[m], width) for m in range(members)]
+    if stage:
+        loads[0].wait()
+    w_in = w_in_ref[...]
+    w_out = w_out_ref[...]
     ahead = None
     behind = None
 
@@ -65,44 +98,41 @@
     def finish(k, rows, low):
         outputs[k, rows, :] = jnp.dot(low, w_out, preferred_element_type=F32).astype(BF16)
 
-    for k, r, shift in parts:
-        rows = pl.ds(r * sub, sub)
-        x = jnp.dot(latents[k, rows, :], w_in, preferred_element_type=F32) + shift
-        if behind is not None:
-            finish(*behind)
-        behind = activate(*ahead) if ahead is not None else None
-        ahead = (k, rows, x)
+    for k in range(members):
+        copies[k].wait()
+        for r in range(size // sub):
+            rows = pl.ds(r * sub, sub)
+            x = jnp.dot(latents[k, rows, :], w_in, preferred_element_type=F32) + shifts[k]
+            if behind is not None:
+                finish(*behind)
+            behind = activate(*ahead) if ahead is not None else None
+            ahead = (k, rows, x)
     if behind is not None:
         finish(*behind)
     finish(*activate(*ahead))
 
 
-def forward(seeds, bias, latents, weight_in, weight_out, first, size, sub=256, group=2, most=256):
+def forward(seeds, bias, latents, weight_in, weight_out, first, size, stage=False, sub=256):
     members, _, depth = latents.shape
     width, variables = weight_out.shape
-    block = min(most, math.gcd(first, size) if first else size)
-    steps = size // block
-    base = first // block
     whole = pl.BlockSpec(memory_space=pltpu.VMEM)
+    far = pl.BlockSpec(memory_space=pltpu.HBM)
+    near = far if stage else whole
+    kept = [bias, weight_in, weight_out] if stage else []
     return pl.pallas_call(
-        partial(forward_body, min(sub, block)),
-        grid=(members // group, steps),
-        in_specs=[
-            pl.BlockSpec(memory_space=pltpu.SMEM),
-            whole,
-            pl.BlockSpec((group, block, depth), lambda m, s: (m, base + s, 0)),
-            whole,
-            whole,
-        ],
-        out_specs=[
-            pl.BlockSpec((group, block, variables), lambda m, s: (m, s, 0)),
-            pl.BlockSpec((group, block, width), lambda m, s: (m, s, 0)),
-            pl.BlockSpec((group, block, width), lambda m, s: (m, s, 0)),
-        ],
+        partial(forward_body, first, min(sub, size), stage),
+        in_specs=[far, near, far, near, near],
+        out_specs=[whole] * (3 + len(kept)),
         out_shape=[
             jax.ShapeDtypeStruct((members, size, variables), BF16),
             jax.ShapeDtypeStruct((members, size, width), BF16),
             jax.ShapeDtypeStruct((members, size, width), F32),
+        ]
+        + [jax.ShapeDtypeStruct(v.shape, v.dtype) for v in kept],
+        scratch_shapes=[
+            pltpu.VMEM((members, size, depth), BF16),
+            pltpu.SMEM((members,), jnp.int32),
+            pltpu.SemaphoreType.DMA((members + 4,)),
         ],
         compiler_params=pltpu.CompilerParams(vmem_limit_bytes=VMEM_LIMIT),
         cost_estimate=pl.CostEstimate(
@@ -111,7 +141,13 @@
             transcendentals=members * size * width,
         ),
         name="forward",
-    )(seeds, bias, latents, weight_in, weight_out)
+    )(
+        in_hbm(seeds),
+        in_hbm(bias) if stage else bias,
+        in_hbm(latents),
+        in_hbm(weight_in) if stage else weight_in,
+        in_hbm(weight_out) if stage else weight_out,
+    )
 
 
 def pair_tiles(own, others, targets, area, grad, start, unroll, first, loss_coef):
@@ -164,27 +200,21 @@
         grad[:, pl.ds(row, TILE), :] = value.astype(BF16).reshape(members, TILE, variables)
 
 
-def backward_body(n_others, first, loss_coef, has_total, unroll, sub, dests, *refs):
-    if dests:
-        where, *refs = refs
+def backward_body(n_others, n_after, first, loss_coef, has_total, unroll, sub, dests, *refs):
     own, *refs = refs
     others, refs = refs[:n_others], refs[n_others:]
-    targets, area, hidden_in, slope_in, latents_in, weight_out, *refs = refs
+    targets, area, hidden, slope, latents_in, weight_out, *refs = refs
     if has_total:
         in_prior, out_prior, bias_prior, *refs = refs
+    refs = refs[n_after:]
     if dests:
         keep, send, *refs = refs
     else:
         in_total, out_total, bias_total, *refs = refs
-    grad, hidden, slope, latents, low, sems = refs
+    grad, latents, low, sem = refs
     members, size, variables = own.shape
-    copies = [
-        pltpu.make_async_copy(slope_in, slope, sems.at[0]),
-        pltpu.make_async_copy(hidden_in, hidden, sems.at[1]),
-        pltpu.make_async_copy(latents_in.at[:, pl.ds(first, size), :], latents, sems.at[2]),
-    ]
-    for copy in copies:
-        copy.start()
+    copy = pltpu.make_async_copy(latents_in.at[:, pl.ds(first, size), :], latents, sem)
+    copy.start()
 
     @pl.loop(0, size // TILE // unroll)
     def _(t):
@@ -193,15 +223,13 @@
     w_out = weight_out[...]
     width = w_out.shape[0]
     bias_sum = bias_prior[...] if has_total else jnp.zeros((TILE, width), F32)
-    copies[0].wait()
     for m in range(members):
         for r in range(size // sub):
             rows = pl.ds(r * sub, sub)
             pre = nt(grad[m, rows, :], w_out) * slope[m, rows, :]
             bias_sum += jnp.sum(pre.reshape(sub // TILE, TILE, width), axis=0)
             low[m, rows, :] = pre.astype(BF16)
-    copies[1].wait()
-    copies[2].wait()
+    copy.wait()
     flat = lambda ref: ref[...].reshape(members * size, ref.shape[2])
     out_sum = tn(flat(hidden), flat(grad))
     in_sum = tn(flat(latents), flat(low))
@@ -213,7 +241,7 @@
         out_total[...] = out_sum
         bias_total[...] = bias_sum
         return
-    core = where[0]
+    core = lax.axis_index("mem") & 1
     share = in_sum.shape[0] // dests
     lanes = out_sum.shape[1]
     groups = width // lanes
@@ -237,12 +265,12 @@
                 send[place] = block
 
 
-def backward(own, others, targets, area, hidden, slope, latents, weight_out, prior, first, loss_coef, core=None, dests=0, unroll=8, sub=256):
+def backward(own, others, targets, area, hidden, slope, latents, weight_out, prior, first, loss_coef, dests=0, after=None, unroll=8, sub=256):
     members, size, variables = own.shape
     depth = latents.shape[2]
     width = weight_out.shape[0]
     whole = pl.BlockSpec(memory_space=pltpu.VMEM)
-    anywhere = pl.BlockSpec(memory_space=pl.ANY)
+    far = pl.BlockSpec(memory_space=pltpu.HBM)
     count = members * (1 + len(others))
     if dests:
         rows = depth // dests * (width // variables + 1) + TILE
@@ -254,20 +282,18 @@
             jax.ShapeDtypeStruct((TILE, width), F32),
         ]
     return pl.pallas_call(
-        partial(backward_body, len(others), first, loss_coef, prior is not None, min(unroll, size // TILE), min(sub, size), dests),
-        in_specs=([pl.BlockSpec(memory_space=pltpu.SMEM)] if dests else [])
-        + [whole] * (3 + len(others))
-        + [anywhere] * 3 + [whole]
-        + ([whole] * 3 if prior is not None else []),
+        partial(backward_body, len(others), 0 if after is None else 1, first, loss_coef, prior is not None, min(unroll, size // TILE), min(sub, size), dests),
+        in_specs=[whole] * (3 + len(others))
+        + [whole, whole, far, whole]
+        + ([whole] * 3 if prior is not None else [])
+        + ([pl.BlockSpec(memory_space=pl.ANY)] if after is not None else []),
         out_specs=[whole] * len(shapes),
         out_shape=shapes,
         scratch_shapes=[
             pltpu.VMEM((members, size, variables), BF16),
-            pltpu.VMEM((members, size, width), BF16),
-            pltpu.VMEM((members, size, width), F32),
             pltpu.VMEM((members, size, depth), BF16),
             pltpu.VMEM((members, size, width), BF16),
-            pltpu.SemaphoreType.DMA((3,)),
+            pltpu.SemaphoreType.DMA,
         ],
         compiler_params=pltpu.CompilerParams(vmem_limit_bytes=VMEM_LIMIT),
         cost_estimate=pl.CostEstimate(
@@ -276,14 +302,14 @@
             transcendentals=0,
         ),
         name="backward",
-    )(*([core] if dests else []), own, *others, targets, area, hidden, slope, latents, weight_out, *(prior or ()))
+    )(own, *others, targets, area, hidden, slope, in_hbm(latents), weight_out, *(prior or ()), *(() if after is None else (after,)))
 
 
 OFFSETS = ((2, 1), (3, 1), (2, 0), (3, 0), (1, 1), (1, 0), (0, 1))
 
 
-def spread_body(where, keep, arrived, mine, *parts):
-    z, x = where[0], where[1]
+def spread_body(keep, arrived, mine, *parts):
+    z, x = lax.axis_index("pts"), lax.axis_index("mem") >> 1
     here = z * 2 + x
     mine[...] = keep[here] + arrived[here]
     for part, (dz, dx) in zip(parts, OFFSETS):
@@ -291,21 +317,21 @@
         part[...] = (keep[there] + arrived[there]).astype(part.dtype)
 
 
-def spread_out(where, keep, arrived, dtype):
+def spread_out(keep, arrived, dtype):
     _, rows, lanes = keep.shape
     whole = pl.BlockSpec(memory_space=pltpu.VMEM)
     return pl.pallas_call(
         spread_body,
-        in_specs=[pl.BlockSpec(memory_space=pltpu.SMEM), whole, whole],
+        in_specs=[whole, whole],
         out_specs=[whole] * (1 + len(OFFSETS)),
         out_shape=[jax.ShapeDtypeStruct((rows, lanes), F32)]
         + [jax.ShapeDtypeStruct((rows, lanes), dtype)] * len(OFFSETS),
         compiler_params=pltpu.CompilerParams(vmem_limit_bytes=SMALL_LIMIT),
         name="spread_out",
-    )(where, keep, arrived)
-
-
-def finish_body(share, where, mine, *refs):
+    )(keep, arrived)
+
+
+def finish_body(share, mine, *refs):
     parts, (in_share, out_share, bias_share) = refs[:-3], refs[-3:]
     total = mine[...]
     for part in parts:
@@ -316,19 +342,19 @@
         in_share[:, q * lanes : (q + 1) * lanes] = total[q * share : (q + 1) * share]
     out_share[...] = total[groups * share : (groups + 1) * share]
     row = jnp.sum(total[(groups + 1) * share :], axis=0, keepdims=True)
-    place = where[2]
+    place = lax.axis_index("mem")
     picked = row[:, :share]
     for k in range(1, lanes // share):
         picked = jnp.where(place == k, row[:, k * share : (k + 1) * share], picked)
     bias_share[...] = picked
 
 
-def finish(where, mine, parts, share, width):
+def finish(mine, parts, share, width):
     lanes = mine.shape[1]
     whole = pl.BlockSpec(memory_space=pltpu.VMEM)
     return pl.pallas_call(
         partial(finish_body, share),
-        in_specs=[pl.BlockSpec(memory_space=pltpu.SMEM)] + [whole] * (1 + len(parts)),
+        in_specs=[whole] * (1 + len(parts)),
         out_specs=[whole] * 3,
         out_shape=[
             jax.ShapeDtypeStruct((share, width), F32),
@@ -337,7 +363,7 @@
         ],
         compiler_params=pltpu.CompilerParams(vmem_limit_bytes=SMALL_LIMIT),
         name="finish",
-    )(where, mine, *parts)
+    )(mine, *parts)
 
 
 def area_of(lat_row, rows_total):
@@ -357,15 +383,6 @@
         for m in range(members)
     ]
     return lax.ppermute(block, ("pts", "mem"), pairs)
-
-
-def gather_members(block):
-    held = [block]
-    bit = lax.axis_size("mem") // 2
-    while bit:
-        held += [swap_members(b, bit) for b in held]
-        bit //= 2
-    return held
 
 
 CHUNKS = (256, 256, 256, 256)
@@ -389,32 +406,38 @@
     area = jnp.broadcast_to(area_of(lat_row, LAT_ROWS)[:, None], (points, variables))
     bias_row = bias_in[None, :]
     packed = dests == 16 and devices_mem == 4
-    mem = lax.axis_index("mem")
-    pts = lax.axis_index("pts")
     plan = list(chunks_of(points))
-    done = []
+    bits = [1 << k for k in reversed(range(devices_mem.bit_length() - 1))]
+    saved = []
     for first, size in plan:
-        out, hidden, slope = forward(
-            member_seeds, bias_row, latents, weight_in, weight_out, first, size
-        )
-        done.append((gather_members(out), hidden, slope))
+        if first == 0:
+            out, hidden, slope, bias_row, weight_in, weight_near = forward(
+                member_seeds, bias_row, latents, weight_in, weight_out, first, size, stage=True
+            )
+        else:
+            out, hidden, slope = forward(
+                member_seeds, bias_row, latents, weight_in, weight_near, first, size
+            )
+        saved.append([[out, swap_members(out, bits[0])], hidden, slope])
     total = None
-    core = (mem & 1).astype(jnp.int32).reshape(1)
-    for (first, size), (held, hidden, slope) in zip(plan, done):
+    for k, (first, size) in enumerate(plan):
+        held, hidden, slope = saved[k]
+        for bit in bits[1:]:
+            held = held + [swap_members(v, bit) for v in held]
         last = first + size == points
-        total = backward(
-            held[0], held[1:], targets, area, hidden, slope, latents, weight_out, total,
-            first, loss_coef, core, dests if last and packed else 0,
-        )
+        total = list(backward(
+            held[0], held[1:], targets, area, hidden, slope, latents, weight_near, total,
+            first, loss_coef, dests if last and packed else 0,
+            after=saved[-1][0][0] if k == 0 else None,
+        ))
     if not packed:
         scatter = lambda v: lax.psum_scatter(v, ("pts", "mem"), scatter_dimension=0, tiled=True)
         return scatter(total[0]), scatter(total[1]), scatter(jnp.sum(total[2], axis=0))
     keep, send = total
     arrived = swap_members(send, 1)
-    where = jnp.stack([pts, mem >> 1, mem]).astype(jnp.int32)
-    mine, *parts = spread_out(where, keep, arrived, LINK)
+    mine, *parts = spread_out(keep, arrived, LINK)
     parts = [swap_points(part, dz, dx) for part, (dz, dx) in zip(parts, OFFSETS)]
-    in_share, out_share, bias_share = finish(where, mine, parts, depth // dests, width)
+    in_share, out_share, bias_share = finish(mine, parts, depth // dests, width)
     return in_share, out_share, bias_share.reshape(depth // dests)
 
 

time: 83.2 us -> 61.6 us (0.74)
  local copies, waits for them, and re-layouts: 20.7 us -> 0.2 us
  Pallas kernels: 30.1 us -> 27.3 us
  waiting for transfers between devices: 13.3 us -> 15.2 us
    unnamed x70 -> x4, local copies, waits for them, and re-layouts: 20.5 us -> 0.01 us
    pallas_call x10, Pallas kernels: 30.1 us -> 27.3 us  [the longest x4 14.2 us: forward(): pl.pallas_call(partial(forward_body, first, min(sub, size), stage), in_sp...]
    ppermute x13, waiting for transfers between devices: 10.4 us -> 11.8 us  [swap_members(): return lax.ppermute(block, 'mem', [(i, i ^ bit) for i in range(size)])]
  transfers between devices with their start and end apart: 20 -> 20, of which waited for: 7 -> 7; matrix products, arithmetic and copies ran while one was open for 0% -> 0% of each run, Pallas kernels for 25% -> 32%
where the time goes in v2:
time: 61.6 us; the launch traced here: 61.4 us
  Pallas kernels  27.3 us (44%)
  starting transfers between devices  17.9 us (29%)
  waiting for transfers between devices  15.2 us (25%)
  between operations  0.8 us (1%)
    pallas_call x4, Pallas kernels, forward(): pl.pallas_call(partial(forward_body, first, min(sub, size), stage), in_sp...  14.2 us
    pallas_call x4, Pallas kernels, backward(): pl.pallas_call(partial(backward_body, len(others), 0 if after is None els...  12.2 us
    ppermute x13, waiting for transfers between devices, swap_members(): return lax.ppermute(block, 'mem', [(i, i ^ bit) for i in range(size)])  11.8 us
    ppermute x7, starting transfers between devices, swap_points(): return lax.ppermute(block, ('pts', 'mem'), pairs)  10.9 us
    ppermute x13, starting transfers between devices, swap_members(): return lax.ppermute(block, 'mem', [(i, i ^ bit) for i in range(size)])  6.98 us
    ppermute x7, waiting for transfers between devices, swap_points(): return lax.ppermute(block, ('pts', 'mem'), pairs)  3.37 us
  transfers between devices with their start and end apart: 20, of which 7 were waited for; matrix products, arithmetic and copies ran while one was open for 0% of the time, Pallas kernels for 32%

profile of v2, /device:TPU:0, one launch (start us, length us, event | category | flops | bytes accessed | tf_op | source)
XLA Modules:
  0.0 61.4 jit_solution(11976602873155588942)
XLA Ops:
  0.6 3.8 %forward.4 = (bf16[4,256,128]{2,1,0:T(8,128)(2,1)S(1)}, bf16[4,256,512]{2,1,0:T(8,128)(2,1)S(1)}, f32[4,256,512]{2,1,0:T(8,128)S(1)}, f32[1,512]{1,0:T(1,128)S(1...) custom-call(s32[4]{0:T(128)} %refs_0_.7, f32[1,512]{1,0:T(1,128)} %bitcast.2, ...), custom_call_target="tpu_custom_call" | custom-call | flops 671088640 | bytes 4456448 | tf_op jit(solution)/shard_map/forward/pallas_call | solution.py:122
  4.4 3.0 %collective-permute-start.9 = (bf16[4,256,128]{2,1,0:T(8,128)(2,1)S(1)}, bf16[4,256,128]{2,1,0:T(8,128)(2,1)S(1)}, u32[]{:S(2)}, u32[]{:S(2)}) collective-permute-start(bf16[4,256,128]{2,1,0:T(8,128)(2,1)S(1)} %get-tuple-element.52.refs_0_), channel_id=1, source_target_pairs={{0,2},{1,3},{2,0},{3,1},{4,6},{5,7},{6,4},{7,5},{8,10},{9,11},{10,... | collective-permute-start | bytes 786440 | tf_op jit(solution)/shard_map/ppermute | solution.py:375
  7.4 0.0 collective-permute-start.10
  7.4 3.5 %forward.7 = (bf16[4,256,128]{2,1,0:T(8,128)(2,1)S(1)}, bf16[4,256,512]{2,1,0:T(8,128)(2,1)S(1)}, f32[4,256,512]{2,1,0:T(8,128)S(1)}) custom-call(s32[4]{0:T(128)} %refs_0_.7, f32[1,512]{1,0:T(1,128)S(1)} %get-tuple-element.40.refs_1_, bf16[4,1024,512]{2,1,0:T(8,128)(2,1)} %refs_8_.7, bf16[512,512]{1,0:T(8,128)(2,1)S(1)} %get-tuple-element.41.refs_3_, ...), custom_call_target="tpu_custom_call" | custom-call | flops 671088640 | bytes 4456448 | tf_op jit(solution)/shard_map/forward/pallas_call | solution.py:122
  10.9 0.2 collective-permute-start.6
  11.1 0.5 collective-permute-start.7
  11.6 3.5 %forward.6 = (bf16[4,256,128]{2,1,0:T(8,128)(2,1)S(1)}, bf16[4,256,512]{2,1,0:T(8,128)(2,1)S(1)}, f32[4,256,512]{2,1,0:T(8,128)S(1)}) custom-call(s32[4]{0:T(128)} %refs_0_.7, f32[1,512]{1,0:T(1,128)S(1)} %get-tuple-element.40.refs_1_, bf16[4,1024,512]{2,1,0:T(8,128)(2,1)} %refs_8_.7, bf16[512,512]{1,0:T(8,128)(2,1)S(1)} %get-tuple-element.41.refs_3_, ...), custom_call_target="tpu_custom_call" | custom-call | flops 671088640 | bytes 4456448 | tf_op jit(solution)/shard_map/forward/pallas_call | solution.py:122
  15.0 0.0 copy-start.1
  15.0 0.0 copy-start
  15.0 1.7 %collective-permute-start.3 = (bf16[4,256,128]{2,1,0:T(8,128)(2,1)S(1)}, bf16[4,256,128]{2,1,0:T(8,128)(2,1)S(1)}, u32[]{:S(2)}, u32[]{:S(2)}) collective-permute-start(bf16[4,256,128]{2,1,0:T(8,128)(2,1)S(1)} %get-tuple-element.46.refs_0_), channel_id=1, source_target_pairs={{0,2},{1,3},{2,0},{3,1},{4,6},{5,7},{6,4},{7,5},{8,10},{9,11},{10,... | collective-permute-start | bytes 786440 | tf_op jit(solution)/shard_map/ppermute | solution.py:375
  16.8 3.5 %forward.5 = (bf16[4,256,128]{2,1,0:T(8,128)(2,1)S(1)}, bf16[4,256,512]{2,1,0:T(8,128)(2,1)S(1)}, f32[4,256,512]{2,1,0:T(8,128)S(1)}) custom-call(s32[4]{0:T(128)} %refs_0_.7, f32[1,512]{1,0:T(1,128)S(1)} %get-tuple-element.40.refs_1_, bf16[4,1024,512]{2,1,0:T(8,128)(2,1)} %refs_8_.7, bf16[512,512]{1,0:T(8,128)(2,1)S(1)} %get-tuple-element.41.refs_3_, ...), custom_call_target="tpu_custom_call" | custom-call | flops 671088640 | bytes 4456448 | tf_op jit(solution)/shard_map/forward/pallas_call | solution.py:122
  20.3 0.0 collective-permute-done.9.refs_1_
  20.3 0.4 collective-permute-start
  20.7 0.0 collective-permute-done.10.refs_2_
  20.7 0.0 collective-permute-start.11
  20.7 0.0 collective-permute-done.6.refs_1_
  20.7 0.5 collective-permute-start.4
  21.2 0.0 collective-permute-done.7.refs_2_
  21.2 0.1 collective-permute-start.8
  21.3 4.4 %collective-permute-done.3.refs_1_ = bf16[4,256,128]{2,1,0:T(8,128)(2,1)S(1)} collective-permute-done((bf16[4,256,128]{2,1,0:T(8,128)(2,1)S(1)}, bf16[4,256,128]{2,1,0:T(8,128)(2,1)S(1)}, u32[]{:S(2)}, u32[]{:S(2)}) %collective-permute-start.3) | collective-permute-done | bytes 262176 | tf_op jit(solution)/shard_map/ppermute | solution.py:375
  25.7 0.0 collective-permute-start.5
  25.7 5.2 %collective-permute-done.refs_1_ = bf16[4,256,128]{2,1,0:T(8,128)(2,1)S(1)} collective-permute-done((bf16[4,256,128]{2,1,0:T(8,128)(2,1)S(1)}, bf16[4,256,128]{2,1,0:T(8,128)(2,1)S(1)}, u32[]{:S(2)}, u32[]{:S(2)}) %collective-permute-start) | collective-permute-done | bytes 262176 | tf_op jit(solution)/shard_map/ppermute | solution.py:375
  30.9 0.0 collective-permute-done.11.refs_3_
  30.9 0.5 collective-permute-start.2
  31.4 0.2 broadcast_in_dim.10.refs_5_
  31.6 3.1 %backward.4 = (f32[512,512]{1,0:T(8,128)S(1)}, f32[512,128]{1,0:T(8,128)S(1)}, f32[16,512]{1,0:T(8,128)S(1)}) custom-call(bf16[4,256,128]{2,1,0:T(8,128)(2,1)S(1)} %get-tuple-element.52.refs_0_, bf16[4,256,128]{2,1,0:T(8,128)(2,1)S(1)} %collective-permute-done.9.refs_1_, bf16[4,256,128]{2,1,0:T(8,128)(2,1)S(1)} %collective-permute-done.10.refs_2_, ...), custom_call_target="tpu_custom_call" | custom-call | flops 1006632960 | bytes 4456448 | tf_op jit(solution)/shard_map/backward/pallas_call | solution.py:284
  34.8 3.0 %backward.5 = (f32[512,512]{1,0:T(8,128)S(1)}, f32[512,128]{1,0:T(8,128)S(1)}, f32[16,512]{1,0:T(8,128)S(1)}) custom-call(bf16[4,256,128]{2,1,0:T(8,128)(2,1)S(1)} %get-tuple-element.49.refs_0_, bf16[4,256,128]{2,1,0:T(8,128)(2,1)S(1)} %collective-permute-done.6.refs_1_, bf16[4,256,128]{2,1,0:T(8,128)(2,1)S(1)} %collective-permute-done.7.refs_2_, ...), custom_call_target="tpu_custom_call" | custom-call | flops 1006632960 | bytes 4456448 | tf_op jit(solution)/shard_map/backward/pallas_call | solution.py:284
  37.7 0.0 collective-permute-done.4.refs_2_
  37.8 2.9 %backward.6 = (f32[512,512]{1,0:T(8,128)S(1)}, f32[512,128]{1,0:T(8,128)S(1)}, f32[16,512]{1,0:T(8,128)S(1)}) custom-call(bf16[4,256,128]{2,1,0:T(8,128)(2,1)S(1)} %get-tuple-element.46.refs_0_, bf16[4,256,128]{2,1,0:T(8,128)(2,1)S(1)} %collective-permute-done.3.refs_1_, bf16[4,256,128]{2,1,0:T(8,128)(2,1)S(1)} %collective-permute-done.4.refs_2_, ...), custom_call_target="tpu_custom_call" | custom-call | flops 1006632960 | bytes 4456448 | tf_op jit(solution)/shard_map/backward/pallas_call | solution.py:284
  40.7 0.0 collective-permute-done.1.refs_2_
  40.7 3.1 %backward.7 = (f32[8,176,128]{2,1,0:T(8,128)S(1)}, f32[8,176,128]{2,1,0:T(8,128)S(1)}) custom-call(bf16[4,256,128]{2,1,0:T(8,128)(2,1)S(1)} %get-tuple-element.43.refs_10_.refs_0_, bf16[4,256,128]{2,1,0:T(8,128)(2,1)S(1)} %collective-permute-done.refs_1_, bf16[4,256,128]{2,1,0:T(8,128)(2,1)S(1)} %collective-permute-done.1.refs_2_, ...), custom_call_target="tpu_custom_call" | custom-call | flops 1006632960 | bytes 4456448 | tf_op jit(solution)/shard_map/backward/pallas_call | solution.py:284
  43.9 0.1 collective-permute-start.12
  44.0 2.2 %collective-permute-done.12.arrived = f32[8,176,128]{2,1,0:T(8,128)S(1)} collective-permute-done((f32[8,176,128]{2,1,0:T(8,128)S(1)}, f32[8,176,128]{2,1,0:T(8,128)S(1)}, u32[]{:S(2)}, u32[]{:S(2)}) %collective-permute-start.12) | collective-permute-done | bytes 720928 | tf_op jit(solution)/shard_map/ppermute | solution.py:375
  46.2 0.1 spread_out.1
  46.2 3.5 %collective-permute-start.13 = (bf16[176,128]{1,0:T(8,128)(2,1)S(1)}, bf16[176,128]{1,0:T(8,128)(2,1)S(1)}, u32[]{:S(2)}, u32[]{:S(2)}) collective-permute-start(bf16[176,128]{1,0:T(8,128)(2,1)S(1)} %get-tuple-element.67), channel_id=1, source_target_pairs={{0,10},{1,11},{2,8},{3,9},{4,14},{5,15},{6,12},{7,13},{8,2},{9,3},... | collective-permute-start | bytes 135176 | tf_op jit(solution)/shard_map/ppermute | solution.py:385
  49.7 1.4 %collective-permute-start.14 = (bf16[176,128]{1,0:T(8,128)(2,1)S(1)}, bf16[176,128]{1,0:T(8,128)(2,1)S(1)}, u32[]{:S(2)}, u32[]{:S(2)}) collective-permute-start(bf16[176,128]{1,0:T(8,128)(2,1)S(1)} %get-tuple-element.68), channel_id=1, source_target_pairs={{0,14},{1,15},{2,12},{3,13},{4,10},{5,11},{6,8},{7,9},{8,6},{9,7},... | collective-permute-start | bytes 135176 | tf_op jit(solution)/shard_map/ppermute | solution.py:385
  51.1 1.7 %collective-permute-start.15 = (bf16[176,128]{1,0:T(8,128)(2,1)S(1)}, bf16[176,128]{1,0:T(8,128)(2,1)S(1)}, u32[]{:S(2)}, u32[]{:S(2)}) collective-permute-start(bf16[176,128]{1,0:T(8,128)(2,1)S(1)} %get-tuple-element.69), channel_id=1, source_target_pairs={{0,8},{1,9},{2,10},{3,11},{4,12},{5,13},{6,14},{7,15},{8,0},{9,1},... | collective-permute-start | bytes 135176 | tf_op jit(solution)/shard_map/ppermute | solution.py:385
  52.8 0.8 %collective-permute-start.16 = (bf16[176,128]{1,0:T(8,128)(2,1)S(1)}, bf16[176,128]{1,0:T(8,128)(2,1)S(1)}, u32[]{:S(2)}, u32[]{:S(2)}) collective-permute-start(bf16[176,128]{1,0:T(8,128)(2,1)S(1)} %get-tuple-element.70), channel_id=1, source_target_pairs={{0,12},{1,13},{2,14},{3,15},{4,8},{5,9},{6,10},{7,11},{8,4},{9,5},... | collective-permute-start | bytes 135176 | tf_op jit(solution)/shard_map/ppermute | solution.py:385
  53.7 1.8 %collective-permute-start.17 = (bf16[176,128]{1,0:T(8,128)(2,1)S(1)}, bf16[176,128]{1,0:T(8,128)(2,1)S(1)}, u32[]{:S(2)}, u32[]{:S(2)}) collective-permute-start(bf16[176,128]{1,0:T(8,128)(2,1)S(1)} %get-tuple-element.71), channel_id=1, source_target_pairs={{0,6},{1,7},{2,4},{3,5},{4,2},{5,3},{6,0},{7,1},{8,14},{9,15},{10,... | collective-permute-start | bytes 135176 | tf_op jit(solution)/shard_map/ppermute | solution.py:385
  55.5 0.0 collective-permute-done.13.refs_0_
  55.5 1.0 %collective-permute-start.18 = (bf16[176,128]{1,0:T(8,128)(2,1)S(1)}, bf16[176,128]{1,0:T(8,128)(2,1)S(1)}, u32[]{:S(2)}, u32[]{:S(2)}) collective-permute-start(bf16[176,128]{1,0:T(8,128)(2,1)S(1)} %get-tuple-element.72), channel_id=1, source_target_pairs={{0,4},{1,5},{2,6},{3,7},{4,0},{5,1},{6,2},{7,3},{8,12},{9,13},{10,... | collective-permute-start | bytes 135176 | tf_op jit(solution)/shard_map/ppermute | solution.py:385
  56.5 0.7 %collective-permute-start.19 = (bf16[176,128]{1,0:T(8,128)(2,1)S(1)}, bf16[176,128]{1,0:T(8,128)(2,1)S(1)}, u32[]{:S(2)}, u32[]{:S(2)}) collective-permute-start(bf16[176,128]{1,0:T(8,128)(2,1)S(1)} %get-tuple-element.73), channel_id=1, source_target_pairs={{0,2},{1,3},{2,0},{3,1},{4,6},{5,7},{6,4},{7,5},{8,10},{9,11},{10,... | collective-permute-start | bytes 135176 | tf_op jit(solution)/shard_map/ppermute | solution.py:385
  57.2 1.7 %collective-permute-done.15.refs_2_ = bf16[176,128]{1,0:T(8,128)(2,1)S(1)} collective-permute-done((bf16[176,128]{1,0:T(8,128)(2,1)S(1)}, bf16[176,128]{1,0:T(8,128)(2,1)S(1)}, u32[]{:S(2)}, u32[]{:S(2)}) %collective-permute-start.15) | collective-permute-done | bytes 45088 | tf_op jit(solution)/shard_map/ppermute | solution.py:385
  58.9 0.0 collective-permute-done.16.refs_3_
  58.9 0.7 %collective-permute-done.17.refs_4_ = bf16[176,128]{1,0:T(8,128)(2,1)S(1)} collective-permute-done((bf16[176,128]{1,0:T(8,128)(2,1)S(1)}, bf16[176,128]{1,0:T(8,128)(2,1)S(1)}, u32[]{:S(2)}, u32[]{:S(2)}) %collective-permute-start.17) | collective-permute-done | bytes 45088 | tf_op jit(solution)/shard_map/ppermute | solution.py:385
  59.6 0.5 collective-permute-done.18.refs_5_
  60.0 0.5 collective-permute-done.19.refs_6_
  60.5 0.9 %finish.1 = (f32[32,512]{1,0:T(8,128)}, f32[32,128]{1,0:T(8,128)}, f32[1,32]{1,0:T(1,128)}) custom-call(f32[176,128]{1,0:T(8,128)S(1)} %get-tuple-element.66.mine, bf16[176,128]{1,0:T(8,128)(2,1)S(1)} %collective-permute-done.13.refs_0_, bf16[176,128]{1,0:T(8,128)(2,1)S(1)} %collective-permute-done.14.refs_1_, ...), custom_call_target="tpu_custom_call" | custom-call | tf_op jit(solution)/shard_map/finish/pallas_call | solution.py:355
  (8 shorter events, 0.1 us)
Async XLA Ops:
  4.4 15.8 %collective-permute-start.9 = (bf16[4,256,128]{2,1,0:T(8,128)(2,1)S(1)}, bf16[4,256,128]{2,1,0:T(8,128)(2,1)S(1)}, u32[]{:S(2)}, u32[]{:S(2)}) collective-permute-start(bf16[4,256,128]{2,1,0:T(8,128)(2,1)S(1)} %get-tuple-element.52.refs_0_), channel_id=1, source_target_pairs={{0,2},{1,3},{2,0},{3,1},{4,6},{5,7},{6,4},{7,5},{8,10},{9,11},{10,... | collective-permute-start | bytes 786440 | tf_op jit(solution)/shard_map/ppermute | solution.py:375
  7.4 13.3 %collective-permute-start.10 = (bf16[4,256,128]{2,1,0:T(8,128)(2,1)S(1)}, bf16[4,256,128]{2,1,0:T(8,128)(2,1)S(1)}, u32[]{:S(2)}, u32[]{:S(2)}) collective-permute-start(bf16[4,256,128]{2,1,0:T(8,128)(2,1)S(1)} %get-tuple-element.52.refs_0_), channel_id=1, source_target_pairs={{0,1},{1,0},{2,3},{3,2},{4,5},{5,4},{6,7},{7,6},{8,9},{9,8},{10,11... | collective-permute-start | bytes 786440 | tf_op jit(solution)/shard_map/ppermute | solution.py:375
  10.9 9.8 %collective-permute-start.6 = (bf16[4,256,128]{2,1,0:T(8,128)(2,1)S(1)}, bf16[4,256,128]{2,1,0:T(8,128)(2,1)S(1)}, u32[]{:S(2)}, u32[]{:S(2)}) collective-permute-start(bf16[4,256,128]{2,1,0:T(8,128)(2,1)S(1)} %get-tuple-element.49.refs_0_), channel_id=1, source_target_pairs={{0,2},{1,3},{2,0},{3,1},{4,6},{5,7},{6,4},{7,5},{8,10},{9,11},{10,... | collective-permute-start | bytes 786440 | tf_op jit(solution)/shard_map/ppermute | solution.py:375
  11.1 10.2 %collective-permute-start.7 = (bf16[4,256,128]{2,1,0:T(8,128)(2,1)S(1)}, bf16[4,256,128]{2,1,0:T(8,128)(2,1)S(1)}, u32[]{:S(2)}, u32[]{:S(2)}) collective-permute-start(bf16[4,256,128]{2,1,0:T(8,128)(2,1)S(1)} %get-tuple-element.49.refs_0_), channel_id=1, source_target_pairs={{0,1},{1,0},{2,3},{3,2},{4,5},{5,4},{6,7},{7,6},{8,9},{9,8},{10,11... | collective-permute-start | bytes 786440 | tf_op jit(solution)/shard_map/ppermute | solution.py:375
  15.0 10.7 %copy-start.1 = (s32[1024]{0:T(1024)S(1)}, s32[1024]{0:T(1024)}, u32[]{:S(2)}) copy-start(s32[1024]{0:T(1024)} %param.10) | copy-start | bytes 12292
  15.0 16.6 %copy-start = (f32[1024,128]{1,0:T(8,128)S(1)}, f32[1024,128]{1,0:T(8,128)}, u32[]{:S(2)}) copy-start(f32[1024,128]{1,0:T(8,128)} %refs_4_.9) | copy-start | bytes 1572868
  15.0 10.6 %collective-permute-start.3 = (bf16[4,256,128]{2,1,0:T(8,128)(2,1)S(1)}, bf16[4,256,128]{2,1,0:T(8,128)(2,1)S(1)}, u32[]{:S(2)}, u32[]{:S(2)}) collective-permute-start(bf16[4,256,128]{2,1,0:T(8,128)(2,1)S(1)} %get-tuple-element.46.refs_0_), channel_id=1, source_target_pairs={{0,2},{1,3},{2,0},{3,1},{4,6},{5,7},{6,4},{7,5},{8,10},{9,11},{10,... | collective-permute-start | bytes 786440 | tf_op jit(solution)/shard_map/ppermute | solution.py:375
  20.3 10.6 %collective-permute-start = (bf16[4,256,128]{2,1,0:T(8,128)(2,1)S(1)}, bf16[4,256,128]{2,1,0:T(8,128)(2,1)S(1)}, u32[]{:S(2)}, u32[]{:S(2)}) collective-permute-start(bf16[4,256,128]{2,1,0:T(8,128)(2,1)S(1)} %get-tuple-element.43.refs_10_.refs_0_), channel_id=1, source_target_pairs={{0,2},{1,3},{2,0},{3,1},{4,6},{5,7},{6,4},{7,5},{8,10},{9,11},{10,... | collective-permute-start | bytes 786440 | tf_op jit(solution)/shard_map/ppermute | solution.py:375
  20.7 10.2 %collective-permute-start.11 = (bf16[4,256,128]{2,1,0:T(8,128)(2,1)S(1)}, bf16[4,256,128]{2,1,0:T(8,128)(2,1)S(1)}, u32[]{:S(2)}, u32[]{:S(2)}) collective-permute-start(bf16[4,256,128]{2,1,0:T(8,128)(2,1)S(1)} %collective-permute-done.9.refs_1_), channel_id=1, source_target_pairs={{0,1},{1,0},{2,3},{3,2},{4,5},{5,4},{6,7},{7,6},{8,9},{9,8},{10,11... | collective-permute-start | bytes 786440 | tf_op jit(solution)/shard_map/ppermute | solution.py:375
  20.7 17.0 %collective-permute-start.4 = (bf16[4,256,128]{2,1,0:T(8,128)(2,1)S(1)}, bf16[4,256,128]{2,1,0:T(8,128)(2,1)S(1)}, u32[]{:S(2)}, u32[]{:S(2)}) collective-permute-start(bf16[4,256,128]{2,1,0:T(8,128)(2,1)S(1)} %get-tuple-element.46.refs_0_), channel_id=1, source_target_pairs={{0,1},{1,0},{2,3},{3,2},{4,5},{5,4},{6,7},{7,6},{8,9},{9,8},{10,11... | collective-permute-start | bytes 786440 | tf_op jit(solution)/shard_map/ppermute | solution.py:375
  21.2 13.6 %collective-permute-start.8 = (bf16[4,256,128]{2,1,0:T(8,128)(2,1)S(1)}, bf16[4,256,128]{2,1,0:T(8,128)(2,1)S(1)}, u32[]{:S(2)}, u32[]{:S(2)}) collective-permute-start(bf16[4,256,128]{2,1,0:T(8,128)(2,1)S(1)} %collective-permute-done.6.refs_1_), channel_id=1, source_target_pairs={{0,1},{1,0},{2,3},{3,2},{4,5},{5,4},{6,7},{7,6},{8,9},{9,8},{10,11... | collective-permute-start | bytes 786440 | tf_op jit(solution)/shard_map/ppermute | solution.py:375
  25.7 12.1 %collective-permute-start.5 = (bf16[4,256,128]{2,1,0:T(8,128)(2,1)S(1)}, bf16[4,256,128]{2,1,0:T(8,128)(2,1)S(1)}, u32[]{:S(2)}, u32[]{:S(2)}) collective-permute-start(bf16[4,256,128]{2,1,0:T(8,128)(2,1)S(1)} %collective-permute-done.3.refs_1_), channel_id=1, source_target_pairs={{0,1},{1,0},{2,3},{3,2},{4,5},{5,4},{6,7},{7,6},{8,9},{9,8},{10,11... | collective-permute-start | bytes 786440 | tf_op jit(solution)/shard_map/ppermute | solution.py:375
  30.9 9.8 %collective-permute-start.1 = (bf16[4,256,128]{2,1,0:T(8,128)(2,1)S(1)}, bf16[4,256,128]{2,1,0:T(8,128)(2,1)S(1)}, u32[]{:S(2)}, u32[]{:S(2)}) collective-permute-start(bf16[4,256,128]{2,1,0:T(8,128)(2,1)S(1)} %get-tuple-element.43.refs_10_.refs_0_), channel_id=1, source_target_pairs={{0,1},{1,0},{2,3},{3,2},{4,5},{5,4},{6,7},{7,6},{8,9},{9,8},{10,11... | collective-permute-start | bytes 786440 | tf_op jit(solution)/shard_map/ppermute | solution.py:375
  30.9 9.8 %collective-permute-start.2 = (bf16[4,256,128]{2,1,0:T(8,128)(2,1)S(1)}, bf16[4,256,128]{2,1,0:T(8,128)(2,1)S(1)}, u32[]{:S(2)}, u32[]{:S(2)}) collective-permute-start(bf16[4,256,128]{2,1,0:T(8,128)(2,1)S(1)} %collective-permute-done.refs_1_), channel_id=1, source_target_pairs={{0,1},{1,0},{2,3},{3,2},{4,5},{5,4},{6,7},{7,6},{8,9},{9,8},{10,11... | collective-permute-start | bytes 786440 | tf_op jit(solution)/shard_map/ppermute | solution.py:375
  43.9 2.3 %collective-permute-start.12 = (f32[8,176,128]{2,1,0:T(8,128)S(1)}, f32[8,176,128]{2,1,0:T(8,128)S(1)}, u32[]{:S(2)}, u32[]{:S(2)}) collective-permute-start(f32[8,176,128]{2,1,0:T(8,128)S(1)} %get-tuple-element.65), channel_id=1, source_target_pairs={{0,1},{1,0},{2,3},{3,2},{4,5},{5,4},{6,7},{7,6},{8,9},{9,8},{10,11... | collective-permute-start | bytes 2162696 | tf_op jit(solution)/shard_map/ppermute | solution.py:375
  46.2 9.2 %collective-permute-start.13 = (bf16[176,128]{1,0:T(8,128)(2,1)S(1)}, bf16[176,128]{1,0:T(8,128)(2,1)S(1)}, u32[]{:S(2)}, u32[]{:S(2)}) collective-permute-start(bf16[176,128]{1,0:T(8,128)(2,1)S(1)} %get-tuple-element.67), channel_id=1, source_target_pairs={{0,10},{1,11},{2,8},{3,9},{4,14},{5,15},{6,12},{7,13},{8,2},{9,3},... | collective-permute-start | bytes 135176 | tf_op jit(solution)/shard_map/ppermute | solution.py:385
  49.7 6.8 %collective-permute-start.14 = (bf16[176,128]{1,0:T(8,128)(2,1)S(1)}, bf16[176,128]{1,0:T(8,128)(2,1)S(1)}, u32[]{:S(2)}, u32[]{:S(2)}) collective-permute-start(bf16[176,128]{1,0:T(8,128)(2,1)S(1)} %get-tuple-element.68), channel_id=1, source_target_pairs={{0,14},{1,15},{2,12},{3,13},{4,10},{5,11},{6,8},{7,9},{8,6},{9,7},... | collective-permute-start | bytes 135176 | tf_op jit(solution)/shard_map/ppermute | solution.py:385
  51.1 7.7 %collective-permute-start.15 = (bf16[176,128]{1,0:T(8,128)(2,1)S(1)}, bf16[176,128]{1,0:T(8,128)(2,1)S(1)}, u32[]{:S(2)}, u32[]{:S(2)}) collective-permute-start(bf16[176,128]{1,0:T(8,128)(2,1)S(1)} %get-tuple-element.69), channel_id=1, source_target_pairs={{0,8},{1,9},{2,10},{3,11},{4,12},{5,13},{6,14},{7,15},{8,0},{9,1},... | collective-permute-start | bytes 135176 | tf_op jit(solution)/shard_map/ppermute | solution.py:385
  52.8 6.0 %collective-permute-start.16 = (bf16[176,128]{1,0:T(8,128)(2,1)S(1)}, bf16[176,128]{1,0:T(8,128)(2,1)S(1)}, u32[]{:S(2)}, u32[]{:S(2)}) collective-permute-start(bf16[176,128]{1,0:T(8,128)(2,1)S(1)} %get-tuple-element.70), channel_id=1, source_target_pairs={{0,12},{1,13},{2,14},{3,15},{4,8},{5,9},{6,10},{7,11},{8,4},{9,5},... | collective-permute-start | bytes 135176 | tf_op jit(solution)/shard_map/ppermute | solution.py:385
  53.7 5.9 %collective-permute-start.17 = (bf16[176,128]{1,0:T(8,128)(2,1)S(1)}, bf16[176,128]{1,0:T(8,128)(2,1)S(1)}, u32[]{:S(2)}, u32[]{:S(2)}) collective-permute-start(bf16[176,128]{1,0:T(8,128)(2,1)S(1)} %get-tuple-element.71), channel_id=1, source_target_pairs={{0,6},{1,7},{2,4},{3,5},{4,2},{5,3},{6,0},{7,1},{8,14},{9,15},{10,... | collective-permute-start | bytes 135176 | tf_op jit(solution)/shard_map/ppermute | solution.py:385
  55.5 4.5 %collective-permute-start.18 = (bf16[176,128]{1,0:T(8,128)(2,1)S(1)}, bf16[176,128]{1,0:T(8,128)(2,1)S(1)}, u32[]{:S(2)}, u32[]{:S(2)}) collective-permute-start(bf16[176,128]{1,0:T(8,128)(2,1)S(1)} %get-tuple-element.72), channel_id=1, source_target_pairs={{0,4},{1,5},{2,6},{3,7},{4,0},{5,1},{6,2},{7,3},{8,12},{9,13},{10,... | collective-permute-start | bytes 135176 | tf_op jit(solution)/shard_map/ppermute | solution.py:385
  56.5 4.0 %collective-permute-start.19 = (bf16[176,128]{1,0:T(8,128)(2,1)S(1)}, bf16[176,128]{1,0:T(8,128)(2,1)S(1)}, u32[]{:S(2)}, u32[]{:S(2)}) collective-permute-start(bf16[176,128]{1,0:T(8,128)(2,1)S(1)} %get-tuple-element.73), channel_id=1, source_target_pairs={{0,2},{1,3},{2,0},{3,1},{4,6},{5,7},{6,4},{7,5},{8,10},{9,11},{10,... | collective-permute-start | bytes 135176 | tf_op jit(solution)/shard_map/ppermute | solution.py:385

commit v3 on v2

--- a/solution.py
+++ b/solution.py
@@ -15,8 +15,11 @@
 F32 = jnp.float32
 BF16 = jnp.bfloat16
 VMEM_LIMIT = 16 * 1024 * 1024
-SMALL_LIMIT = 16 * 1024 * 1024
+SMALL_LIMIT = 8 * 1024 * 1024
+TINY_LIMIT = 1024 * 1024
 LINK = BF16
+COST = 2
+LAG = 1
 GELU_A = math.sqrt(2.0 / math.pi)
 GELU_B = GELU_A * 0.044715
 
@@ -43,44 +46,33 @@
     return (rest.astype(F32) / 65521.0 - 0.5) * 2.0
 
 
-def forward_body(first, sub, stage, *refs):
-    seeds_in, bias_in, latents_in, w_in_ref, w_out_ref, *refs = refs
+def forward_body(first, size, sub, stage, *refs):
     if stage:
-        outputs, hidden, slope, bias_ref, w_in_kept, w_out_kept, *refs = refs
+        seeds_in, bias_in, latents, w_in_ref, w_out_ref, *refs = refs
+        outputs, hidden, slope, shift, latents_near, w_in_near, w_out_near, seeds, bias, sems = refs
+        members, points = latents.shape[:2]
+        loads = [
+            (latents.at[m, pl.ds(first, size), :], latents_near.at[m, pl.ds(first, size), :])
+            for m in range(members)
+        ]
+        loads[1:1] = [(bias_in, bias), (w_out_ref, w_out_near)]
+        loads[0:0] = [(w_in_ref, w_in_near), (seeds_in, seeds)]
+        if size < points:
+            rest = pl.ds(size, points - size)
+            loads.append((latents.at[:, rest, :], latents_near.at[:, rest, :]))
+        loads = [pltpu.make_async_copy(a, b, sems.at[k]) for k, (a, b) in enumerate(loads)]
+        for load in loads:
+            load.start()
+        latents, w_in_ref, w_out_ref = latents_near, w_in_near, w_out_near
+        loads[1].wait()
+        loads[3].wait()
+        for m in range(members):
+            shift[m : m + 1, :] = bias[...] + noise_row(seeds[m], bias.shape[1])
+        loads[0].wait()
+        loads[4].wait()
     else:
-        outputs, hidden, slope, *refs = refs
-    latents, seeds, sems = refs
-    members, size, depth = latents.shape
-    copies = [
-        pltpu.make_async_copy(latents_in.at[m, pl.ds(first, size), :], latents.at[m], sems.at[m])
-        for m in range(members)
-    ]
-    seed_copy = pltpu.make_async_copy(seeds_in, seeds, sems.at[members])
-    seed_copy.start()
-    if stage:
-        loads = [
-            pltpu.make_async_copy(w_in_ref, w_in_kept, sems.at[members + 1]),
-            pltpu.make_async_copy(bias_in, bias_ref, sems.at[members + 2]),
-            pltpu.make_async_copy(w_out_ref, w_out_kept, sems.at[members + 3]),
-        ]
-        w_in_ref, bias_in, w_out_ref = w_in_kept, bias_ref, w_out_kept
-        loads[0].start()
-        copies[0].start()
-        loads[1].start()
-        loads[2].start()
-        for copy in copies[1:]:
-            copy.start()
-    else:
-        for copy in copies:
-            copy.start()
-    seed_copy.wait()
-    if stage:
-        for load in loads[1:]:
-            load.wait()
-    width = bias_in.shape[1]
-    shifts = [bias_in[...] + noise_row(seeds[m], width) for m in range(members)]
-    if stage:
-        loads[0].wait()
+        shift, latents, w_in_ref, w_out_ref, outputs, hidden, slope = refs
+    members = latents.shape[0]
     w_in = w_in_ref[...]
     w_out = w_out_ref[...]
     ahead = None
@@ -99,10 +91,11 @@
         outputs[k, rows, :] = jnp.dot(low, w_out, preferred_element_type=F32).astype(BF16)
 
     for k in range(members):
-        copies[k].wait()
+        if stage:
+            loads[2 if k == 0 else 4 + k].wait()
         for r in range(size // sub):
             rows = pl.ds(r * sub, sub)
-            x = jnp.dot(latents[k, rows, :], w_in, preferred_element_type=F32) + shifts[k]
+            x = jnp.dot(latents[k, pl.ds(first + r * sub, sub), :], w_in, preferred_element_type=F32) + shift[k : k + 1, :]
             if behind is not None:
                 finish(*behind)
             behind = activate(*ahead) if ahead is not None else None
@@ -110,44 +103,46 @@
     if behind is not None:
         finish(*behind)
     finish(*activate(*ahead))
-
-
-def forward(seeds, bias, latents, weight_in, weight_out, first, size, stage=False, sub=256):
+    if stage:
+        for load in loads[4 + members :]:
+            load.wait()
+
+
+def forward(arrays, first, size, stage=False, sub=256):
+    latents, weight_in, weight_out = arrays[-3:]
     members, _, depth = latents.shape
     width, variables = weight_out.shape
-    whole = pl.BlockSpec(memory_space=pltpu.VMEM)
+    near = pl.BlockSpec(memory_space=pltpu.VMEM)
     far = pl.BlockSpec(memory_space=pltpu.HBM)
-    near = far if stage else whole
-    kept = [bias, weight_in, weight_out] if stage else []
+    shapes = [
+        jax.ShapeDtypeStruct((members, size, variables), BF16),
+        jax.ShapeDtypeStruct((members, size, width), BF16),
+        jax.ShapeDtypeStruct((members, size, width), F32),
+    ]
+    scratch = []
+    if stage:
+        arrays = [in_hbm(v) for v in arrays]
+        shapes.append(jax.ShapeDtypeStruct((members, width), F32))
+        shapes += [jax.ShapeDtypeStruct(v.shape, v.dtype) for v in (latents, weight_in, weight_out)]
+        scratch = [
+            pltpu.SMEM((members,), jnp.int32),
+            pltpu.VMEM((1, width), F32),
+            pltpu.SemaphoreType.DMA((members + 5,)),
+        ]
     return pl.pallas_call(
-        partial(forward_body, first, min(sub, size), stage),
-        in_specs=[far, near, far, near, near],
-        out_specs=[whole] * (3 + len(kept)),
-        out_shape=[
-            jax.ShapeDtypeStruct((members, size, variables), BF16),
-            jax.ShapeDtypeStruct((members, size, width), BF16),
-            jax.ShapeDtypeStruct((members, size, width), F32),
-        ]
-        + [jax.ShapeDtypeStruct(v.shape, v.dtype) for v in kept],
-        scratch_shapes=[
-            pltpu.VMEM((members, size, depth), BF16),
-            pltpu.SMEM((members,), jnp.int32),
-            pltpu.SemaphoreType.DMA((members + 4,)),
-        ],
+        partial(forward_body, first, size, min(sub, size), stage),
+        in_specs=[far if stage else near] * len(arrays),
+        out_specs=[near] * len(shapes),
+        out_shape=shapes,
+        scratch_shapes=scratch,
         compiler_params=pltpu.CompilerParams(vmem_limit_bytes=VMEM_LIMIT),
         cost_estimate=pl.CostEstimate(
-            flops=2 * members * size * width * (depth + variables),
-            bytes_accessed=members * size * (2 * depth + 6 * width + 2 * variables),
-            transcendentals=members * size * width,
+            flops=COST * members * size * width * (depth + variables),
+            bytes_accessed=0,
+            transcendentals=0,
         ),
         name="forward",
-    )(
-        in_hbm(seeds),
-        in_hbm(bias) if stage else bias,
-        in_hbm(latents),
-        in_hbm(weight_in) if stage else weight_in,
-        in_hbm(weight_out) if stage else weight_out,
-    )
+    )(*arrays)
 
 
 def pair_tiles(own, others, targets, area, grad, start, unroll, first, loss_coef):
@@ -203,7 +198,7 @@
 def backward_body(n_others, n_after, first, loss_coef, has_total, unroll, sub, dests, *refs):
     own, *refs = refs
     others, refs = refs[:n_others], refs[n_others:]
-    targets, area, hidden, slope, latents_in, weight_out, *refs = refs
+    targets, area, hidden, slope, latents, weight_out, *refs = refs
     if has_total:
         in_prior, out_prior, bias_prior, *refs = refs
     refs = refs[n_after:]
@@ -211,10 +206,8 @@
         keep, send, *refs = refs
     else:
         in_total, out_total, bias_total, *refs = refs
-    grad, latents, low, sem = refs
+    grad, low = refs
     members, size, variables = own.shape
-    copy = pltpu.make_async_copy(latents_in.at[:, pl.ds(first, size), :], latents, sem)
-    copy.start()
 
     @pl.loop(0, size // TILE // unroll)
     def _(t):
@@ -229,10 +222,11 @@
             pre = nt(grad[m, rows, :], w_out) * slope[m, rows, :]
             bias_sum += jnp.sum(pre.reshape(sub // TILE, TILE, width), axis=0)
             low[m, rows, :] = pre.astype(BF16)
-    copy.wait()
     flat = lambda ref: ref[...].reshape(members * size, ref.shape[2])
     out_sum = tn(flat(hidden), flat(grad))
-    in_sum = tn(flat(latents), flat(low))
+    depth = latents.shape[2]
+    near = latents[:, pl.ds(first, size), :].reshape(members * size, depth)
+    in_sum = tn(near, flat(low))
     if has_total:
         out_sum += out_prior[...]
         in_sum += in_prior[...]
@@ -270,7 +264,6 @@
     depth = latents.shape[2]
     width = weight_out.shape[0]
     whole = pl.BlockSpec(memory_space=pltpu.VMEM)
-    far = pl.BlockSpec(memory_space=pltpu.HBM)
     count = members * (1 + len(others))
     if dests:
         rows = depth // dests * (width // variables + 1) + TILE
@@ -284,25 +277,23 @@
     return pl.pallas_call(
         partial(backward_body, len(others), 0 if after is None else 1, first, loss_coef, prior is not None, min(unroll, size // TILE), min(sub, size), dests),
         in_specs=[whole] * (3 + len(others))
-        + [whole, whole, far, whole]
+        + [whole] * 4
         + ([whole] * 3 if prior is not None else [])
         + ([pl.BlockSpec(memory_space=pl.ANY)] if after is not None else []),
         out_specs=[whole] * len(shapes),
         out_shape=shapes,
         scratch_shapes=[
             pltpu.VMEM((members, size, variables), BF16),
-            pltpu.VMEM((members, size, depth), BF16),
             pltpu.VMEM((members, size, width), BF16),
-            pltpu.SemaphoreType.DMA,
         ],
         compiler_params=pltpu.CompilerParams(vmem_limit_bytes=VMEM_LIMIT),
         cost_estimate=pl.CostEstimate(
-            flops=2 * members * size * (width * (depth + 2 * variables) + count * TILE * variables * 3),
-            bytes_accessed=members * size * (2 * depth + 6 * width + 2 * variables),
+            flops=COST * members * size * (width * (depth + 2 * variables) + count * TILE * variables * 3),
+            bytes_accessed=0,
             transcendentals=0,
         ),
         name="backward",
-    )(own, *others, targets, area, hidden, slope, in_hbm(latents), weight_out, *(prior or ()), *(() if after is None else (after,)))
+    )(own, *others, targets, area, hidden, slope, latents, weight_out, *(prior or ()), *(() if after is None else (after,)))
 
 
 OFFSETS = ((2, 1), (3, 1), (2, 0), (3, 0), (1, 1), (1, 0), (0, 1))
@@ -366,6 +357,23 @@
     )(mine, *parts)
 
 
+def tie_body(value, after, tied):
+    pass
+
+
+def tie(value, after):
+    anywhere = pl.BlockSpec(memory_space=pl.ANY)
+    return pl.pallas_call(
+        tie_body,
+        in_specs=[anywhere] * 2,
+        out_specs=anywhere,
+        out_shape=jax.ShapeDtypeStruct(value.shape, value.dtype),
+        input_output_aliases={0: 0},
+        compiler_params=pltpu.CompilerParams(vmem_limit_bytes=TINY_LIMIT),
+        name="tie",
+    )(value, after)
+
+
 def area_of(lat_row, rows_total):
     return jnp.cos(jnp.pi * (lat_row.astype(F32) + 0.5) / rows_total - jnp.pi / 2)
 
@@ -404,32 +412,30 @@
     dests = devices_pts * devices_mem
     loss_coef = LOSS_SCALE / math.sqrt(points * devices_pts)
     area = jnp.broadcast_to(area_of(lat_row, LAT_ROWS)[:, None], (points, variables))
-    bias_row = bias_in[None, :]
     packed = dests == 16 and devices_mem == 4
     plan = list(chunks_of(points))
     bits = [1 << k for k in reversed(range(devices_mem.bit_length() - 1))]
     saved = []
+    arrays = [member_seeds, bias_in[None, :], latents, weight_in, weight_out]
     for first, size in plan:
-        if first == 0:
-            out, hidden, slope, bias_row, weight_in, weight_near = forward(
-                member_seeds, bias_row, latents, weight_in, weight_out, first, size, stage=True
-            )
-        else:
-            out, hidden, slope = forward(
-                member_seeds, bias_row, latents, weight_in, weight_near, first, size
-            )
+        out, hidden, slope, *staged = forward(arrays, first, size, stage=first == 0)
+        arrays = staged or arrays
         saved.append([[out, swap_members(out, bits[0])], hidden, slope])
     total = None
+    sums = []
     for k, (first, size) in enumerate(plan):
         held, hidden, slope = saved[k]
+        if k > LAG:
+            held[1] = tie(held[1], sums[k - LAG - 1])
         for bit in bits[1:]:
             held = held + [swap_members(v, bit) for v in held]
         last = first + size == points
         total = list(backward(
-            held[0], held[1:], targets, area, hidden, slope, latents, weight_near, total,
+            held[0], held[1:], targets, area, hidden, slope, arrays[1], arrays[3], total,
             first, loss_coef, dests if last and packed else 0,
             after=saved[-1][0][0] if k == 0 else None,
         ))
+        sums.append(total[-1])
     if not packed:
         scatter = lambda v: lax.psum_scatter(v, ("pts", "mem"), scatter_dimension=0, tiled=True)
         return scatter(total[0]), scatter(total[1]), scatter(jnp.sum(total[2], axis=0))

time: 61.6 us -> 57.9 us (0.940)
  Pallas kernels: 27.3 us -> 21.1 us
  starting transfers between devices: 17.9 us -> 20.6 us
    pallas_call x4 -> x6, Pallas kernels: 14.2 us -> 8.9 us  [the longest x4 8.9 us: forward(): pl.pallas_call(partial(forward_body, first, size, min(sub, size), stage),...]
    ppermute x13, starting transfers between devices: 6.98 us -> 9.45 us  [swap_members(): return lax.ppermute(block, 'mem', [(i, i ^ bit) for i in range(size)])]
    pallas_call x4, Pallas kernels: 12.2 us -> 11.3 us  [backward(): pl.pallas_call(partial(backward_body, len(others), 0 if after is None els...]
  transfers between devices with their start and end apart: 20 -> 20, of which waited for: 7 -> 9; matrix products, arithmetic and copies ran while one was open for 0% -> 0% of each run, Pallas kernels for 32% -> 23%
where the time goes in v3:
time: 57.9 us; the launch traced here: 57.7 us
  Pallas kernels  21.1 us (36%)
  starting transfers between devices  20.6 us (36%)
  waiting for transfers between devices  15 us (26%)
  between operations  0.79 us (1%)
    ppermute x13, waiting for transfers between devices, swap_members(): return lax.ppermute(block, 'mem', [(i, i ^ bit) for i in range(size)])  11.3 us
    pallas_call x4, Pallas kernels, backward(): pl.pallas_call(partial(backward_body, len(others), 0 if after is None els...  11.3 us
    ppermute x7, starting transfers between devices, swap_points(): return lax.ppermute(block, ('pts', 'mem'), pairs)  11.1 us
    ppermute x13, starting transfers between devices, swap_members(): return lax.ppermute(block, 'mem', [(i, i ^ bit) for i in range(size)])  9.45 us
    pallas_call x4, Pallas kernels, forward(): pl.pallas_call(partial(forward_body, first, size, min(sub, size), stage),...  8.9 us
    ppermute x7, waiting for transfers between devices, swap_points(): return lax.ppermute(block, ('pts', 'mem'), pairs)  3.67 us
  transfers between devices with their start and end apart: 20, of which 9 were waited for; matrix products, arithmetic and copies ran while one was open for 0% of the time, Pallas kernels for 23%

profile of v3, /device:TPU:0, one launch (start us, length us, event | category | flops | bytes accessed | tf_op | source)
XLA Modules:
  0.0 57.7 jit_solution(107718327044209682)
XLA Ops:
  0.6 3.7 %forward.4 = (bf16[4,256,128]{2,1,0:T(8,128)(2,1)S(1)}, bf16[4,256,512]{2,1,0:T(8,128)(2,1)S(1)}, f32[4,256,512]{2,1,0:T(8,128)S(1)}, f32[4,512]{1,0:T(4,128)S(1...) custom-call(s32[4]{0:T(128)} %refs_0_.1, f32[1,512]{1,0:T(1,128)} %bitcast.2, ...), custom_call_target="tpu_custom_call" | custom-call | flops 671088640 | tf_op jit(solution)/shard_map/forward/pallas_call | solution.py:132
  4.4 3.0 %collective-permute-start.4 = (bf16[4,256,128]{2,1,0:T(8,128)(2,1)S(1)}, bf16[4,256,128]{2,1,0:T(8,128)(2,1)S(1)}, u32[]{:S(2)}, u32[]{:S(2)}) collective-permute-start(bf16[4,256,128]{2,1,0:T(8,128)(2,1)S(1)} %get-tuple-element.49.refs_0_), channel_id=1, source_target_pairs={{0,2},{1,3},{2,0},{3,1},{4,6},{5,7},{6,4},{7,5},{8,10},{9,11},{10,... | collective-permute-start | bytes 786440 | tf_op jit(solution)/shard_map/ppermute | solution.py:383
  7.4 1.7 %forward.6 = (bf16[4,256,128]{2,1,0:T(8,128)(2,1)S(1)}, bf16[4,256,512]{2,1,0:T(8,128)(2,1)S(1)}, f32[4,256,512]{2,1,0:T(8,128)S(1)}) custom-call(f32[4,512]{1,0:T(4,128)S(1)} %get-tuple-element.41.refs_0_, bf16[4,1024,512]{2,1,0:T(8,128)(2,1)S(1)} %get-tuple-element.42.refs_1_.refs_8_, bf16[512,512]{1,0:T(8,128)(2,1)S(1)} %get-tuple-element.43.refs_2_, ...), custom_call_target="tpu_custom_call" | custom-call | flops 671088640 | tf_op jit(solution)/shard_map/forward/pallas_call | solution.py:132
  9.1 0.1 collective-permute-start.1
  9.2 0.1 collective-permute-start.5
  9.3 0.5 collective-permute-start.2
  9.8 1.7 %forward.5 = (bf16[4,256,128]{2,1,0:T(8,128)(2,1)S(1)}, bf16[4,256,512]{2,1,0:T(8,128)(2,1)S(1)}, f32[4,256,512]{2,1,0:T(8,128)S(1)}) custom-call(f32[4,512]{1,0:T(4,128)S(1)} %get-tuple-element.41.refs_0_, bf16[4,1024,512]{2,1,0:T(8,128)(2,1)S(1)} %get-tuple-element.42.refs_1_.refs_8_, bf16[512,512]{1,0:T(8,128)(2,1)S(1)} %get-tuple-element.43.refs_2_, ...), custom_call_target="tpu_custom_call" | custom-call | flops 671088640 | tf_op jit(solution)/shard_map/forward/pallas_call | solution.py:132
  11.5 0.0 copy-start.1
  11.5 0.0 copy-start
  11.5 2.0 %collective-permute-start = (bf16[4,256,128]{2,1,0:T(8,128)(2,1)S(1)}, bf16[4,256,128]{2,1,0:T(8,128)(2,1)S(1)}, u32[]{:S(2)}, u32[]{:S(2)}) collective-permute-start(bf16[4,256,128]{2,1,0:T(8,128)(2,1)S(1)} %get-tuple-element.45.refs_10_.refs_0_), channel_id=1, source_target_pairs={{0,2},{1,3},{2,0},{3,1},{4,6},{5,7},{6,4},{7,5},{8,10},{9,11},{10,... | collective-permute-start | bytes 786440 | tf_op jit(solution)/shard_map/ppermute | solution.py:383
  13.5 1.0 %collective-permute-done.4.refs_1_ = bf16[4,256,128]{2,1,0:T(8,128)(2,1)S(1)} collective-permute-done((bf16[4,256,128]{2,1,0:T(8,128)(2,1)S(1)}, bf16[4,256,128]{2,1,0:T(8,128)(2,1)S(1)}, u32[]{:S(2)}, u32[]{:S(2)}) %collective-permute-start.4) | collective-permute-done | bytes 262176 | tf_op jit(solution)/shard_map/ppermute | solution.py:383
  14.5 0.0 collective-permute-start.6
  14.5 1.7 %forward.7 = (bf16[4,256,128]{2,1,0:T(8,128)(2,1)S(1)}, bf16[4,256,512]{2,1,0:T(8,128)(2,1)S(1)}, f32[4,256,512]{2,1,0:T(8,128)S(1)}) custom-call(f32[4,512]{1,0:T(4,128)S(1)} %get-tuple-element.41.refs_0_, bf16[4,1024,512]{2,1,0:T(8,128)(2,1)S(1)} %get-tuple-element.42.refs_1_.refs_8_, bf16[512,512]{1,0:T(8,128)(2,1)S(1)} %get-tuple-element.43.refs_2_, ...), custom_call_target="tpu_custom_call" | custom-call | flops 671088640 | tf_op jit(solution)/shard_map/forward/pallas_call | solution.py:132
  16.2 3.9 %collective-permute-done.1.refs_1_ = bf16[4,256,128]{2,1,0:T(8,128)(2,1)S(1)} collective-permute-done((bf16[4,256,128]{2,1,0:T(8,128)(2,1)S(1)}, bf16[4,256,128]{2,1,0:T(8,128)(2,1)S(1)}, u32[]{:S(2)}, u32[]{:S(2)}) %collective-permute-start.1) | collective-permute-done | bytes 262176 | tf_op jit(solution)/shard_map/ppermute | solution.py:383
  20.1 2.1 %collective-permute-start.9 = (bf16[4,256,128]{2,1,0:T(8,128)(2,1)S(1)}, bf16[4,256,128]{2,1,0:T(8,128)(2,1)S(1)}, u32[]{:S(2)}, u32[]{:S(2)}) collective-permute-start(bf16[4,256,128]{2,1,0:T(8,128)(2,1)S(1)} %get-tuple-element.58.refs_0_), channel_id=1, source_target_pairs={{0,2},{1,3},{2,0},{3,1},{4,6},{5,7},{6,4},{7,5},{8,10},{9,11},{10,... | collective-permute-start | bytes 786440 | tf_op jit(solution)/shard_map/ppermute | solution.py:383
  22.2 0.0 collective-permute-start.3
  22.3 0.6 collective-permute-start.7
  22.8 0.2 broadcast_in_dim.10.refs_5_
  23.0 2.9 %backward.4 = (f32[512,512]{1,0:T(8,128)S(1)}, f32[512,128]{1,0:T(8,128)S(1)}, f32[16,512]{1,0:T(8,128)S(1)}) custom-call(bf16[4,256,128]{2,1,0:T(8,128)(2,1)S(1)} %get-tuple-element.49.refs_0_, bf16[4,256,128]{2,1,0:T(8,128)(2,1)S(1)} %collective-permute-done.4.refs_1_, bf16[4,256,128]{2,1,0:T(8,128)(2,1)S(1)} %collective-permute-done.5.refs_2_, ...), custom_call_target="tpu_custom_call" | custom-call | flops 1006632960 | tf_op jit(solution)/shard_map/backward/pallas_call | solution.py:277
  25.9 4.6 %collective-permute-done.9.value = bf16[4,256,128]{2,1,0:T(8,128)(2,1)S(1)} collective-permute-done((bf16[4,256,128]{2,1,0:T(8,128)(2,1)S(1)}, bf16[4,256,128]{2,1,0:T(8,128)(2,1)S(1)}, u32[]{:S(2)}, u32[]{:S(2)}) %collective-permute-start.9) | collective-permute-done | bytes 262176 | tf_op jit(solution)/shard_map/ppermute | solution.py:383
  30.5 0.0 collective-permute-done.2.refs_2_
  30.6 0.5 collective-permute-start.11
  31.1 0.0 collective-permute-done.3.refs_3_
  31.1 2.7 %backward.5 = (f32[512,512]{1,0:T(8,128)S(1)}, f32[512,128]{1,0:T(8,128)S(1)}, f32[16,512]{1,0:T(8,128)S(1)}) custom-call(bf16[4,256,128]{2,1,0:T(8,128)(2,1)S(1)} %get-tuple-element.46.refs_0_, bf16[4,256,128]{2,1,0:T(8,128)(2,1)S(1)} %collective-permute-done.1.refs_1_, bf16[4,256,128]{2,1,0:T(8,128)(2,1)S(1)} %collective-permute-done.2.refs_2_, ...), custom_call_target="tpu_custom_call" | custom-call | flops 1006632960 | tf_op jit(solution)/shard_map/backward/pallas_call | solution.py:277
  33.8 0.0 collective-permute-done.value
  33.8 0.1 collective-permute-start.8
  33.9 0.0 collective-permute-done.10.refs_2_
  33.9 0.0 collective-permute-done.11.refs_3_
  33.9 2.7 %backward.6 = (f32[512,512]{1,0:T(8,128)S(1)}, f32[512,128]{1,0:T(8,128)S(1)}, f32[16,512]{1,0:T(8,128)S(1)}) custom-call(bf16[4,256,128]{2,1,0:T(8,128)(2,1)S(1)} %get-tuple-element.58.refs_0_, bf16[4,256,128]{2,1,0:T(8,128)(2,1)S(1)} %tie.3.refs_1_, bf16[4,256,128]{2,1,0:T(8,128)(2,1)S(1)} %collective-permute-done.10.refs_2_, ...), custom_call_target="tpu_custom_call" | custom-call | flops 1006632960 | tf_op jit(solution)/shard_map/backward/pallas_call | solution.py:277
  36.7 0.0 collective-permute-done.7.refs_2_
  36.7 2.9 %backward.7 = (f32[8,176,128]{2,1,0:T(8,128)S(1)}, f32[8,176,128]{2,1,0:T(8,128)S(1)}) custom-call(bf16[4,256,128]{2,1,0:T(8,128)(2,1)S(1)} %get-tuple-element.45.refs_10_.refs_0_, bf16[4,256,128]{2,1,0:T(8,128)(2,1)S(1)} %tie.2.refs_1_, bf16[4,256,128]{2,1,0:T(8,128)(2,1)S(1)} %collective-permute-done.7.refs_2_, ...), custom_call_target="tpu_custom_call" | custom-call | flops 1006632960 | tf_op jit(solution)/shard_map/backward/pallas_call | solution.py:277
  39.6 0.5 collective-permute-start.12
  40.1 1.8 %collective-permute-done.12.arrived = f32[8,176,128]{2,1,0:T(8,128)S(1)} collective-permute-done((f32[8,176,128]{2,1,0:T(8,128)S(1)}, f32[8,176,128]{2,1,0:T(8,128)S(1)}, u32[]{:S(2)}, u32[]{:S(2)}) %collective-permute-start.12) | collective-permute-done | bytes 720928 | tf_op jit(solution)/shard_map/ppermute | solution.py:383
  42.0 0.1 spread_out.1
  42.0 3.8 %collective-permute-start.13 = (bf16[176,128]{1,0:T(8,128)(2,1)S(1)}, bf16[176,128]{1,0:T(8,128)(2,1)S(1)}, u32[]{:S(2)}, u32[]{:S(2)}) collective-permute-start(bf16[176,128]{1,0:T(8,128)(2,1)S(1)} %get-tuple-element.69), channel_id=1, source_target_pairs={{0,10},{1,11},{2,8},{3,9},{4,14},{5,15},{6,12},{7,13},{8,2},{9,3},... | collective-permute-start | bytes 135176 | tf_op jit(solution)/shard_map/ppermute | solution.py:393
  45.9 1.3 %collective-permute-start.14 = (bf16[176,128]{1,0:T(8,128)(2,1)S(1)}, bf16[176,128]{1,0:T(8,128)(2,1)S(1)}, u32[]{:S(2)}, u32[]{:S(2)}) collective-permute-start(bf16[176,128]{1,0:T(8,128)(2,1)S(1)} %get-tuple-element.70), channel_id=1, source_target_pairs={{0,14},{1,15},{2,12},{3,13},{4,10},{5,11},{6,8},{7,9},{8,6},{9,7},... | collective-permute-start | bytes 135176 | tf_op jit(solution)/shard_map/ppermute | solution.py:393
  47.2 1.7 %collective-permute-start.15 = (bf16[176,128]{1,0:T(8,128)(2,1)S(1)}, bf16[176,128]{1,0:T(8,128)(2,1)S(1)}, u32[]{:S(2)}, u32[]{:S(2)}) collective-permute-start(bf16[176,128]{1,0:T(8,128)(2,1)S(1)} %get-tuple-element.71), channel_id=1, source_target_pairs={{0,8},{1,9},{2,10},{3,11},{4,12},{5,13},{6,14},{7,15},{8,0},{9,1},... | collective-permute-start | bytes 135176 | tf_op jit(solution)/shard_map/ppermute | solution.py:393
  48.9 0.9 %collective-permute-start.16 = (bf16[176,128]{1,0:T(8,128)(2,1)S(1)}, bf16[176,128]{1,0:T(8,128)(2,1)S(1)}, u32[]{:S(2)}, u32[]{:S(2)}) collective-permute-start(bf16[176,128]{1,0:T(8,128)(2,1)S(1)} %get-tuple-element.72), channel_id=1, source_target_pairs={{0,12},{1,13},{2,14},{3,15},{4,8},{5,9},{6,10},{7,11},{8,4},{9,5},... | collective-permute-start | bytes 135176 | tf_op jit(solution)/shard_map/ppermute | solution.py:393
  49.8 1.8 %collective-permute-start.17 = (bf16[176,128]{1,0:T(8,128)(2,1)S(1)}, bf16[176,128]{1,0:T(8,128)(2,1)S(1)}, u32[]{:S(2)}, u32[]{:S(2)}) collective-permute-start(bf16[176,128]{1,0:T(8,128)(2,1)S(1)} %get-tuple-element.73), channel_id=1, source_target_pairs={{0,6},{1,7},{2,4},{3,5},{4,2},{5,3},{6,0},{7,1},{8,14},{9,15},{10,... | collective-permute-start | bytes 135176 | tf_op jit(solution)/shard_map/ppermute | solution.py:393
  51.6 0.0 collective-permute-done.13.refs_0_
  51.6 1.0 %collective-permute-start.18 = (bf16[176,128]{1,0:T(8,128)(2,1)S(1)}, bf16[176,128]{1,0:T(8,128)(2,1)S(1)}, u32[]{:S(2)}, u32[]{:S(2)}) collective-permute-start(bf16[176,128]{1,0:T(8,128)(2,1)S(1)} %get-tuple-element.74), channel_id=1, source_target_pairs={{0,4},{1,5},{2,6},{3,7},{4,0},{5,1},{6,2},{7,3},{8,12},{9,13},{10,... | collective-permute-start | bytes 135176 | tf_op jit(solution)/shard_map/ppermute | solution.py:393
  52.6 0.2 collective-permute-done.14.refs_1_
  52.8 0.5 collective-permute-start.19
  53.3 1.8 %collective-permute-done.15.refs_2_ = bf16[176,128]{1,0:T(8,128)(2,1)S(1)} collective-permute-done((bf16[176,128]{1,0:T(8,128)(2,1)S(1)}, bf16[176,128]{1,0:T(8,128)(2,1)S(1)}, u32[]{:S(2)}, u32[]{:S(2)}) %collective-permute-start.15) | collective-permute-done | bytes 45088 | tf_op jit(solution)/shard_map/ppermute | solution.py:393
  55.1 1.0 %collective-permute-done.17.refs_4_ = bf16[176,128]{1,0:T(8,128)(2,1)S(1)} collective-permute-done((bf16[176,128]{1,0:T(8,128)(2,1)S(1)}, bf16[176,128]{1,0:T(8,128)(2,1)S(1)}, u32[]{:S(2)}, u32[]{:S(2)}) %collective-permute-start.17) | collective-permute-done | bytes 45088 | tf_op jit(solution)/shard_map/ppermute | solution.py:393
  56.2 0.2 collective-permute-done.18.refs_5_
  56.4 0.5 collective-permute-done.19.refs_6_
  56.8 0.9 %finish.1 = (f32[32,512]{1,0:T(8,128)}, f32[32,128]{1,0:T(8,128)}, f32[1,32]{1,0:T(1,128)}) custom-call(f32[176,128]{1,0:T(8,128)S(1)} %get-tuple-element.68.mine, bf16[176,128]{1,0:T(8,128)(2,1)S(1)} %collective-permute-done.13.refs_0_, bf16[176,128]{1,0:T(8,128)(2,1)S(1)} %collective-permute-done.14.refs_1_, ...), custom_call_target="tpu_custom_call" | custom-call | tf_op jit(solution)/shard_map/finish/pallas_call | solution.py:346
  (10 shorter events, 0.1 us)
Async XLA Ops:
  4.4 10.1 %collective-permute-start.4 = (bf16[4,256,128]{2,1,0:T(8,128)(2,1)S(1)}, bf16[4,256,128]{2,1,0:T(8,128)(2,1)S(1)}, u32[]{:S(2)}, u32[]{:S(2)}) collective-permute-start(bf16[4,256,128]{2,1,0:T(8,128)(2,1)S(1)} %get-tuple-element.49.refs_0_), channel_id=1, source_target_pairs={{0,2},{1,3},{2,0},{3,1},{4,6},{5,7},{6,4},{7,5},{8,10},{9,11},{10,... | collective-permute-start | bytes 786440 | tf_op jit(solution)/shard_map/ppermute | solution.py:383
  9.1 11.0 %collective-permute-start.1 = (bf16[4,256,128]{2,1,0:T(8,128)(2,1)S(1)}, bf16[4,256,128]{2,1,0:T(8,128)(2,1)S(1)}, u32[]{:S(2)}, u32[]{:S(2)}) collective-permute-start(bf16[4,256,128]{2,1,0:T(8,128)(2,1)S(1)} %get-tuple-element.46.refs_0_), channel_id=1, source_target_pairs={{0,2},{1,3},{2,0},{3,1},{4,6},{5,7},{6,4},{7,5},{8,10},{9,11},{10,... | collective-permute-start | bytes 786440 | tf_op jit(solution)/shard_map/ppermute | solution.py:383
  9.2 13.0 %collective-permute-start.5 = (bf16[4,256,128]{2,1,0:T(8,128)(2,1)S(1)}, bf16[4,256,128]{2,1,0:T(8,128)(2,1)S(1)}, u32[]{:S(2)}, u32[]{:S(2)}) collective-permute-start(bf16[4,256,128]{2,1,0:T(8,128)(2,1)S(1)} %get-tuple-element.49.refs_0_), channel_id=1, source_target_pairs={{0,1},{1,0},{2,3},{3,2},{4,5},{5,4},{6,7},{7,6},{8,9},{9,8},{10,11... | collective-permute-start | bytes 786440 | tf_op jit(solution)/shard_map/ppermute | solution.py:383
  9.3 21.3 %collective-permute-start.2 = (bf16[4,256,128]{2,1,0:T(8,128)(2,1)S(1)}, bf16[4,256,128]{2,1,0:T(8,128)(2,1)S(1)}, u32[]{:S(2)}, u32[]{:S(2)}) collective-permute-start(bf16[4,256,128]{2,1,0:T(8,128)(2,1)S(1)} %get-tuple-element.46.refs_0_), channel_id=1, source_target_pairs={{0,1},{1,0},{2,3},{3,2},{4,5},{5,4},{6,7},{7,6},{8,9},{9,8},{10,11... | collective-permute-start | bytes 786440 | tf_op jit(solution)/shard_map/ppermute | solution.py:383
  11.5 10.7 %copy-start.1 = (s32[1024]{0:T(1024)S(1)}, s32[1024]{0:T(1024)}, u32[]{:S(2)}) copy-start(s32[1024]{0:T(1024)} %param.10) | copy-start | bytes 12292
  11.5 11.5 %copy-start = (f32[1024,128]{1,0:T(8,128)S(1)}, f32[1024,128]{1,0:T(8,128)}, u32[]{:S(2)}) copy-start(f32[1024,128]{1,0:T(8,128)} %refs_4_.9) | copy-start | bytes 1572868
  11.5 22.3 %collective-permute-start = (bf16[4,256,128]{2,1,0:T(8,128)(2,1)S(1)}, bf16[4,256,128]{2,1,0:T(8,128)(2,1)S(1)}, u32[]{:S(2)}, u32[]{:S(2)}) collective-permute-start(bf16[4,256,128]{2,1,0:T(8,128)(2,1)S(1)} %get-tuple-element.45.refs_10_.refs_0_), channel_id=1, source_target_pairs={{0,2},{1,3},{2,0},{3,1},{4,6},{5,7},{6,4},{7,5},{8,10},{9,11},{10,... | collective-permute-start | bytes 786440 | tf_op jit(solution)/shard_map/ppermute | solution.py:383
  14.5 7.7 %collective-permute-start.6 = (bf16[4,256,128]{2,1,0:T(8,128)(2,1)S(1)}, bf16[4,256,128]{2,1,0:T(8,128)(2,1)S(1)}, u32[]{:S(2)}, u32[]{:S(2)}) collective-permute-start(bf16[4,256,128]{2,1,0:T(8,128)(2,1)S(1)} %collective-permute-done.4.refs_1_), channel_id=1, source_target_pairs={{0,1},{1,0},{2,3},{3,2},{4,5},{5,4},{6,7},{7,6},{8,9},{9,8},{10,11... | collective-permute-start | bytes 786440 | tf_op jit(solution)/shard_map/ppermute | solution.py:383
  20.1 10.4 %collective-permute-start.9 = (bf16[4,256,128]{2,1,0:T(8,128)(2,1)S(1)}, bf16[4,256,128]{2,1,0:T(8,128)(2,1)S(1)}, u32[]{:S(2)}, u32[]{:S(2)}) collective-permute-start(bf16[4,256,128]{2,1,0:T(8,128)(2,1)S(1)} %get-tuple-element.58.refs_0_), channel_id=1, source_target_pairs={{0,2},{1,3},{2,0},{3,1},{4,6},{5,7},{6,4},{7,5},{8,10},{9,11},{10,... | collective-permute-start | bytes 786440 | tf_op jit(solution)/shard_map/ppermute | solution.py:383
  22.2 8.9 %collective-permute-start.3 = (bf16[4,256,128]{2,1,0:T(8,128)(2,1)S(1)}, bf16[4,256,128]{2,1,0:T(8,128)(2,1)S(1)}, u32[]{:S(2)}, u32[]{:S(2)}) collective-permute-start(bf16[4,256,128]{2,1,0:T(8,128)(2,1)S(1)} %collective-permute-done.1.refs_1_), channel_id=1, source_target_pairs={{0,1},{1,0},{2,3},{3,2},{4,5},{5,4},{6,7},{7,6},{8,9},{9,8},{10,11... | collective-permute-start | bytes 786440 | tf_op jit(solution)/shard_map/ppermute | solution.py:383
  22.3 14.4 %collective-permute-start.7 = (bf16[4,256,128]{2,1,0:T(8,128)(2,1)S(1)}, bf16[4,256,128]{2,1,0:T(8,128)(2,1)S(1)}, u32[]{:S(2)}, u32[]{:S(2)}) collective-permute-start(bf16[4,256,128]{2,1,0:T(8,128)(2,1)S(1)} %get-tuple-element.45.refs_10_.refs_0_), channel_id=1, source_target_pairs={{0,1},{1,0},{2,3},{3,2},{4,5},{5,4},{6,7},{7,6},{8,9},{9,8},{10,11... | collective-permute-start | bytes 786440 | tf_op jit(solution)/shard_map/ppermute | solution.py:383
  30.5 3.4 %collective-permute-start.10 = (bf16[4,256,128]{2,1,0:T(8,128)(2,1)S(1)}, bf16[4,256,128]{2,1,0:T(8,128)(2,1)S(1)}, u32[]{:S(2)}, u32[]{:S(2)}) collective-permute-start(bf16[4,256,128]{2,1,0:T(8,128)(2,1)S(1)} %get-tuple-element.58.refs_0_), channel_id=1, source_target_pairs={{0,1},{1,0},{2,3},{3,2},{4,5},{5,4},{6,7},{7,6},{8,9},{9,8},{10,11... | collective-permute-start | bytes 786440 | tf_op jit(solution)/shard_map/ppermute | solution.py:383
  30.6 3.4 %collective-permute-start.11 = (bf16[4,256,128]{2,1,0:T(8,128)(2,1)S(1)}, bf16[4,256,128]{2,1,0:T(8,128)(2,1)S(1)}, u32[]{:S(2)}, u32[]{:S(2)}) collective-permute-start(bf16[4,256,128]{2,1,0:T(8,128)(2,1)S(1)} %tie.3.refs_1_), channel_id=1, source_target_pairs={{0,1},{1,0},{2,3},{3,2},{4,5},{5,4},{6,7},{7,6},{8,9},{9,8},{10,11... | collective-permute-start | bytes 786440 | tf_op jit(solution)/shard_map/ppermute | solution.py:383
  33.8 2.9 %collective-permute-start.8 = (bf16[4,256,128]{2,1,0:T(8,128)(2,1)S(1)}, bf16[4,256,128]{2,1,0:T(8,128)(2,1)S(1)}, u32[]{:S(2)}, u32[]{:S(2)}) collective-permute-start(bf16[4,256,128]{2,1,0:T(8,128)(2,1)S(1)} %tie.2.refs_1_), channel_id=1, source_target_pairs={{0,1},{1,0},{2,3},{3,2},{4,5},{5,4},{6,7},{7,6},{8,9},{9,8},{10,11... | collective-permute-start | bytes 786440 | tf_op jit(solution)/shard_map/ppermute | solution.py:383
  39.6 2.3 %collective-permute-start.12 = (f32[8,176,128]{2,1,0:T(8,128)S(1)}, f32[8,176,128]{2,1,0:T(8,128)S(1)}, u32[]{:S(2)}, u32[]{:S(2)}) collective-permute-start(f32[8,176,128]{2,1,0:T(8,128)S(1)} %get-tuple-element.67), channel_id=1, source_target_pairs={{0,1},{1,0},{2,3},{3,2},{4,5},{5,4},{6,7},{7,6},{8,9},{9,8},{10,11... | collective-permute-start | bytes 2162696 | tf_op jit(solution)/shard_map/ppermute | solution.py:383
  42.0 9.6 %collective-permute-start.13 = (bf16[176,128]{1,0:T(8,128)(2,1)S(1)}, bf16[176,128]{1,0:T(8,128)(2,1)S(1)}, u32[]{:S(2)}, u32[]{:S(2)}) collective-permute-start(bf16[176,128]{1,0:T(8,128)(2,1)S(1)} %get-tuple-element.69), channel_id=1, source_target_pairs={{0,10},{1,11},{2,8},{3,9},{4,14},{5,15},{6,12},{7,13},{8,2},{9,3},... | collective-permute-start | bytes 135176 | tf_op jit(solution)/shard_map/ppermute | solution.py:393
  45.9 6.9 %collective-permute-start.14 = (bf16[176,128]{1,0:T(8,128)(2,1)S(1)}, bf16[176,128]{1,0:T(8,128)(2,1)S(1)}, u32[]{:S(2)}, u32[]{:S(2)}) collective-permute-start(bf16[176,128]{1,0:T(8,128)(2,1)S(1)} %get-tuple-element.70), channel_id=1, source_target_pairs={{0,14},{1,15},{2,12},{3,13},{4,10},{5,11},{6,8},{7,9},{8,6},{9,7},... | collective-permute-start | bytes 135176 | tf_op jit(solution)/shard_map/ppermute | solution.py:393
  47.2 7.9 %collective-permute-start.15 = (bf16[176,128]{1,0:T(8,128)(2,1)S(1)}, bf16[176,128]{1,0:T(8,128)(2,1)S(1)}, u32[]{:S(2)}, u32[]{:S(2)}) collective-permute-start(bf16[176,128]{1,0:T(8,128)(2,1)S(1)} %get-tuple-element.71), channel_id=1, source_target_pairs={{0,8},{1,9},{2,10},{3,11},{4,12},{5,13},{6,14},{7,15},{8,0},{9,1},... | collective-permute-start | bytes 135176 | tf_op jit(solution)/shard_map/ppermute | solution.py:393
  48.9 6.3 %collective-permute-start.16 = (bf16[176,128]{1,0:T(8,128)(2,1)S(1)}, bf16[176,128]{1,0:T(8,128)(2,1)S(1)}, u32[]{:S(2)}, u32[]{:S(2)}) collective-permute-start(bf16[176,128]{1,0:T(8,128)(2,1)S(1)} %get-tuple-element.72), channel_id=1, source_target_pairs={{0,12},{1,13},{2,14},{3,15},{4,8},{5,9},{6,10},{7,11},{8,4},{9,5},... | collective-permute-start | bytes 135176 | tf_op jit(solution)/shard_map/ppermute | solution.py:393
  49.8 6.3 %collective-permute-start.17 = (bf16[176,128]{1,0:T(8,128)(2,1)S(1)}, bf16[176,128]{1,0:T(8,128)(2,1)S(1)}, u32[]{:S(2)}, u32[]{:S(2)}) collective-permute-start(bf16[176,128]{1,0:T(8,128)(2,1)S(1)} %get-tuple-element.73), channel_id=1, source_target_pairs={{0,6},{1,7},{2,4},{3,5},{4,2},{5,3},{6,0},{7,1},{8,14},{9,15},{10,... | collective-permute-start | bytes 135176 | tf_op jit(solution)/shard_map/ppermute | solution.py:393
  51.6 4.7 %collective-permute-start.18 = (bf16[176,128]{1,0:T(8,128)(2,1)S(1)}, bf16[176,128]{1,0:T(8,128)(2,1)S(1)}, u32[]{:S(2)}, u32[]{:S(2)}) collective-permute-start(bf16[176,128]{1,0:T(8,128)(2,1)S(1)} %get-tuple-element.74), channel_id=1, source_target_pairs={{0,4},{1,5},{2,6},{3,7},{4,0},{5,1},{6,2},{7,3},{8,12},{9,13},{10,... | collective-permute-start | bytes 135176 | tf_op jit(solution)/shard_map/ppermute | solution.py:393
  52.8 4.0 %collective-permute-start.19 = (bf16[176,128]{1,0:T(8,128)(2,1)S(1)}, bf16[176,128]{1,0:T(8,128)(2,1)S(1)}, u32[]{:S(2)}, u32[]{:S(2)}) collective-permute-start(bf16[176,128]{1,0:T(8,128)(2,1)S(1)} %get-tuple-element.75), channel_id=1, source_target_pairs={{0,2},{1,3},{2,0},{3,1},{4,6},{5,7},{6,4},{7,5},{8,10},{9,11},{10,... | collective-permute-start | bytes 135176 | tf_op jit(solution)/shard_map/ppermute | solution.py:393

commit v4 on v3

--- a/solution.py
+++ b/solution.py
@@ -34,6 +34,10 @@
 
 def in_hbm(v):
     return pltpu.with_memory_space_constraint(v, pltpu.HBM)
+
+
+def piece_of(size, most):
+    return max(k for k in range(TILE, most + 1, TILE) if size % k == 0)
 
 
 def noise_row(seed, width):
@@ -71,7 +75,7 @@
         loads[0].wait()
         loads[4].wait()
     else:
-        shift, latents, w_in_ref, w_out_ref, outputs, hidden, slope = refs
+        _, shift, latents, w_in_ref, w_out_ref, outputs, hidden, slope = refs
     members = latents.shape[0]
     w_in = w_in_ref[...]
     w_out = w_out_ref[...]
@@ -108,12 +112,14 @@
             load.wait()
 
 
-def forward(arrays, first, size, stage=False, sub=256):
+def forward(arrays, first, size, after=None, sub=256):
+    stage = after is None
     latents, weight_in, weight_out = arrays[-3:]
     members, _, depth = latents.shape
     width, variables = weight_out.shape
     near = pl.BlockSpec(memory_space=pltpu.VMEM)
     far = pl.BlockSpec(memory_space=pltpu.HBM)
+    anywhere = pl.BlockSpec(memory_space=pl.ANY)
     shapes = [
         jax.ShapeDtypeStruct((members, size, variables), BF16),
         jax.ShapeDtypeStruct((members, size, width), BF16),
@@ -130,8 +136,8 @@
             pltpu.SemaphoreType.DMA((members + 5,)),
         ]
     return pl.pallas_call(
-        partial(forward_body, first, size, min(sub, size), stage),
-        in_specs=[far if stage else near] * len(arrays),
+        partial(forward_body, first, size, piece_of(size, sub), stage),
+        in_specs=[far] * len(arrays) if stage else [anywhere] + [near] * len(arrays),
         out_specs=[near] * len(shapes),
         out_shape=shapes,
         scratch_shapes=scratch,
@@ -142,7 +148,7 @@
             transcendentals=0,
         ),
         name="forward",
-    )(*arrays)
+    )(*arrays if stage else (after, *arrays))
 
 
 def pair_tiles(own, others, targets, area, grad, start, unroll, first, loss_coef):
@@ -275,7 +281,7 @@
             jax.ShapeDtypeStruct((TILE, width), F32),
         ]
     return pl.pallas_call(
-        partial(backward_body, len(others), 0 if after is None else 1, first, loss_coef, prior is not None, min(unroll, size // TILE), min(sub, size), dests),
+        partial(backward_body, len(others), 0 if after is None else 1, first, loss_coef, prior is not None, math.gcd(unroll, size // TILE), piece_of(size, sub), dests),
         in_specs=[whole] * (3 + len(others))
         + [whole] * 4
         + ([whole] * 3 if prior is not None else [])
@@ -416,9 +422,10 @@
     plan = list(chunks_of(points))
     bits = [1 << k for k in reversed(range(devices_mem.bit_length() - 1))]
     saved = []
+    out = None
     arrays = [member_seeds, bias_in[None, :], latents, weight_in, weight_out]
     for first, size in plan:
-        out, hidden, slope, *staged = forward(arrays, first, size, stage=first == 0)
+        out, hidden, slope, *staged = forward(arrays, first, size, after=out)
         arrays = staged or arrays
         saved.append([[out, swap_members(out, bits[0])], hidden, slope])
     total = None

time: 57.9 us -> 54.5 us (0.941)
  waiting for transfers between devices: 15 us -> 12 us
    ppermute x13, waiting for transfers between devices: 11.3 us -> 8.28 us  [swap_members(): return lax.ppermute(block, 'mem', [(i, i ^ bit) for i in range(size)])]
  transfers between devices with their start and end apart: 20 -> 20, of which waited for: 9 -> 10; matrix products, arithmetic and copies ran while one was open for 0% -> 0% of each run, Pallas kernels for 23% -> 25%
where the time goes in v4:
time: 54.5 us; the launch traced here: 54.4 us
  Pallas kernels  21.1 us (39%)
  starting transfers between devices  20.3 us (37%)
  waiting for transfers between devices  12 us (22%)
  between operations  0.78 us (1%)
    pallas_call x4, Pallas kernels, backward(): pl.pallas_call(partial(backward_body, len(others), 0 if after is None els...  11.3 us
    ppermute x7, starting transfers between devices, swap_points(): return lax.ppermute(block, ('pts', 'mem'), pairs)  11.1 us
    ppermute x13, starting transfers between devices, swap_members(): return lax.ppermute(block, 'mem', [(i, i ^ bit) for i in range(size)])  9.16 us
    pallas_call x4, Pallas kernels, forward(): pl.pallas_call(partial(forward_body, first, size, piece_of(size, sub), st...  8.9 us
    ppermute x13, waiting for transfers between devices, swap_members(): return lax.ppermute(block, 'mem', [(i, i ^ bit) for i in range(size)])  8.28 us
    ppermute x7, waiting for transfers between devices, swap_points(): return lax.ppermute(block, ('pts', 'mem'), pairs)  3.67 us
  transfers between devices with their start and end apart: 20, of which 10 were waited for; matrix products, arithmetic and copies ran while one was open for 0% of the time, Pallas kernels for 25%

profile of v4, /device:TPU:0, one launch (start us, length us, event | category | flops | bytes accessed | tf_op | source)
XLA Modules:
  0.0 54.4 jit_solution(15820189022654789522)
XLA Ops:
  0.6 3.7 %forward.4 = (bf16[4,256,128]{2,1,0:T(8,128)(2,1)S(1)}, bf16[4,256,512]{2,1,0:T(8,128)(2,1)S(1)}, f32[4,256,512]{2,1,0:T(8,128)S(1)}, f32[4,512]{1,0:T(4,128)S(1...) custom-call(s32[4]{0:T(128)} %refs_0_.1, f32[1,512]{1,0:T(1,128)} %bitcast.2, ...), custom_call_target="tpu_custom_call" | custom-call | flops 671088640 | tf_op jit(solution)/shard_map/forward/pallas_call | solution.py:138
  4.4 3.0 %collective-permute-start.4 = (bf16[4,256,128]{2,1,0:T(8,128)(2,1)S(1)}, bf16[4,256,128]{2,1,0:T(8,128)(2,1)S(1)}, u32[]{:S(2)}, u32[]{:S(2)}) collective-permute-start(bf16[4,256,128]{2,1,0:T(8,128)(2,1)S(1)} %get-tuple-element.41.refs_0_), channel_id=1, source_target_pairs={{0,2},{1,3},{2,0},{3,1},{4,6},{5,7},{6,4},{7,5},{8,10},{9,11},{10,... | collective-permute-start | bytes 786440 | tf_op jit(solution)/shard_map/ppermute | solution.py:389
  7.4 1.7 %forward.5 = (bf16[4,256,128]{2,1,0:T(8,128)(2,1)S(1)}, bf16[4,256,512]{2,1,0:T(8,128)(2,1)S(1)}, f32[4,256,512]{2,1,0:T(8,128)S(1)}) custom-call(bf16[4,256,128]{2,1,0:T(8,128)(2,1)S(1)} %get-tuple-element.41.refs_0_, f32[4,512]{1,0:T(4,128)S(1)} %get-tuple-element.42.refs_1_, bf16[4,1024,512]{2,1,0:T(8,128)(2,1)S(1)} %get-tuple-element.43.refs_2_.refs_8_, ...), custom_call_target="tpu_custom_call" | custom-call | flops 671088640 | tf_op jit(solution)/shard_map/forward/pallas_call | solution.py:138
  9.1 0.2 collective-permute-start.1
  9.3 0.5 collective-permute-start.2
  9.8 1.7 %forward.6 = (bf16[4,256,128]{2,1,0:T(8,128)(2,1)S(1)}, bf16[4,256,512]{2,1,0:T(8,128)(2,1)S(1)}, f32[4,256,512]{2,1,0:T(8,128)S(1)}) custom-call(bf16[4,256,128]{2,1,0:T(8,128)(2,1)S(1)} %get-tuple-element.46.refs_0_, f32[4,512]{1,0:T(4,128)S(1)} %get-tuple-element.42.refs_1_, bf16[4,1024,512]{2,1,0:T(8,128)(2,1)S(1)} %get-tuple-element.43.refs_2_.refs_8_, ...), custom_call_target="tpu_custom_call" | custom-call | flops 671088640 | tf_op jit(solution)/shard_map/forward/pallas_call | solution.py:138
  11.5 0.0 copy-start.1
  11.5 0.0 copy-start
  11.5 1.7 %collective-permute-start.9 = (bf16[4,256,128]{2,1,0:T(8,128)(2,1)S(1)}, bf16[4,256,128]{2,1,0:T(8,128)(2,1)S(1)}, u32[]{:S(2)}, u32[]{:S(2)}) collective-permute-start(bf16[4,256,128]{2,1,0:T(8,128)(2,1)S(1)} %get-tuple-element.47.refs_0_), channel_id=1, source_target_pairs={{0,2},{1,3},{2,0},{3,1},{4,6},{5,7},{6,4},{7,5},{8,10},{9,11},{10,... | collective-permute-start | bytes 786440 | tf_op jit(solution)/shard_map/ppermute | solution.py:389
  13.2 1.3 %collective-permute-done.4.refs_1_ = bf16[4,256,128]{2,1,0:T(8,128)(2,1)S(1)} collective-permute-done((bf16[4,256,128]{2,1,0:T(8,128)(2,1)S(1)}, bf16[4,256,128]{2,1,0:T(8,128)(2,1)S(1)}, u32[]{:S(2)}, u32[]{:S(2)}) %collective-permute-start.4) | collective-permute-done | bytes 262176 | tf_op jit(solution)/shard_map/ppermute | solution.py:389
  14.5 1.7 %forward.7 = (bf16[4,256,128]{2,1,0:T(8,128)(2,1)S(1)}, bf16[4,256,512]{2,1,0:T(8,128)(2,1)S(1)}, f32[4,256,512]{2,1,0:T(8,128)S(1)}) custom-call(bf16[4,256,128]{2,1,0:T(8,128)(2,1)S(1)} %get-tuple-element.47.refs_0_, f32[4,512]{1,0:T(4,128)S(1)} %get-tuple-element.42.refs_1_, bf16[4,1024,512]{2,1,0:T(8,128)(2,1)S(1)} %get-tuple-element.43.refs_2_.refs_8_, ...), custom_call_target="tpu_custom_call" | custom-call | flops 671088640 | tf_op jit(solution)/shard_map/forward/pallas_call | solution.py:138
  16.2 0.0 collective-permute-done.5.refs_2_
  16.3 2.1 %collective-permute-start = (bf16[4,256,128]{2,1,0:T(8,128)(2,1)S(1)}, bf16[4,256,128]{2,1,0:T(8,128)(2,1)S(1)}, u32[]{:S(2)}, u32[]{:S(2)}) collective-permute-start(bf16[4,256,128]{2,1,0:T(8,128)(2,1)S(1)} %get-tuple-element.48.refs_10_.refs_0_), channel_id=1, source_target_pairs={{0,2},{1,3},{2,0},{3,1},{4,6},{5,7},{6,4},{7,5},{8,10},{9,11},{10,... | collective-permute-start | bytes 786440 | tf_op jit(solution)/shard_map/ppermute | solution.py:389
  18.4 1.8 %collective-permute-done.1.refs_1_ = bf16[4,256,128]{2,1,0:T(8,128)(2,1)S(1)} collective-permute-done((bf16[4,256,128]{2,1,0:T(8,128)(2,1)S(1)}, bf16[4,256,128]{2,1,0:T(8,128)(2,1)S(1)}, u32[]{:S(2)}, u32[]{:S(2)}) %collective-permute-start.1) | collective-permute-done | bytes 262176 | tf_op jit(solution)/shard_map/ppermute | solution.py:389
  20.1 0.0 collective-permute-start.3
  20.2 0.6 %collective-permute-start.10 = (bf16[4,256,128]{2,1,0:T(8,128)(2,1)S(1)}, bf16[4,256,128]{2,1,0:T(8,128)(2,1)S(1)}, u32[]{:S(2)}, u32[]{:S(2)}) collective-permute-start(bf16[4,256,128]{2,1,0:T(8,128)(2,1)S(1)} %get-tuple-element.47.refs_0_), channel_id=1, source_target_pairs={{0,1},{1,0},{2,3},{3,2},{4,5},{5,4},{6,7},{7,6},{8,9},{9,8},{10,11... | collective-permute-start | bytes 786440 | tf_op jit(solution)/shard_map/ppermute | solution.py:389
  20.8 0.2 broadcast_in_dim.10.refs_5_
  21.0 2.9 %backward.4 = (f32[512,512]{1,0:T(8,128)S(1)}, f32[512,128]{1,0:T(8,128)S(1)}, f32[16,512]{1,0:T(8,128)S(1)}) custom-call(bf16[4,256,128]{2,1,0:T(8,128)(2,1)S(1)} %get-tuple-element.41.refs_0_, bf16[4,256,128]{2,1,0:T(8,128)(2,1)S(1)} %collective-permute-done.4.refs_1_, bf16[4,256,128]{2,1,0:T(8,128)(2,1)S(1)} %collective-permute-done.5.refs_2_, ...), custom_call_target="tpu_custom_call" | custom-call | flops 1006632960 | tf_op jit(solution)/shard_map/backward/pallas_call | solution.py:283
  23.9 1.9 %collective-permute-done.9.value = bf16[4,256,128]{2,1,0:T(8,128)(2,1)S(1)} collective-permute-done((bf16[4,256,128]{2,1,0:T(8,128)(2,1)S(1)}, bf16[4,256,128]{2,1,0:T(8,128)(2,1)S(1)}, u32[]{:S(2)}, u32[]{:S(2)}) %collective-permute-start.9) | collective-permute-done | bytes 262176 | tf_op jit(solution)/shard_map/ppermute | solution.py:389
  25.7 0.0 collective-permute-start.7
  25.8 0.0 collective-permute-done.2.refs_2_
  25.8 0.5 collective-permute-start.11
  26.3 0.0 collective-permute-done.3.refs_3_
  26.3 2.7 %backward.5 = (f32[512,512]{1,0:T(8,128)S(1)}, f32[512,128]{1,0:T(8,128)S(1)}, f32[16,512]{1,0:T(8,128)S(1)}) custom-call(bf16[4,256,128]{2,1,0:T(8,128)(2,1)S(1)} %get-tuple-element.46.refs_0_, bf16[4,256,128]{2,1,0:T(8,128)(2,1)S(1)} %collective-permute-done.1.refs_1_, bf16[4,256,128]{2,1,0:T(8,128)(2,1)S(1)} %collective-permute-done.2.refs_2_, ...), custom_call_target="tpu_custom_call" | custom-call | flops 1006632960 | tf_op jit(solution)/shard_map/backward/pallas_call | solution.py:283
  29.0 1.6 %collective-permute-done.value = bf16[4,256,128]{2,1,0:T(8,128)(2,1)S(1)} collective-permute-done((bf16[4,256,128]{2,1,0:T(8,128)(2,1)S(1)}, bf16[4,256,128]{2,1,0:T(8,128)(2,1)S(1)}, u32[]{:S(2)}, u32[]{:S(2)}) %collective-permute-start) | collective-permute-done | bytes 262176 | tf_op jit(solution)/shard_map/ppermute | solution.py:389
  30.5 0.0 collective-permute-start.8
  30.5 0.0 collective-permute-done.10.refs_2_
  30.6 0.0 collective-permute-done.11.refs_3_
  30.6 2.7 %backward.6 = (f32[512,512]{1,0:T(8,128)S(1)}, f32[512,128]{1,0:T(8,128)S(1)}, f32[16,512]{1,0:T(8,128)S(1)}) custom-call(bf16[4,256,128]{2,1,0:T(8,128)(2,1)S(1)} %get-tuple-element.47.refs_0_, bf16[4,256,128]{2,1,0:T(8,128)(2,1)S(1)} %tie.3.refs_1_, bf16[4,256,128]{2,1,0:T(8,128)(2,1)S(1)} %collective-permute-done.10.refs_2_, ...), custom_call_target="tpu_custom_call" | custom-call | flops 1006632960 | tf_op jit(solution)/shard_map/backward/pallas_call | solution.py:283
  33.3 0.0 collective-permute-done.7.refs_2_
  33.3 2.9 %backward.7 = (f32[8,176,128]{2,1,0:T(8,128)S(1)}, f32[8,176,128]{2,1,0:T(8,128)S(1)}) custom-call(bf16[4,256,128]{2,1,0:T(8,128)(2,1)S(1)} %get-tuple-element.48.refs_10_.refs_0_, bf16[4,256,128]{2,1,0:T(8,128)(2,1)S(1)} %tie.2.refs_1_, bf16[4,256,128]{2,1,0:T(8,128)(2,1)S(1)} %collective-permute-done.7.refs_2_, ...), custom_call_target="tpu_custom_call" | custom-call | flops 1006632960 | tf_op jit(solution)/shard_map/backward/pallas_call | solution.py:283
  36.3 0.6 %collective-permute-start.12 = (f32[8,176,128]{2,1,0:T(8,128)S(1)}, f32[8,176,128]{2,1,0:T(8,128)S(1)}, u32[]{:S(2)}, u32[]{:S(2)}) collective-permute-start(f32[8,176,128]{2,1,0:T(8,128)S(1)} %get-tuple-element.67), channel_id=1, source_target_pairs={{0,1},{1,0},{2,3},{3,2},{4,5},{5,4},{6,7},{7,6},{8,9},{9,8},{10,11... | collective-permute-start | bytes 2162696 | tf_op jit(solution)/shard_map/ppermute | solution.py:389
  36.8 1.8 %collective-permute-done.12.arrived = f32[8,176,128]{2,1,0:T(8,128)S(1)} collective-permute-done((f32[8,176,128]{2,1,0:T(8,128)S(1)}, f32[8,176,128]{2,1,0:T(8,128)S(1)}, u32[]{:S(2)}, u32[]{:S(2)}) %collective-permute-start.12) | collective-permute-done | bytes 720928 | tf_op jit(solution)/shard_map/ppermute | solution.py:389
  38.6 0.1 spread_out.1
  38.7 3.8 %collective-permute-start.13 = (bf16[176,128]{1,0:T(8,128)(2,1)S(1)}, bf16[176,128]{1,0:T(8,128)(2,1)S(1)}, u32[]{:S(2)}, u32[]{:S(2)}) collective-permute-start(bf16[176,128]{1,0:T(8,128)(2,1)S(1)} %get-tuple-element.69), channel_id=1, source_target_pairs={{0,10},{1,11},{2,8},{3,9},{4,14},{5,15},{6,12},{7,13},{8,2},{9,3},... | collective-permute-start | bytes 135176 | tf_op jit(solution)/shard_map/ppermute | solution.py:399
  42.6 1.3 %collective-permute-start.14 = (bf16[176,128]{1,0:T(8,128)(2,1)S(1)}, bf16[176,128]{1,0:T(8,128)(2,1)S(1)}, u32[]{:S(2)}, u32[]{:S(2)}) collective-permute-start(bf16[176,128]{1,0:T(8,128)(2,1)S(1)} %get-tuple-element.70), channel_id=1, source_target_pairs={{0,14},{1,15},{2,12},{3,13},{4,10},{5,11},{6,8},{7,9},{8,6},{9,7},... | collective-permute-start | bytes 135176 | tf_op jit(solution)/shard_map/ppermute | solution.py:399
  43.9 1.7 %collective-permute-start.15 = (bf16[176,128]{1,0:T(8,128)(2,1)S(1)}, bf16[176,128]{1,0:T(8,128)(2,1)S(1)}, u32[]{:S(2)}, u32[]{:S(2)}) collective-permute-start(bf16[176,128]{1,0:T(8,128)(2,1)S(1)} %get-tuple-element.71), channel_id=1, source_target_pairs={{0,8},{1,9},{2,10},{3,11},{4,12},{5,13},{6,14},{7,15},{8,0},{9,1},... | collective-permute-start | bytes 135176 | tf_op jit(solution)/shard_map/ppermute | solution.py:399
  45.6 0.9 %collective-permute-start.16 = (bf16[176,128]{1,0:T(8,128)(2,1)S(1)}, bf16[176,128]{1,0:T(8,128)(2,1)S(1)}, u32[]{:S(2)}, u32[]{:S(2)}) collective-permute-start(bf16[176,128]{1,0:T(8,128)(2,1)S(1)} %get-tuple-element.72), channel_id=1, source_target_pairs={{0,12},{1,13},{2,14},{3,15},{4,8},{5,9},{6,10},{7,11},{8,4},{9,5},... | collective-permute-start | bytes 135176 | tf_op jit(solution)/shard_map/ppermute | solution.py:399
  46.5 1.8 %collective-permute-start.17 = (bf16[176,128]{1,0:T(8,128)(2,1)S(1)}, bf16[176,128]{1,0:T(8,128)(2,1)S(1)}, u32[]{:S(2)}, u32[]{:S(2)}) collective-permute-start(bf16[176,128]{1,0:T(8,128)(2,1)S(1)} %get-tuple-element.73), channel_id=1, source_target_pairs={{0,6},{1,7},{2,4},{3,5},{4,2},{5,3},{6,0},{7,1},{8,14},{9,15},{10,... | collective-permute-start | bytes 135176 | tf_op jit(solution)/shard_map/ppermute | solution.py:399
  48.3 0.0 collective-permute-done.13.refs_0_
  48.3 1.0 %collective-permute-start.18 = (bf16[176,128]{1,0:T(8,128)(2,1)S(1)}, bf16[176,128]{1,0:T(8,128)(2,1)S(1)}, u32[]{:S(2)}, u32[]{:S(2)}) collective-permute-start(bf16[176,128]{1,0:T(8,128)(2,1)S(1)} %get-tuple-element.74), channel_id=1, source_target_pairs={{0,4},{1,5},{2,6},{3,7},{4,0},{5,1},{6,2},{7,3},{8,12},{9,13},{10,... | collective-permute-start | bytes 135176 | tf_op jit(solution)/shard_map/ppermute | solution.py:399
  49.3 0.2 collective-permute-done.14.refs_1_
  49.5 0.5 collective-permute-start.19
  50.0 1.8 %collective-permute-done.15.refs_2_ = bf16[176,128]{1,0:T(8,128)(2,1)S(1)} collective-permute-done((bf16[176,128]{1,0:T(8,128)(2,1)S(1)}, bf16[176,128]{1,0:T(8,128)(2,1)S(1)}, u32[]{:S(2)}, u32[]{:S(2)}) %collective-permute-start.15) | collective-permute-done | bytes 45088 | tf_op jit(solution)/shard_map/ppermute | solution.py:399
  51.8 1.0 %collective-permute-done.17.refs_4_ = bf16[176,128]{1,0:T(8,128)(2,1)S(1)} collective-permute-done((bf16[176,128]{1,0:T(8,128)(2,1)S(1)}, bf16[176,128]{1,0:T(8,128)(2,1)S(1)}, u32[]{:S(2)}, u32[]{:S(2)}) %collective-permute-start.17) | collective-permute-done | bytes 45088 | tf_op jit(solution)/shard_map/ppermute | solution.py:399
  52.8 0.2 collective-permute-done.18.refs_5_
  53.0 0.5 collective-permute-done.19.refs_6_
  53.5 0.9 %finish.1 = (f32[32,512]{1,0:T(8,128)}, f32[32,128]{1,0:T(8,128)}, f32[1,32]{1,0:T(1,128)}) custom-call(f32[176,128]{1,0:T(8,128)S(1)} %get-tuple-element.68.mine, bf16[176,128]{1,0:T(8,128)(2,1)S(1)} %collective-permute-done.13.refs_0_, bf16[176,128]{1,0:T(8,128)(2,1)S(1)} %collective-permute-done.14.refs_1_, ...), custom_call_target="tpu_custom_call" | custom-call | tf_op jit(solution)/shard_map/finish/pallas_call | solution.py:352
  (10 shorter events, 0.1 us)
Async XLA Ops:
  4.4 10.1 %collective-permute-start.4 = (bf16[4,256,128]{2,1,0:T(8,128)(2,1)S(1)}, bf16[4,256,128]{2,1,0:T(8,128)(2,1)S(1)}, u32[]{:S(2)}, u32[]{:S(2)}) collective-permute-start(bf16[4,256,128]{2,1,0:T(8,128)(2,1)S(1)} %get-tuple-element.41.refs_0_), channel_id=1, source_target_pairs={{0,2},{1,3},{2,0},{3,1},{4,6},{5,7},{6,4},{7,5},{8,10},{9,11},{10,... | collective-permute-start | bytes 786440 | tf_op jit(solution)/shard_map/ppermute | solution.py:389
  7.4 8.9 %collective-permute-start.5 = (bf16[4,256,128]{2,1,0:T(8,128)(2,1)S(1)}, bf16[4,256,128]{2,1,0:T(8,128)(2,1)S(1)}, u32[]{:S(2)}, u32[]{:S(2)}) collective-permute-start(bf16[4,256,128]{2,1,0:T(8,128)(2,1)S(1)} %get-tuple-element.41.refs_0_), channel_id=1, source_target_pairs={{0,1},{1,0},{2,3},{3,2},{4,5},{5,4},{6,7},{7,6},{8,9},{9,8},{10,11... | collective-permute-start | bytes 786440 | tf_op jit(solution)/shard_map/ppermute | solution.py:389
  9.1 11.0 %collective-permute-start.1 = (bf16[4,256,128]{2,1,0:T(8,128)(2,1)S(1)}, bf16[4,256,128]{2,1,0:T(8,128)(2,1)S(1)}, u32[]{:S(2)}, u32[]{:S(2)}) collective-permute-start(bf16[4,256,128]{2,1,0:T(8,128)(2,1)S(1)} %get-tuple-element.46.refs_0_), channel_id=1, source_target_pairs={{0,2},{1,3},{2,0},{3,1},{4,6},{5,7},{6,4},{7,5},{8,10},{9,11},{10,... | collective-permute-start | bytes 786440 | tf_op jit(solution)/shard_map/ppermute | solution.py:389
  9.3 16.5 %collective-permute-start.2 = (bf16[4,256,128]{2,1,0:T(8,128)(2,1)S(1)}, bf16[4,256,128]{2,1,0:T(8,128)(2,1)S(1)}, u32[]{:S(2)}, u32[]{:S(2)}) collective-permute-start(bf16[4,256,128]{2,1,0:T(8,128)(2,1)S(1)} %get-tuple-element.46.refs_0_), channel_id=1, source_target_pairs={{0,1},{1,0},{2,3},{3,2},{4,5},{5,4},{6,7},{7,6},{8,9},{9,8},{10,11... | collective-permute-start | bytes 786440 | tf_op jit(solution)/shard_map/ppermute | solution.py:389
  11.5 8.6 %copy-start.1 = (s32[1024]{0:T(1024)S(1)}, s32[1024]{0:T(1024)}, u32[]{:S(2)}) copy-start(s32[1024]{0:T(1024)} %param.10) | copy-start | bytes 12292
  11.5 9.5 %copy-start = (f32[1024,128]{1,0:T(8,128)S(1)}, f32[1024,128]{1,0:T(8,128)}, u32[]{:S(2)}) copy-start(f32[1024,128]{1,0:T(8,128)} %refs_4_.9) | copy-start | bytes 1572868
  11.5 14.2 %collective-permute-start.9 = (bf16[4,256,128]{2,1,0:T(8,128)(2,1)S(1)}, bf16[4,256,128]{2,1,0:T(8,128)(2,1)S(1)}, u32[]{:S(2)}, u32[]{:S(2)}) collective-permute-start(bf16[4,256,128]{2,1,0:T(8,128)(2,1)S(1)} %get-tuple-element.47.refs_0_), channel_id=1, source_target_pairs={{0,2},{1,3},{2,0},{3,1},{4,6},{5,7},{6,4},{7,5},{8,10},{9,11},{10,... | collective-permute-start | bytes 786440 | tf_op jit(solution)/shard_map/ppermute | solution.py:389
  14.5 5.7 %collective-permute-start.6 = (bf16[4,256,128]{2,1,0:T(8,128)(2,1)S(1)}, bf16[4,256,128]{2,1,0:T(8,128)(2,1)S(1)}, u32[]{:S(2)}, u32[]{:S(2)}) collective-permute-start(bf16[4,256,128]{2,1,0:T(8,128)(2,1)S(1)} %collective-permute-done.4.refs_1_), channel_id=1, source_target_pairs={{0,1},{1,0},{2,3},{3,2},{4,5},{5,4},{6,7},{7,6},{8,9},{9,8},{10,11... | collective-permute-start | bytes 786440 | tf_op jit(solution)/shard_map/ppermute | solution.py:389
  16.3 14.3 %collective-permute-start = (bf16[4,256,128]{2,1,0:T(8,128)(2,1)S(1)}, bf16[4,256,128]{2,1,0:T(8,128)(2,1)S(1)}, u32[]{:S(2)}, u32[]{:S(2)}) collective-permute-start(bf16[4,256,128]{2,1,0:T(8,128)(2,1)S(1)} %get-tuple-element.48.refs_10_.refs_0_), channel_id=1, source_target_pairs={{0,2},{1,3},{2,0},{3,1},{4,6},{5,7},{6,4},{7,5},{8,10},{9,11},{10,... | collective-permute-start | bytes 786440 | tf_op jit(solution)/shard_map/ppermute | solution.py:389
  20.1 6.1 %collective-permute-start.3 = (bf16[4,256,128]{2,1,0:T(8,128)(2,1)S(1)}, bf16[4,256,128]{2,1,0:T(8,128)(2,1)S(1)}, u32[]{:S(2)}, u32[]{:S(2)}) collective-permute-start(bf16[4,256,128]{2,1,0:T(8,128)(2,1)S(1)} %collective-permute-done.1.refs_1_), channel_id=1, source_target_pairs={{0,1},{1,0},{2,3},{3,2},{4,5},{5,4},{6,7},{7,6},{8,9},{9,8},{10,11... | collective-permute-start | bytes 786440 | tf_op jit(solution)/shard_map/ppermute | solution.py:389
  20.2 10.4 %collective-permute-start.10 = (bf16[4,256,128]{2,1,0:T(8,128)(2,1)S(1)}, bf16[4,256,128]{2,1,0:T(8,128)(2,1)S(1)}, u32[]{:S(2)}, u32[]{:S(2)}) collective-permute-start(bf16[4,256,128]{2,1,0:T(8,128)(2,1)S(1)} %get-tuple-element.47.refs_0_), channel_id=1, source_target_pairs={{0,1},{1,0},{2,3},{3,2},{4,5},{5,4},{6,7},{7,6},{8,9},{9,8},{10,11... | collective-permute-start | bytes 786440 | tf_op jit(solution)/shard_map/ppermute | solution.py:389
  25.7 7.5 %collective-permute-start.7 = (bf16[4,256,128]{2,1,0:T(8,128)(2,1)S(1)}, bf16[4,256,128]{2,1,0:T(8,128)(2,1)S(1)}, u32[]{:S(2)}, u32[]{:S(2)}) collective-permute-start(bf16[4,256,128]{2,1,0:T(8,128)(2,1)S(1)} %get-tuple-element.48.refs_10_.refs_0_), channel_id=1, source_target_pairs={{0,1},{1,0},{2,3},{3,2},{4,5},{5,4},{6,7},{7,6},{8,9},{9,8},{10,11... | collective-permute-start | bytes 786440 | tf_op jit(solution)/shard_map/ppermute | solution.py:389
  25.8 4.8 %collective-permute-start.11 = (bf16[4,256,128]{2,1,0:T(8,128)(2,1)S(1)}, bf16[4,256,128]{2,1,0:T(8,128)(2,1)S(1)}, u32[]{:S(2)}, u32[]{:S(2)}) collective-permute-start(bf16[4,256,128]{2,1,0:T(8,128)(2,1)S(1)} %tie.3.refs_1_), channel_id=1, source_target_pairs={{0,1},{1,0},{2,3},{3,2},{4,5},{5,4},{6,7},{7,6},{8,9},{9,8},{10,11... | collective-permute-start | bytes 786440 | tf_op jit(solution)/shard_map/ppermute | solution.py:389
  30.5 2.8 %collective-permute-start.8 = (bf16[4,256,128]{2,1,0:T(8,128)(2,1)S(1)}, bf16[4,256,128]{2,1,0:T(8,128)(2,1)S(1)}, u32[]{:S(2)}, u32[]{:S(2)}) collective-permute-start(bf16[4,256,128]{2,1,0:T(8,128)(2,1)S(1)} %tie.2.refs_1_), channel_id=1, source_target_pairs={{0,1},{1,0},{2,3},{3,2},{4,5},{5,4},{6,7},{7,6},{8,9},{9,8},{10,11... | collective-permute-start | bytes 786440 | tf_op jit(solution)/shard_map/ppermute | solution.py:389
  36.3 2.4 %collective-permute-start.12 = (f32[8,176,128]{2,1,0:T(8,128)S(1)}, f32[8,176,128]{2,1,0:T(8,128)S(1)}, u32[]{:S(2)}, u32[]{:S(2)}) collective-permute-start(f32[8,176,128]{2,1,0:T(8,128)S(1)} %get-tuple-element.67), channel_id=1, source_target_pairs={{0,1},{1,0},{2,3},{3,2},{4,5},{5,4},{6,7},{7,6},{8,9},{9,8},{10,11... | collective-permute-start | bytes 2162696 | tf_op jit(solution)/shard_map/ppermute | solution.py:389
  38.7 9.6 %collective-permute-start.13 = (bf16[176,128]{1,0:T(8,128)(2,1)S(1)}, bf16[176,128]{1,0:T(8,128)(2,1)S(1)}, u32[]{:S(2)}, u32[]{:S(2)}) collective-permute-start(bf16[176,128]{1,0:T(8,128)(2,1)S(1)} %get-tuple-element.69), channel_id=1, source_target_pairs={{0,10},{1,11},{2,8},{3,9},{4,14},{5,15},{6,12},{7,13},{8,2},{9,3},... | collective-permute-start | bytes 135176 | tf_op jit(solution)/shard_map/ppermute | solution.py:399
  42.6 6.9 %collective-permute-start.14 = (bf16[176,128]{1,0:T(8,128)(2,1)S(1)}, bf16[176,128]{1,0:T(8,128)(2,1)S(1)}, u32[]{:S(2)}, u32[]{:S(2)}) collective-permute-start(bf16[176,128]{1,0:T(8,128)(2,1)S(1)} %get-tuple-element.70), channel_id=1, source_target_pairs={{0,14},{1,15},{2,12},{3,13},{4,10},{5,11},{6,8},{7,9},{8,6},{9,7},... | collective-permute-start | bytes 135176 | tf_op jit(solution)/shard_map/ppermute | solution.py:399
  43.9 7.9 %collective-permute-start.15 = (bf16[176,128]{1,0:T(8,128)(2,1)S(1)}, bf16[176,128]{1,0:T(8,128)(2,1)S(1)}, u32[]{:S(2)}, u32[]{:S(2)}) collective-permute-start(bf16[176,128]{1,0:T(8,128)(2,1)S(1)} %get-tuple-element.71), channel_id=1, source_target_pairs={{0,8},{1,9},{2,10},{3,11},{4,12},{5,13},{6,14},{7,15},{8,0},{9,1},... | collective-permute-start | bytes 135176 | tf_op jit(solution)/shard_map/ppermute | solution.py:399
  45.6 6.3 %collective-permute-start.16 = (bf16[176,128]{1,0:T(8,128)(2,1)S(1)}, bf16[176,128]{1,0:T(8,128)(2,1)S(1)}, u32[]{:S(2)}, u32[]{:S(2)}) collective-permute-start(bf16[176,128]{1,0:T(8,128)(2,1)S(1)} %get-tuple-element.72), channel_id=1, source_target_pairs={{0,12},{1,13},{2,14},{3,15},{4,8},{5,9},{6,10},{7,11},{8,4},{9,5},... | collective-permute-start | bytes 135176 | tf_op jit(solution)/shard_map/ppermute | solution.py:399
  46.5 6.3 %collective-permute-start.17 = (bf16[176,128]{1,0:T(8,128)(2,1)S(1)}, bf16[176,128]{1,0:T(8,128)(2,1)S(1)}, u32[]{:S(2)}, u32[]{:S(2)}) collective-permute-start(bf16[176,128]{1,0:T(8,128)(2,1)S(1)} %get-tuple-element.73), channel_id=1, source_target_pairs={{0,6},{1,7},{2,4},{3,5},{4,2},{5,3},{6,0},{7,1},{8,14},{9,15},{10,... | collective-permute-start | bytes 135176 | tf_op jit(solution)/shard_map/ppermute | solution.py:399
  48.3 4.7 %collective-permute-start.18 = (bf16[176,128]{1,0:T(8,128)(2,1)S(1)}, bf16[176,128]{1,0:T(8,128)(2,1)S(1)}, u32[]{:S(2)}, u32[]{:S(2)}) collective-permute-start(bf16[176,128]{1,0:T(8,128)(2,1)S(1)} %get-tuple-element.74), channel_id=1, source_target_pairs={{0,4},{1,5},{2,6},{3,7},{4,0},{5,1},{6,2},{7,3},{8,12},{9,13},{10,... | collective-permute-start | bytes 135176 | tf_op jit(solution)/shard_map/ppermute | solution.py:399
  49.5 4.0 %collective-permute-start.19 = (bf16[176,128]{1,0:T(8,128)(2,1)S(1)}, bf16[176,128]{1,0:T(8,128)(2,1)S(1)}, u32[]{:S(2)}, u32[]{:S(2)}) collective-permute-start(bf16[176,128]{1,0:T(8,128)(2,1)S(1)} %get-tuple-element.75), channel_id=1, source_target_pairs={{0,2},{1,3},{2,0},{3,1},{4,6},{5,7},{6,4},{7,5},{8,10},{9,11},{10,... | collective-permute-start | bytes 135176 | tf_op jit(solution)/shard_map/ppermute | solution.py:399

commit v5 on v4

--- a/solution.py
+++ b/solution.py
@@ -18,8 +18,10 @@
 SMALL_LIMIT = 8 * 1024 * 1024
 TINY_LIMIT = 1024 * 1024
 LINK = BF16
-COST = 2
-LAG = 1
+LAST = BF16
+COST_F = 2
+COST_B = 2
+LAGS = (9, 1, 1)
 GELU_A = math.sqrt(2.0 / math.pi)
 GELU_B = GELU_A * 0.044715
 
@@ -65,7 +67,7 @@
             rest = pl.ds(size, points - size)
             loads.append((latents.at[:, rest, :], latents_near.at[:, rest, :]))
         loads = [pltpu.make_async_copy(a, b, sems.at[k]) for k, (a, b) in enumerate(loads)]
-        for load in loads:
+        for load in loads[: 4 + members]:
             load.start()
         latents, w_in_ref, w_out_ref = latents_near, w_in_near, w_out_near
         loads[1].wait()
@@ -74,6 +76,8 @@
             shift[m : m + 1, :] = bias[...] + noise_row(seeds[m], bias.shape[1])
         loads[0].wait()
         loads[4].wait()
+        for load in loads[4 + members :]:
+            load.start()
     else:
         _, shift, latents, w_in_ref, w_out_ref, outputs, hidden, slope = refs
     members = latents.shape[0]
@@ -143,7 +147,7 @@
         scratch_shapes=scratch,
         compiler_params=pltpu.CompilerParams(vmem_limit_bytes=VMEM_LIMIT),
         cost_estimate=pl.CostEstimate(
-            flops=COST * members * size * width * (depth + variables),
+            flops=int(COST_F * members * size * width * (depth + variables)),
             bytes_accessed=0,
             transcendentals=0,
         ),
@@ -294,7 +298,7 @@
         ],
         compiler_params=pltpu.CompilerParams(vmem_limit_bytes=VMEM_LIMIT),
         cost_estimate=pl.CostEstimate(
-            flops=COST * members * size * (width * (depth + 2 * variables) + count * TILE * variables * 3),
+            flops=int(COST_B * members * size * (width * (depth + 2 * variables) + count * TILE * variables * 3)),
             bytes_accessed=0,
             transcendentals=0,
         ),
@@ -302,30 +306,57 @@
     )(own, *others, targets, area, hidden, slope, latents, weight_out, *(prior or ()), *(() if after is None else (after,)))
 
 
-OFFSETS = ((2, 1), (3, 1), (2, 0), (3, 0), (1, 1), (1, 0), (0, 1))
+SQUARE = ((1, 1), (1, 0), (0, 1))
 
 
 def spread_body(keep, arrived, mine, *parts):
-    z, x = lax.axis_index("pts"), lax.axis_index("mem") >> 1
-    here = z * 2 + x
-    mine[...] = keep[here] + arrived[here]
-    for part, (dz, dx) in zip(parts, OFFSETS):
-        there = (z ^ dz) * 2 + (x ^ dx)
-        part[...] = (keep[there] + arrived[there]).astype(part.dtype)
-
-
-def spread_out(keep, arrived, dtype):
+    z, x = lax.axis_index("pts") & 1, lax.axis_index("mem") >> 1
+    for high in range(2):
+        here = (2 * high + z) * 2 + x
+        mine[high] = keep[here] + arrived[here]
+        for part, (dz, dx) in zip(parts, SQUARE):
+            there = (2 * high + (z ^ dz)) * 2 + (x ^ dx)
+            part[high] = (keep[there] + arrived[there]).astype(part.dtype)
+
+
+def spread_out(keep, arrived):
     _, rows, lanes = keep.shape
     whole = pl.BlockSpec(memory_space=pltpu.VMEM)
     return pl.pallas_call(
         spread_body,
         in_specs=[whole, whole],
-        out_specs=[whole] * (1 + len(OFFSETS)),
-        out_shape=[jax.ShapeDtypeStruct((rows, lanes), F32)]
-        + [jax.ShapeDtypeStruct((rows, lanes), dtype)] * len(OFFSETS),
+        out_specs=[whole] * (1 + len(SQUARE)),
+        out_shape=[jax.ShapeDtypeStruct((2, rows, lanes), F32)]
+        + [jax.ShapeDtypeStruct((2, rows, lanes), LINK)] * len(SQUARE),
         compiler_params=pltpu.CompilerParams(vmem_limit_bytes=SMALL_LIMIT),
         name="spread_out",
     )(keep, arrived)
+
+
+def fold_body(mine, *refs):
+    parts, (keep, send) = refs[:-2], refs[-2:]
+    high = lax.axis_index("pts") >> 1
+    for place, out in ((high, keep), (1 - high, send)):
+        total = mine[place]
+        for part in parts:
+            total += part[place].astype(F32)
+        out[...] = total.astype(out.dtype)
+
+
+def fold(mine, parts):
+    _, rows, lanes = mine.shape
+    whole = pl.BlockSpec(memory_space=pltpu.VMEM)
+    return pl.pallas_call(
+        fold_body,
+        in_specs=[whole] * (1 + len(parts)),
+        out_specs=[whole] * 2,
+        out_shape=[
+            jax.ShapeDtypeStruct((rows, lanes), F32),
+            jax.ShapeDtypeStruct((rows, lanes), LAST),
+        ],
+        compiler_params=pltpu.CompilerParams(vmem_limit_bytes=SMALL_LIMIT),
+        name="fold",
+    )(mine, *parts)
 
 
 def finish_body(share, mine, *refs):
@@ -432,8 +463,8 @@
     sums = []
     for k, (first, size) in enumerate(plan):
         held, hidden, slope = saved[k]
-        if k > LAG:
-            held[1] = tie(held[1], sums[k - LAG - 1])
+        if k and LAGS[k - 1] < k:
+            held[1] = tie(held[1], sums[k - 1 - LAGS[k - 1]])
         for bit in bits[1:]:
             held = held + [swap_members(v, bit) for v in held]
         last = first + size == points
@@ -448,9 +479,10 @@
         return scatter(total[0]), scatter(total[1]), scatter(jnp.sum(total[2], axis=0))
     keep, send = total
     arrived = swap_members(send, 1)
-    mine, *parts = spread_out(keep, arrived, LINK)
-    parts = [swap_points(part, dz, dx) for part, (dz, dx) in zip(parts, OFFSETS)]
-    in_share, out_share, bias_share = finish(mine, parts, depth // dests, width)
+    mine, *parts = spread_out(keep, arrived)
+    parts = [swap_points(part, dz, dx) for part, (dz, dx) in zip(parts, SQUARE)]
+    keep, send = fold(mine, parts)
+    in_share, out_share, bias_share = finish(keep, [swap_points(send, 2, 0)], depth // dests, width)
     return in_share, out_share, bias_share.reshape(depth // dests)
 
 

time: 54.5 us -> 52.9 us (0.971)
  starting transfers between devices: 20.3 us -> 15.4 us
  waiting for transfers between devices: 12 us -> 15.2 us
    ppermute x7 -> x4, starting transfers between devices: 11.1 us -> 6.25 us  [swap_points(): return lax.ppermute(block, ('pts', 'mem'), pairs)]
    ppermute x7 -> x4, waiting for transfers between devices: 3.67 us -> 6.91 us  [swap_points(): return lax.ppermute(block, ('pts', 'mem'), pairs)]
  transfers between devices with their start and end apart: 20 -> 17, of which waited for: 10 -> 8; matrix products, arithmetic and copies ran while one was open for 0% -> 0% of each run, Pallas kernels for 25% -> 26%
where the time goes in v5:
time: 52.9 us; the launch traced here: 52.8 us
  Pallas kernels  21.1 us (40%)
  starting transfers between devices  15.4 us (29%)
  waiting for transfers between devices  15.2 us (29%)
  between operations  0.78 us (1%)
    pallas_call x4, Pallas kernels, backward(): pl.pallas_call(partial(backward_body, len(others), 0 if after is None els...  11.3 us
    ppermute x13, starting transfers between devices, swap_members(): return lax.ppermute(block, 'mem', [(i, i ^ bit) for i in range(size)])  9.16 us
    pallas_call x4, Pallas kernels, forward(): pl.pallas_call(partial(forward_body, first, size, piece_of(size, sub), st...  8.91 us
    ppermute x13, waiting for transfers between devices, swap_members(): return lax.ppermute(block, 'mem', [(i, i ^ bit) for i in range(size)])  8.28 us
    ppermute x4, waiting for transfers between devices, swap_points(): return lax.ppermute(block, ('pts', 'mem'), pairs)  6.91 us
    ppermute x4, starting transfers between devices, swap_points(): return lax.ppermute(block, ('pts', 'mem'), pairs)  6.25 us
  transfers between devices with their start and end apart: 17, of which 8 were waited for; matrix products, arithmetic and copies ran while one was open for 0% of the time, Pallas kernels for 26%

profile of v5, /device:TPU:0, one launch (start us, length us, event | category | flops | bytes accessed | tf_op | source)
XLA Modules:
  0.0 52.8 jit_solution(956754131229150993)
XLA Ops:
  0.6 3.7 %forward.4 = (bf16[4,256,128]{2,1,0:T(8,128)(2,1)S(1)}, bf16[4,256,512]{2,1,0:T(8,128)(2,1)S(1)}, f32[4,256,512]{2,1,0:T(8,128)S(1)}, f32[4,512]{1,0:T(4,128)S(1...) custom-call(s32[4]{0:T(128)} %refs_0_.1, f32[1,512]{1,0:T(1,128)} %bitcast.2, ...), custom_call_target="tpu_custom_call" | custom-call | flops 671088640 | tf_op jit(solution)/shard_map/forward/pallas_call | solution.py:142
  4.4 3.0 %collective-permute-start.4 = (bf16[4,256,128]{2,1,0:T(8,128)(2,1)S(1)}, bf16[4,256,128]{2,1,0:T(8,128)(2,1)S(1)}, u32[]{:S(2)}, u32[]{:S(2)}) collective-permute-start(bf16[4,256,128]{2,1,0:T(8,128)(2,1)S(1)} %get-tuple-element.39.refs_0_), channel_id=1, source_target_pairs={{0,2},{1,3},{2,0},{3,1},{4,6},{5,7},{6,4},{7,5},{8,10},{9,11},{10,... | collective-permute-start | bytes 786440 | tf_op jit(solution)/shard_map/ppermute | solution.py:420
  7.4 0.0 collective-permute-start.5
  7.4 1.7 %forward.5 = (bf16[4,256,128]{2,1,0:T(8,128)(2,1)S(1)}, bf16[4,256,512]{2,1,0:T(8,128)(2,1)S(1)}, f32[4,256,512]{2,1,0:T(8,128)S(1)}) custom-call(bf16[4,256,128]{2,1,0:T(8,128)(2,1)S(1)} %get-tuple-element.39.refs_0_, f32[4,512]{1,0:T(4,128)S(1)} %get-tuple-element.40.refs_1_, bf16[4,1024,512]{2,1,0:T(8,128)(2,1)S(1)} %get-tuple-element.41.refs_2_.refs_8_, ...), custom_call_target="tpu_custom_call" | custom-call | flops 671088640 | tf_op jit(solution)/shard_map/forward/pallas_call | solution.py:142
  9.1 0.2 collective-permute-start.1
  9.3 0.5 collective-permute-start.2
  9.8 1.7 %forward.6 = (bf16[4,256,128]{2,1,0:T(8,128)(2,1)S(1)}, bf16[4,256,512]{2,1,0:T(8,128)(2,1)S(1)}, f32[4,256,512]{2,1,0:T(8,128)S(1)}) custom-call(bf16[4,256,128]{2,1,0:T(8,128)(2,1)S(1)} %get-tuple-element.44.refs_0_, f32[4,512]{1,0:T(4,128)S(1)} %get-tuple-element.40.refs_1_, bf16[4,1024,512]{2,1,0:T(8,128)(2,1)S(1)} %get-tuple-element.41.refs_2_.refs_8_, ...), custom_call_target="tpu_custom_call" | custom-call | flops 671088640 | tf_op jit(solution)/shard_map/forward/pallas_call | solution.py:142
  11.5 0.0 copy-start.1
  11.5 0.0 copy-start
  11.5 1.7 %collective-permute-start.9 = (bf16[4,256,128]{2,1,0:T(8,128)(2,1)S(1)}, bf16[4,256,128]{2,1,0:T(8,128)(2,1)S(1)}, u32[]{:S(2)}, u32[]{:S(2)}) collective-permute-start(bf16[4,256,128]{2,1,0:T(8,128)(2,1)S(1)} %get-tuple-element.45.refs_0_), channel_id=1, source_target_pairs={{0,2},{1,3},{2,0},{3,1},{4,6},{5,7},{6,4},{7,5},{8,10},{9,11},{10,... | collective-permute-start | bytes 786440 | tf_op jit(solution)/shard_map/ppermute | solution.py:420
  13.2 1.3 %collective-permute-done.4.refs_1_ = bf16[4,256,128]{2,1,0:T(8,128)(2,1)S(1)} collective-permute-done((bf16[4,256,128]{2,1,0:T(8,128)(2,1)S(1)}, bf16[4,256,128]{2,1,0:T(8,128)(2,1)S(1)}, u32[]{:S(2)}, u32[]{:S(2)}) %collective-permute-start.4) | collective-permute-done | bytes 262176 | tf_op jit(solution)/shard_map/ppermute | solution.py:420
  14.5 0.0 collective-permute-start.6
  14.5 1.7 %forward.7 = (bf16[4,256,128]{2,1,0:T(8,128)(2,1)S(1)}, bf16[4,256,512]{2,1,0:T(8,128)(2,1)S(1)}, f32[4,256,512]{2,1,0:T(8,128)S(1)}) custom-call(bf16[4,256,128]{2,1,0:T(8,128)(2,1)S(1)} %get-tuple-element.45.refs_0_, f32[4,512]{1,0:T(4,128)S(1)} %get-tuple-element.40.refs_1_, bf16[4,1024,512]{2,1,0:T(8,128)(2,1)S(1)} %get-tuple-element.41.refs_2_.refs_8_, ...), custom_call_target="tpu_custom_call" | custom-call | flops 671088640 | tf_op jit(solution)/shard_map/forward/pallas_call | solution.py:142
  16.3 0.0 collective-permute-done.5.refs_2_
  16.3 2.1 %collective-permute-start = (bf16[4,256,128]{2,1,0:T(8,128)(2,1)S(1)}, bf16[4,256,128]{2,1,0:T(8,128)(2,1)S(1)}, u32[]{:S(2)}, u32[]{:S(2)}) collective-permute-start(bf16[4,256,128]{2,1,0:T(8,128)(2,1)S(1)} %get-tuple-element.46.refs_10_.refs_0_), channel_id=1, source_target_pairs={{0,2},{1,3},{2,0},{3,1},{4,6},{5,7},{6,4},{7,5},{8,10},{9,11},{10,... | collective-permute-start | bytes 786440 | tf_op jit(solution)/shard_map/ppermute | solution.py:420
  18.4 1.7 %collective-permute-done.1.refs_1_ = bf16[4,256,128]{2,1,0:T(8,128)(2,1)S(1)} collective-permute-done((bf16[4,256,128]{2,1,0:T(8,128)(2,1)S(1)}, bf16[4,256,128]{2,1,0:T(8,128)(2,1)S(1)}, u32[]{:S(2)}, u32[]{:S(2)}) %collective-permute-start.1) | collective-permute-done | bytes 262176 | tf_op jit(solution)/shard_map/ppermute | solution.py:420
  20.1 0.0 collective-permute-start.3
  20.2 0.0 collective-permute-done.6.refs_3_
  20.2 0.6 %collective-permute-start.10 = (bf16[4,256,128]{2,1,0:T(8,128)(2,1)S(1)}, bf16[4,256,128]{2,1,0:T(8,128)(2,1)S(1)}, u32[]{:S(2)}, u32[]{:S(2)}) collective-permute-start(bf16[4,256,128]{2,1,0:T(8,128)(2,1)S(1)} %get-tuple-element.45.refs_0_), channel_id=1, source_target_pairs={{0,1},{1,0},{2,3},{3,2},{4,5},{5,4},{6,7},{7,6},{8,9},{9,8},{10,11... | collective-permute-start | bytes 786440 | tf_op jit(solution)/shard_map/ppermute | solution.py:420
  20.8 0.2 broadcast_in_dim.10.refs_5_
  21.0 0.0 copy-done
  21.0 2.9 %backward.4 = (f32[512,512]{1,0:T(8,128)S(1)}, f32[512,128]{1,0:T(8,128)S(1)}, f32[16,512]{1,0:T(8,128)S(1)}) custom-call(bf16[4,256,128]{2,1,0:T(8,128)(2,1)S(1)} %get-tuple-element.39.refs_0_, bf16[4,256,128]{2,1,0:T(8,128)(2,1)S(1)} %collective-permute-done.4.refs_1_, bf16[4,256,128]{2,1,0:T(8,128)(2,1)S(1)} %collective-permute-done.5.refs_2_, ...), custom_call_target="tpu_custom_call" | custom-call | flops 1006632960 | tf_op jit(solution)/shard_map/backward/pallas_call | solution.py:287
  23.9 1.9 %collective-permute-done.9.value = bf16[4,256,128]{2,1,0:T(8,128)(2,1)S(1)} collective-permute-done((bf16[4,256,128]{2,1,0:T(8,128)(2,1)S(1)}, bf16[4,256,128]{2,1,0:T(8,128)(2,1)S(1)}, u32[]{:S(2)}, u32[]{:S(2)}) %collective-permute-start.9) | collective-permute-done | bytes 262176 | tf_op jit(solution)/shard_map/ppermute | solution.py:420
  25.8 0.0 collective-permute-start.7
  25.8 0.0 collective-permute-done.2.refs_2_
  25.8 0.5 collective-permute-start.11
  26.3 0.0 collective-permute-done.3.refs_3_
  26.3 2.7 %backward.5 = (f32[512,512]{1,0:T(8,128)S(1)}, f32[512,128]{1,0:T(8,128)S(1)}, f32[16,512]{1,0:T(8,128)S(1)}) custom-call(bf16[4,256,128]{2,1,0:T(8,128)(2,1)S(1)} %get-tuple-element.44.refs_0_, bf16[4,256,128]{2,1,0:T(8,128)(2,1)S(1)} %collective-permute-done.1.refs_1_, bf16[4,256,128]{2,1,0:T(8,128)(2,1)S(1)} %collective-permute-done.2.refs_2_, ...), custom_call_target="tpu_custom_call" | custom-call | flops 1006632960 | tf_op jit(solution)/shard_map/backward/pallas_call | solution.py:287
  29.0 1.5 %collective-permute-done.value = bf16[4,256,128]{2,1,0:T(8,128)(2,1)S(1)} collective-permute-done((bf16[4,256,128]{2,1,0:T(8,128)(2,1)S(1)}, bf16[4,256,128]{2,1,0:T(8,128)(2,1)S(1)}, u32[]{:S(2)}, u32[]{:S(2)}) %collective-permute-start) | collective-permute-done | bytes 262176 | tf_op jit(solution)/shard_map/ppermute | solution.py:420
  30.5 0.0 collective-permute-start.8
  30.5 0.0 collective-permute-done.10.refs_2_
  30.5 0.0 collective-permute-done.11.refs_3_
  30.6 2.7 %backward.6 = (f32[512,512]{1,0:T(8,128)S(1)}, f32[512,128]{1,0:T(8,128)S(1)}, f32[16,512]{1,0:T(8,128)S(1)}) custom-call(bf16[4,256,128]{2,1,0:T(8,128)(2,1)S(1)} %get-tuple-element.45.refs_0_, bf16[4,256,128]{2,1,0:T(8,128)(2,1)S(1)} %tie.3.refs_1_, bf16[4,256,128]{2,1,0:T(8,128)(2,1)S(1)} %collective-permute-done.10.refs_2_, ...), custom_call_target="tpu_custom_call" | custom-call | flops 1006632960 | tf_op jit(solution)/shard_map/backward/pallas_call | solution.py:287
  33.3 0.0 collective-permute-done.7.refs_2_
  33.3 0.0 collective-permute-done.8.refs_3_
  33.3 2.9 %backward.7 = (f32[8,176,128]{2,1,0:T(8,128)S(1)}, f32[8,176,128]{2,1,0:T(8,128)S(1)}) custom-call(bf16[4,256,128]{2,1,0:T(8,128)(2,1)S(1)} %get-tuple-element.46.refs_10_.refs_0_, bf16[4,256,128]{2,1,0:T(8,128)(2,1)S(1)} %tie.2.refs_1_, bf16[4,256,128]{2,1,0:T(8,128)(2,1)S(1)} %collective-permute-done.7.refs_2_, ...), custom_call_target="tpu_custom_call" | custom-call | flops 1006632960 | tf_op jit(solution)/shard_map/backward/pallas_call | solution.py:287
  36.2 0.6 %collective-permute-start.12 = (f32[8,176,128]{2,1,0:T(8,128)S(1)}, f32[8,176,128]{2,1,0:T(8,128)S(1)}, u32[]{:S(2)}, u32[]{:S(2)}) collective-permute-start(f32[8,176,128]{2,1,0:T(8,128)S(1)} %get-tuple-element.65), channel_id=1, source_target_pairs={{0,1},{1,0},{2,3},{3,2},{4,5},{5,4},{6,7},{7,6},{8,9},{9,8},{10,11... | collective-permute-start | bytes 2162696 | tf_op jit(solution)/shard_map/ppermute | solution.py:420
  36.8 1.8 %collective-permute-done.12.arrived = f32[8,176,128]{2,1,0:T(8,128)S(1)} collective-permute-done((f32[8,176,128]{2,1,0:T(8,128)S(1)}, f32[8,176,128]{2,1,0:T(8,128)S(1)}, u32[]{:S(2)}, u32[]{:S(2)}) %collective-permute-start.12) | collective-permute-done | bytes 720928 | tf_op jit(solution)/shard_map/ppermute | solution.py:420
  38.6 0.1 spread_out.1
  38.7 2.8 %collective-permute-start.13 = (bf16[2,176,128]{2,1,0:T(8,128)(2,1)S(1)}, bf16[2,176,128]{2,1,0:T(8,128)(2,1)S(1)}, u32[]{:S(2)}, u32[]{:S(2)}) collective-permute-start(bf16[2,176,128]{2,1,0:T(8,128)(2,1)S(1)} %get-tuple-element.67), channel_id=1, source_target_pairs={{0,6},{1,7},{2,4},{3,5},{4,2},{5,3},{6,0},{7,1},{8,14},{9,15},{10,... | collective-permute-start | bytes 270344 | tf_op jit(solution)/shard_map/ppermute | solution.py:430
  41.5 0.4 collective-permute-start.14
  42.0 0.3 collective-permute-start.15
  42.3 2.8 %collective-permute-done.13.refs_0_ = bf16[2,176,128]{2,1,0:T(8,128)(2,1)S(1)} collective-permute-done((bf16[2,176,128]{2,1,0:T(8,128)(2,1)S(1)}, bf16[2,176,128]{2,1,0:T(8,128)(2,1)S(1)}, u32[]{:S(2)}, u32[]{:S(2)}) %collective-permute-start.13) | collective-permute-done | bytes 90144 | tf_op jit(solution)/shard_map/ppermute | solution.py:430
  45.1 1.7 %collective-permute-done.14.refs_1_ = bf16[2,176,128]{2,1,0:T(8,128)(2,1)S(1)} collective-permute-done((bf16[2,176,128]{2,1,0:T(8,128)(2,1)S(1)}, bf16[2,176,128]{2,1,0:T(8,128)(2,1)S(1)}, u32[]{:S(2)}, u32[]{:S(2)}) %collective-permute-start.14) | collective-permute-done | bytes 90144 | tf_op jit(solution)/shard_map/ppermute | solution.py:430
  46.8 0.0 collective-permute-done.15.refs_2_
  46.8 2.7 %collective-permute-start.16 = (bf16[176,128]{1,0:T(8,128)(2,1)S(1)}, bf16[176,128]{1,0:T(8,128)(2,1)S(1)}, u32[]{:S(2)}, u32[]{:S(2)}) collective-permute-start(bf16[176,128]{1,0:T(8,128)(2,1)S(1)} %get-tuple-element.71), channel_id=1, source_target_pairs={{0,8},{1,9},{2,10},{3,11},{4,12},{5,13},{6,14},{7,15},{8,0},{9,1},... | collective-permute-start | bytes 135176 | tf_op jit(solution)/shard_map/ppermute | solution.py:430
  49.5 2.4 %collective-permute-done.16.refs_0_ = bf16[176,128]{1,0:T(8,128)(2,1)S(1)} collective-permute-done((bf16[176,128]{1,0:T(8,128)(2,1)S(1)}, bf16[176,128]{1,0:T(8,128)(2,1)S(1)}, u32[]{:S(2)}, u32[]{:S(2)}) %collective-permute-start.16) | collective-permute-done | bytes 45088 | tf_op jit(solution)/shard_map/ppermute | solution.py:430
  51.9 0.8 %finish.1 = (f32[32,512]{1,0:T(8,128)}, f32[32,128]{1,0:T(8,128)}, f32[1,32]{1,0:T(1,128)}) custom-call(f32[176,128]{1,0:T(8,128)S(1)} %get-tuple-element.70.mine, bf16[176,128]{1,0:T(8,128)(2,1)S(1)} %collective-permute-done.16.refs_0_), custom_call_target="tpu_custom_call" | custom-call | tf_op jit(solution)/shard_map/finish/pallas_call | solution.py:383
  (5 shorter events, 0.1 us)
Async XLA Ops:
  4.4 10.1 %collective-permute-start.4 = (bf16[4,256,128]{2,1,0:T(8,128)(2,1)S(1)}, bf16[4,256,128]{2,1,0:T(8,128)(2,1)S(1)}, u32[]{:S(2)}, u32[]{:S(2)}) collective-permute-start(bf16[4,256,128]{2,1,0:T(8,128)(2,1)S(1)} %get-tuple-element.39.refs_0_), channel_id=1, source_target_pairs={{0,2},{1,3},{2,0},{3,1},{4,6},{5,7},{6,4},{7,5},{8,10},{9,11},{10,... | collective-permute-start | bytes 786440 | tf_op jit(solution)/shard_map/ppermute | solution.py:420
  7.4 8.9 %collective-permute-start.5 = (bf16[4,256,128]{2,1,0:T(8,128)(2,1)S(1)}, bf16[4,256,128]{2,1,0:T(8,128)(2,1)S(1)}, u32[]{:S(2)}, u32[]{:S(2)}) collective-permute-start(bf16[4,256,128]{2,1,0:T(8,128)(2,1)S(1)} %get-tuple-element.39.refs_0_), channel_id=1, source_target_pairs={{0,1},{1,0},{2,3},{3,2},{4,5},{5,4},{6,7},{7,6},{8,9},{9,8},{10,11... | collective-permute-start | bytes 786440 | tf_op jit(solution)/shard_map/ppermute | solution.py:420
  9.1 11.0 %collective-permute-start.1 = (bf16[4,256,128]{2,1,0:T(8,128)(2,1)S(1)}, bf16[4,256,128]{2,1,0:T(8,128)(2,1)S(1)}, u32[]{:S(2)}, u32[]{:S(2)}) collective-permute-start(bf16[4,256,128]{2,1,0:T(8,128)(2,1)S(1)} %get-tuple-element.44.refs_0_), channel_id=1, source_target_pairs={{0,2},{1,3},{2,0},{3,1},{4,6},{5,7},{6,4},{7,5},{8,10},{9,11},{10,... | collective-permute-start | bytes 786440 | tf_op jit(solution)/shard_map/ppermute | solution.py:420
  9.3 16.5 %collective-permute-start.2 = (bf16[4,256,128]{2,1,0:T(8,128)(2,1)S(1)}, bf16[4,256,128]{2,1,0:T(8,128)(2,1)S(1)}, u32[]{:S(2)}, u32[]{:S(2)}) collective-permute-start(bf16[4,256,128]{2,1,0:T(8,128)(2,1)S(1)} %get-tuple-element.44.refs_0_), channel_id=1, source_target_pairs={{0,1},{1,0},{2,3},{3,2},{4,5},{5,4},{6,7},{7,6},{8,9},{9,8},{10,11... | collective-permute-start | bytes 786440 | tf_op jit(solution)/shard_map/ppermute | solution.py:420
  11.5 8.6 %copy-start.1 = (s32[1024]{0:T(1024)S(1)}, s32[1024]{0:T(1024)}, u32[]{:S(2)}) copy-start(s32[1024]{0:T(1024)} %param.10) | copy-start | bytes 12292
  11.5 9.5 %copy-start = (f32[1024,128]{1,0:T(8,128)S(1)}, f32[1024,128]{1,0:T(8,128)}, u32[]{:S(2)}) copy-start(f32[1024,128]{1,0:T(8,128)} %refs_4_.9) | copy-start | bytes 1572868
  11.5 14.2 %collective-permute-start.9 = (bf16[4,256,128]{2,1,0:T(8,128)(2,1)S(1)}, bf16[4,256,128]{2,1,0:T(8,128)(2,1)S(1)}, u32[]{:S(2)}, u32[]{:S(2)}) collective-permute-start(bf16[4,256,128]{2,1,0:T(8,128)(2,1)S(1)} %get-tuple-element.45.refs_0_), channel_id=1, source_target_pairs={{0,2},{1,3},{2,0},{3,1},{4,6},{5,7},{6,4},{7,5},{8,10},{9,11},{10,... | collective-permute-start | bytes 786440 | tf_op jit(solution)/shard_map/ppermute | solution.py:420
  14.5 5.7 %collective-permute-start.6 = (bf16[4,256,128]{2,1,0:T(8,128)(2,1)S(1)}, bf16[4,256,128]{2,1,0:T(8,128)(2,1)S(1)}, u32[]{:S(2)}, u32[]{:S(2)}) collective-permute-start(bf16[4,256,128]{2,1,0:T(8,128)(2,1)S(1)} %collective-permute-done.4.refs_1_), channel_id=1, source_target_pairs={{0,1},{1,0},{2,3},{3,2},{4,5},{5,4},{6,7},{7,6},{8,9},{9,8},{10,11... | collective-permute-start | bytes 786440 | tf_op jit(solution)/shard_map/ppermute | solution.py:420
  16.3 14.3 %collective-permute-start = (bf16[4,256,128]{2,1,0:T(8,128)(2,1)S(1)}, bf16[4,256,128]{2,1,0:T(8,128)(2,1)S(1)}, u32[]{:S(2)}, u32[]{:S(2)}) collective-permute-start(bf16[4,256,128]{2,1,0:T(8,128)(2,1)S(1)} %get-tuple-element.46.refs_10_.refs_0_), channel_id=1, source_target_pairs={{0,2},{1,3},{2,0},{3,1},{4,6},{5,7},{6,4},{7,5},{8,10},{9,11},{10,... | collective-permute-start | bytes 786440 | tf_op jit(solution)/shard_map/ppermute | solution.py:420
  20.1 6.1 %collective-permute-start.3 = (bf16[4,256,128]{2,1,0:T(8,128)(2,1)S(1)}, bf16[4,256,128]{2,1,0:T(8,128)(2,1)S(1)}, u32[]{:S(2)}, u32[]{:S(2)}) collective-permute-start(bf16[4,256,128]{2,1,0:T(8,128)(2,1)S(1)} %collective-permute-done.1.refs_1_), channel_id=1, source_target_pairs={{0,1},{1,0},{2,3},{3,2},{4,5},{5,4},{6,7},{7,6},{8,9},{9,8},{10,11... | collective-permute-start | bytes 786440 | tf_op jit(solution)/shard_map/ppermute | solution.py:420
  20.2 10.3 %collective-permute-start.10 = (bf16[4,256,128]{2,1,0:T(8,128)(2,1)S(1)}, bf16[4,256,128]{2,1,0:T(8,128)(2,1)S(1)}, u32[]{:S(2)}, u32[]{:S(2)}) collective-permute-start(bf16[4,256,128]{2,1,0:T(8,128)(2,1)S(1)} %get-tuple-element.45.refs_0_), channel_id=1, source_target_pairs={{0,1},{1,0},{2,3},{3,2},{4,5},{5,4},{6,7},{7,6},{8,9},{9,8},{10,11... | collective-permute-start | bytes 786440 | tf_op jit(solution)/shard_map/ppermute | solution.py:420
  25.8 7.5 %collective-permute-start.7 = (bf16[4,256,128]{2,1,0:T(8,128)(2,1)S(1)}, bf16[4,256,128]{2,1,0:T(8,128)(2,1)S(1)}, u32[]{:S(2)}, u32[]{:S(2)}) collective-permute-start(bf16[4,256,128]{2,1,0:T(8,128)(2,1)S(1)} %get-tuple-element.46.refs_10_.refs_0_), channel_id=1, source_target_pairs={{0,1},{1,0},{2,3},{3,2},{4,5},{5,4},{6,7},{7,6},{8,9},{9,8},{10,11... | collective-permute-start | bytes 786440 | tf_op jit(solution)/shard_map/ppermute | solution.py:420
  25.8 4.8 %collective-permute-start.11 = (bf16[4,256,128]{2,1,0:T(8,128)(2,1)S(1)}, bf16[4,256,128]{2,1,0:T(8,128)(2,1)S(1)}, u32[]{:S(2)}, u32[]{:S(2)}) collective-permute-start(bf16[4,256,128]{2,1,0:T(8,128)(2,1)S(1)} %tie.3.refs_1_), channel_id=1, source_target_pairs={{0,1},{1,0},{2,3},{3,2},{4,5},{5,4},{6,7},{7,6},{8,9},{9,8},{10,11... | collective-permute-start | bytes 786440 | tf_op jit(solution)/shard_map/ppermute | solution.py:420
  30.5 2.8 %collective-permute-start.8 = (bf16[4,256,128]{2,1,0:T(8,128)(2,1)S(1)}, bf16[4,256,128]{2,1,0:T(8,128)(2,1)S(1)}, u32[]{:S(2)}, u32[]{:S(2)}) collective-permute-start(bf16[4,256,128]{2,1,0:T(8,128)(2,1)S(1)} %tie.2.refs_1_), channel_id=1, source_target_pairs={{0,1},{1,0},{2,3},{3,2},{4,5},{5,4},{6,7},{7,6},{8,9},{9,8},{10,11... | collective-permute-start | bytes 786440 | tf_op jit(solution)/shard_map/ppermute | solution.py:420
  36.2 2.4 %collective-permute-start.12 = (f32[8,176,128]{2,1,0:T(8,128)S(1)}, f32[8,176,128]{2,1,0:T(8,128)S(1)}, u32[]{:S(2)}, u32[]{:S(2)}) collective-permute-start(f32[8,176,128]{2,1,0:T(8,128)S(1)} %get-tuple-element.65), channel_id=1, source_target_pairs={{0,1},{1,0},{2,3},{3,2},{4,5},{5,4},{6,7},{7,6},{8,9},{9,8},{10,11... | collective-permute-start | bytes 2162696 | tf_op jit(solution)/shard_map/ppermute | solution.py:420
  38.7 6.4 %collective-permute-start.13 = (bf16[2,176,128]{2,1,0:T(8,128)(2,1)S(1)}, bf16[2,176,128]{2,1,0:T(8,128)(2,1)S(1)}, u32[]{:S(2)}, u32[]{:S(2)}) collective-permute-start(bf16[2,176,128]{2,1,0:T(8,128)(2,1)S(1)} %get-tuple-element.67), channel_id=1, source_target_pairs={{0,6},{1,7},{2,4},{3,5},{4,2},{5,3},{6,0},{7,1},{8,14},{9,15},{10,... | collective-permute-start | bytes 270344 | tf_op jit(solution)/shard_map/ppermute | solution.py:430
  41.5 5.2 %collective-permute-start.14 = (bf16[2,176,128]{2,1,0:T(8,128)(2,1)S(1)}, bf16[2,176,128]{2,1,0:T(8,128)(2,1)S(1)}, u32[]{:S(2)}, u32[]{:S(2)}) collective-permute-start(bf16[2,176,128]{2,1,0:T(8,128)(2,1)S(1)} %get-tuple-element.68), channel_id=1, source_target_pairs={{0,4},{1,5},{2,6},{3,7},{4,0},{5,1},{6,2},{7,3},{8,12},{9,13},{10,... | collective-permute-start | bytes 270344 | tf_op jit(solution)/shard_map/ppermute | solution.py:430
  42.0 4.8 %collective-permute-start.15 = (bf16[2,176,128]{2,1,0:T(8,128)(2,1)S(1)}, bf16[2,176,128]{2,1,0:T(8,128)(2,1)S(1)}, u32[]{:S(2)}, u32[]{:S(2)}) collective-permute-start(bf16[2,176,128]{2,1,0:T(8,128)(2,1)S(1)} %get-tuple-element.69), channel_id=1, source_target_pairs={{0,2},{1,3},{2,0},{3,1},{4,6},{5,7},{6,4},{7,5},{8,10},{9,11},{10,... | collective-permute-start | bytes 270344 | tf_op jit(solution)/shard_map/ppermute | solution.py:430
  46.8 5.1 %collective-permute-start.16 = (bf16[176,128]{1,0:T(8,128)(2,1)S(1)}, bf16[176,128]{1,0:T(8,128)(2,1)S(1)}, u32[]{:S(2)}, u32[]{:S(2)}) collective-permute-start(bf16[176,128]{1,0:T(8,128)(2,1)S(1)} %get-tuple-element.71), channel_id=1, source_target_pairs={{0,8},{1,9},{2,10},{3,11},{4,12},{5,13},{6,14},{7,15},{8,0},{9,1},... | collective-permute-start | bytes 135176 | tf_op jit(solution)/shard_map/ppermute | solution.py:430

commit v6 on v4

--- a/solution.py
+++ b/solution.py
@@ -18,8 +18,9 @@
 SMALL_LIMIT = 8 * 1024 * 1024
 TINY_LIMIT = 1024 * 1024
 LINK = BF16
-COST = 2
-LAG = 1
+COST_F = 2
+COST_B = 8
+LAGS = (1, 1, 1)
 GELU_A = math.sqrt(2.0 / math.pi)
 GELU_B = GELU_A * 0.044715
 
@@ -65,7 +66,7 @@
             rest = pl.ds(size, points - size)
             loads.append((latents.at[:, rest, :], latents_near.at[:, rest, :]))
         loads = [pltpu.make_async_copy(a, b, sems.at[k]) for k, (a, b) in enumerate(loads)]
-        for load in loads:
+        for load in loads[: 4 + members]:
             load.start()
         latents, w_in_ref, w_out_ref = latents_near, w_in_near, w_out_near
         loads[1].wait()
@@ -74,6 +75,8 @@
             shift[m : m + 1, :] = bias[...] + noise_row(seeds[m], bias.shape[1])
         loads[0].wait()
         loads[4].wait()
+        for load in loads[4 + members :]:
+            load.start()
     else:
         _, shift, latents, w_in_ref, w_out_ref, outputs, hidden, slope = refs
     members = latents.shape[0]
@@ -143,7 +146,7 @@
         scratch_shapes=scratch,
         compiler_params=pltpu.CompilerParams(vmem_limit_bytes=VMEM_LIMIT),
         cost_estimate=pl.CostEstimate(
-            flops=COST * members * size * width * (depth + variables),
+            flops=int(COST_F * members * size * width * (depth + variables)),
             bytes_accessed=0,
             transcendentals=0,
         ),
@@ -265,7 +268,7 @@
                 send[place] = block
 
 
-def backward(own, others, targets, area, hidden, slope, latents, weight_out, prior, first, loss_coef, dests=0, after=None, unroll=8, sub=256):
+def backward(own, others, targets, area, hidden, slope, latents, weight_out, prior, first, loss_coef, dests=0, after=None, unroll=10, sub=256):
     members, size, variables = own.shape
     depth = latents.shape[2]
     width = weight_out.shape[0]
@@ -281,7 +284,7 @@
             jax.ShapeDtypeStruct((TILE, width), F32),
         ]
     return pl.pallas_call(
-        partial(backward_body, len(others), 0 if after is None else 1, first, loss_coef, prior is not None, math.gcd(unroll, size // TILE), piece_of(size, sub), dests),
+        partial(backward_body, len(others), 0 if after is None else 1, first, loss_coef, prior is not None, piece_of(size, unroll * TILE) // TILE, piece_of(size, sub), dests),
         in_specs=[whole] * (3 + len(others))
         + [whole] * 4
         + ([whole] * 3 if prior is not None else [])
@@ -294,7 +297,7 @@
         ],
         compiler_params=pltpu.CompilerParams(vmem_limit_bytes=VMEM_LIMIT),
         cost_estimate=pl.CostEstimate(
-            flops=COST * members * size * (width * (depth + 2 * variables) + count * TILE * variables * 3),
+            flops=int(COST_B * members * size * (width * (depth + 2 * variables) + count * TILE * variables * 3)),
             bytes_accessed=0,
             transcendentals=0,
         ),
@@ -302,7 +305,7 @@
     )(own, *others, targets, area, hidden, slope, latents, weight_out, *(prior or ()), *(() if after is None else (after,)))
 
 
-OFFSETS = ((2, 1), (3, 1), (2, 0), (3, 0), (1, 1), (1, 0), (0, 1))
+OFFSETS = ((1, 0), (2, 1), (2, 0), (3, 1), (3, 0), (1, 1), (0, 1))
 
 
 def spread_body(keep, arrived, mine, *parts):
@@ -399,7 +402,7 @@
     return lax.ppermute(block, ("pts", "mem"), pairs)
 
 
-CHUNKS = (256, 256, 256, 256)
+CHUNKS = (288, 288, 224, 224)
 
 
 def chunks_of(points):
@@ -432,8 +435,8 @@
     sums = []
     for k, (first, size) in enumerate(plan):
         held, hidden, slope = saved[k]
-        if k > LAG:
-            held[1] = tie(held[1], sums[k - LAG - 1])
+        if k and LAGS[k - 1] < k:
+            held[1] = tie(held[1], sums[k - 1 - LAGS[k - 1]])
         for bit in bits[1:]:
             held = held + [swap_members(v, bit) for v in held]
         last = first + size == points

time: 54.5 us -> 54 us (level)
  waiting for transfers between devices: 12 us -> 11.2 us
  transfers between devices with their start and end apart: 20 -> 20, of which waited for: 10 -> 7; matrix products, arithmetic and copies ran while one was open for 0% -> 0% of each run, Pallas kernels for 25% -> 26%
where the time goes in v6:
time: 54 us; the launch traced here: 53.9 us
  Pallas kernels  21.4 us (40%)
  starting transfers between devices  20.2 us (37%)
  waiting for transfers between devices  11.2 us (21%)
  between operations  0.78 us (1%)
    pallas_call x4, Pallas kernels, backward(): pl.pallas_call(partial(backward_body, len(others), 0 if after is None els...  11.7 us
    ppermute x7, starting transfers between devices, swap_points(): return lax.ppermute(block, ('pts', 'mem'), pairs)  11.1 us
    ppermute x13, starting transfers between devices, swap_members(): return lax.ppermute(block, 'mem', [(i, i ^ bit) for i in range(size)])  9.07 us
    pallas_call x4, Pallas kernels, forward(): pl.pallas_call(partial(forward_body, first, size, piece_of(size, sub), st...  8.76 us
    ppermute x13, waiting for transfers between devices, swap_members(): return lax.ppermute(block, 'mem', [(i, i ^ bit) for i in range(size)])  7.86 us
    ppermute x7, waiting for transfers between devices, swap_points(): return lax.ppermute(block, ('pts', 'mem'), pairs)  3.39 us
  transfers between devices with their start and end apart: 20, of which 7 were waited for; matrix products, arithmetic and copies ran while one was open for 0% of the time, Pallas kernels for 26%

profile of v6, /device:TPU:0, one launch (start us, length us, event | category | flops | bytes accessed | tf_op | source)
XLA Modules:
  0.0 53.9 jit_solution(14452932625489037133)
XLA Ops:
  0.6 3.8 %forward.4 = (bf16[4,288,128]{2,1,0:T(8,128)(2,1)S(1)}, bf16[4,288,512]{2,1,0:T(8,128)(2,1)S(1)}, f32[4,288,512]{2,1,0:T(8,128)S(1)}, f32[4,512]{1,0:T(4,128)S(1...) custom-call(s32[4]{0:T(128)} %refs_0_.1, f32[1,512]{1,0:T(1,128)} %bitcast.2, ...), custom_call_target="tpu_custom_call" | custom-call | flops 754974720 | tf_op jit(solution)/shard_map/forward/pallas_call | solution.py:141
  4.4 3.0 %collective-permute-start.4 = (bf16[4,288,128]{2,1,0:T(8,128)(2,1)S(1)}, bf16[4,288,128]{2,1,0:T(8,128)(2,1)S(1)}, u32[]{:S(2)}, u32[]{:S(2)}) collective-permute-start(bf16[4,288,128]{2,1,0:T(8,128)(2,1)S(1)} %get-tuple-element.41.refs_0_), channel_id=1, source_target_pairs={{0,2},{1,3},{2,0},{3,1},{4,6},{5,7},{6,4},{7,5},{8,10},{9,11},{10,... | collective-permute-start | bytes 884744 | tf_op jit(solution)/shard_map/ppermute | solution.py:392
  7.5 0.0 collective-permute-start.5
  7.5 1.9 %forward.5 = (bf16[4,288,128]{2,1,0:T(8,128)(2,1)S(1)}, bf16[4,288,512]{2,1,0:T(8,128)(2,1)S(1)}, f32[4,288,512]{2,1,0:T(8,128)S(1)}) custom-call(bf16[4,288,128]{2,1,0:T(8,128)(2,1)S(1)} %get-tuple-element.41.refs_0_, f32[4,512]{1,0:T(4,128)S(1)} %get-tuple-element.42.refs_1_, bf16[4,1024,512]{2,1,0:T(8,128)(2,1)S(1)} %get-tuple-element.43.refs_2_.refs_8_, ...), custom_call_target="tpu_custom_call" | custom-call | flops 754974720 | tf_op jit(solution)/shard_map/forward/pallas_call | solution.py:141
  9.3 0.2 collective-permute-start.1
  9.5 0.5 collective-permute-start.2
  10.0 5.3 %collective-permute-done.4.refs_1_ = bf16[4,288,128]{2,1,0:T(8,128)(2,1)S(1)} collective-permute-done((bf16[4,288,128]{2,1,0:T(8,128)(2,1)S(1)}, bf16[4,288,128]{2,1,0:T(8,128)(2,1)S(1)}, u32[]{:S(2)}, u32[]{:S(2)}) %collective-permute-start.4) | collective-permute-done | bytes 294944 | tf_op jit(solution)/shard_map/ppermute | solution.py:392
  15.3 0.0 collective-permute-start.6
  15.3 1.5 %forward.6 = (bf16[4,224,128]{2,1,0:T(8,128)(2,1)S(1)}, bf16[4,224,512]{2,1,0:T(8,128)(2,1)S(1)}, f32[4,224,512]{2,1,0:T(8,128)S(1)}) custom-call(bf16[4,288,128]{2,1,0:T(8,128)(2,1)S(1)} %get-tuple-element.46.refs_0_, f32[4,512]{1,0:T(4,128)S(1)} %get-tuple-element.42.refs_1_, bf16[4,1024,512]{2,1,0:T(8,128)(2,1)S(1)} %get-tuple-element.43.refs_2_.refs_8_, ...), custom_call_target="tpu_custom_call" | custom-call | flops 587202560 | tf_op jit(solution)/shard_map/forward/pallas_call | solution.py:141
  16.8 0.0 copy-start.1
  16.9 0.0 copy-start
  16.9 2.1 %collective-permute-start.9 = (bf16[4,224,128]{2,1,0:T(8,128)(2,1)S(1)}, bf16[4,224,128]{2,1,0:T(8,128)(2,1)S(1)}, u32[]{:S(2)}, u32[]{:S(2)}) collective-permute-start(bf16[4,224,128]{2,1,0:T(8,128)(2,1)S(1)} %get-tuple-element.47.refs_0_), channel_id=1, source_target_pairs={{0,2},{1,3},{2,0},{3,1},{4,6},{5,7},{6,4},{7,5},{8,10},{9,11},{10,... | collective-permute-start | bytes 688136 | tf_op jit(solution)/shard_map/ppermute | solution.py:392
  19.0 1.5 %forward.7 = (bf16[4,224,128]{2,1,0:T(8,128)(2,1)S(1)}, bf16[4,224,512]{2,1,0:T(8,128)(2,1)S(1)}, f32[4,224,512]{2,1,0:T(8,128)S(1)}) custom-call(bf16[4,224,128]{2,1,0:T(8,128)(2,1)S(1)} %get-tuple-element.47.refs_0_, f32[4,512]{1,0:T(4,128)S(1)} %get-tuple-element.42.refs_1_, bf16[4,1024,512]{2,1,0:T(8,128)(2,1)S(1)} %get-tuple-element.43.refs_2_.refs_8_, ...), custom_call_target="tpu_custom_call" | custom-call | flops 587202560 | tf_op jit(solution)/shard_map/forward/pallas_call | solution.py:141
  20.6 0.0 collective-permute-done.5.refs_2_
  20.6 0.3 collective-permute-start.10
  20.9 0.2 collective-permute-done.1.refs_1_
  21.1 1.7 %collective-permute-start = (bf16[4,224,128]{2,1,0:T(8,128)(2,1)S(1)}, bf16[4,224,128]{2,1,0:T(8,128)(2,1)S(1)}, u32[]{:S(2)}, u32[]{:S(2)}) collective-permute-start(bf16[4,224,128]{2,1,0:T(8,128)(2,1)S(1)} %get-tuple-element.48.refs_10_.refs_0_), channel_id=1, source_target_pairs={{0,2},{1,3},{2,0},{3,1},{4,6},{5,7},{6,4},{7,5},{8,10},{9,11},{10,... | collective-permute-start | bytes 688136 | tf_op jit(solution)/shard_map/ppermute | solution.py:392
  22.9 0.0 collective-permute-done.6.refs_3_
  22.9 0.0 collective-permute-start.3
  22.9 0.2 broadcast_in_dim.10.refs_5_
  23.1 3.3 %backward.4 = (f32[512,512]{1,0:T(8,128)S(1)}, f32[512,128]{1,0:T(8,128)S(1)}, f32[16,512]{1,0:T(8,128)S(1)}) custom-call(bf16[4,288,128]{2,1,0:T(8,128)(2,1)S(1)} %get-tuple-element.41.refs_0_, bf16[4,288,128]{2,1,0:T(8,128)(2,1)S(1)} %collective-permute-done.4.refs_1_, bf16[4,288,128]{2,1,0:T(8,128)(2,1)S(1)} %collective-permute-done.5.refs_2_, ...), custom_call_target="tpu_custom_call" | custom-call | flops 4529848320 | tf_op jit(solution)/shard_map/backward/pallas_call | solution.py:286
  26.4 0.0 collective-permute-done.9.value
  26.4 0.6 %collective-permute-start.7 = (bf16[4,224,128]{2,1,0:T(8,128)(2,1)S(1)}, bf16[4,224,128]{2,1,0:T(8,128)(2,1)S(1)}, u32[]{:S(2)}, u32[]{:S(2)}) collective-permute-start(bf16[4,224,128]{2,1,0:T(8,128)(2,1)S(1)} %get-tuple-element.48.refs_10_.refs_0_), channel_id=1, source_target_pairs={{0,1},{1,0},{2,3},{3,2},{4,5},{5,4},{6,7},{7,6},{8,9},{9,8},{10,11... | collective-permute-start | bytes 688136 | tf_op jit(solution)/shard_map/ppermute | solution.py:392
  26.9 0.0 collective-permute-done.2.refs_2_
  27.0 0.1 collective-permute-start.11
  27.0 0.0 collective-permute-done.3.refs_3_
  27.1 3.1 %backward.5 = (f32[512,512]{1,0:T(8,128)S(1)}, f32[512,128]{1,0:T(8,128)S(1)}, f32[16,512]{1,0:T(8,128)S(1)}) custom-call(bf16[4,288,128]{2,1,0:T(8,128)(2,1)S(1)} %get-tuple-element.46.refs_0_, bf16[4,288,128]{2,1,0:T(8,128)(2,1)S(1)} %collective-permute-done.1.refs_1_, bf16[4,288,128]{2,1,0:T(8,128)(2,1)S(1)} %collective-permute-done.2.refs_2_, ...), custom_call_target="tpu_custom_call" | custom-call | flops 4529848320 | tf_op jit(solution)/shard_map/backward/pallas_call | solution.py:286
  30.1 0.5 collective-permute-done.value
  30.6 0.0 collective-permute-start.8
  30.7 2.6 %backward.6 = (f32[512,512]{1,0:T(8,128)S(1)}, f32[512,128]{1,0:T(8,128)S(1)}, f32[16,512]{1,0:T(8,128)S(1)}) custom-call(bf16[4,224,128]{2,1,0:T(8,128)(2,1)S(1)} %get-tuple-element.47.refs_0_, bf16[4,224,128]{2,1,0:T(8,128)(2,1)S(1)} %tie.3.refs_1_, bf16[4,224,128]{2,1,0:T(8,128)(2,1)S(1)} %collective-permute-done.10.refs_2_, ...), custom_call_target="tpu_custom_call" | custom-call | flops 3523215360 | tf_op jit(solution)/shard_map/backward/pallas_call | solution.py:286
  33.3 2.8 %backward.7 = (f32[8,176,128]{2,1,0:T(8,128)S(1)}, f32[8,176,128]{2,1,0:T(8,128)S(1)}) custom-call(bf16[4,224,128]{2,1,0:T(8,128)(2,1)S(1)} %get-tuple-element.48.refs_10_.refs_0_, bf16[4,224,128]{2,1,0:T(8,128)(2,1)S(1)} %tie.2.refs_1_, bf16[4,224,128]{2,1,0:T(8,128)(2,1)S(1)} %collective-permute-done.7.refs_2_, ...), custom_call_target="tpu_custom_call" | custom-call | flops 3523215360 | tf_op jit(solution)/shard_map/backward/pallas_call | solution.py:286
  36.0 0.5 %collective-permute-start.12 = (f32[8,176,128]{2,1,0:T(8,128)S(1)}, f32[8,176,128]{2,1,0:T(8,128)S(1)}, u32[]{:S(2)}, u32[]{:S(2)}) collective-permute-start(f32[8,176,128]{2,1,0:T(8,128)S(1)} %get-tuple-element.67), channel_id=1, source_target_pairs={{0,1},{1,0},{2,3},{3,2},{4,5},{5,4},{6,7},{7,6},{8,9},{9,8},{10,11... | collective-permute-start | bytes 2162696 | tf_op jit(solution)/shard_map/ppermute | solution.py:392
  36.6 1.8 %collective-permute-done.12.arrived = f32[8,176,128]{2,1,0:T(8,128)S(1)} collective-permute-done((f32[8,176,128]{2,1,0:T(8,128)S(1)}, f32[8,176,128]{2,1,0:T(8,128)S(1)}, u32[]{:S(2)}, u32[]{:S(2)}) %collective-permute-start.12) | collective-permute-done | bytes 720928 | tf_op jit(solution)/shard_map/ppermute | solution.py:392
  38.4 0.1 spread_out.1
  38.5 1.9 %collective-permute-start.13 = (bf16[176,128]{1,0:T(8,128)(2,1)S(1)}, bf16[176,128]{1,0:T(8,128)(2,1)S(1)}, u32[]{:S(2)}, u32[]{:S(2)}) collective-permute-start(bf16[176,128]{1,0:T(8,128)(2,1)S(1)} %get-tuple-element.69), channel_id=1, source_target_pairs={{0,4},{1,5},{2,6},{3,7},{4,0},{5,1},{6,2},{7,3},{8,12},{9,13},{10,... | collective-permute-start | bytes 135176 | tf_op jit(solution)/shard_map/ppermute | solution.py:402
  40.4 3.5 %collective-permute-start.14 = (bf16[176,128]{1,0:T(8,128)(2,1)S(1)}, bf16[176,128]{1,0:T(8,128)(2,1)S(1)}, u32[]{:S(2)}, u32[]{:S(2)}) collective-permute-start(bf16[176,128]{1,0:T(8,128)(2,1)S(1)} %get-tuple-element.70), channel_id=1, source_target_pairs={{0,10},{1,11},{2,8},{3,9},{4,14},{5,15},{6,12},{7,13},{8,2},{9,3},... | collective-permute-start | bytes 135176 | tf_op jit(solution)/shard_map/ppermute | solution.py:402
  43.9 0.3 collective-permute-start.15
  44.2 2.4 %collective-permute-start.16 = (bf16[176,128]{1,0:T(8,128)(2,1)S(1)}, bf16[176,128]{1,0:T(8,128)(2,1)S(1)}, u32[]{:S(2)}, u32[]{:S(2)}) collective-permute-start(bf16[176,128]{1,0:T(8,128)(2,1)S(1)} %get-tuple-element.72), channel_id=1, source_target_pairs={{0,14},{1,15},{2,12},{3,13},{4,10},{5,11},{6,8},{7,9},{8,6},{9,7},... | collective-permute-start | bytes 135176 | tf_op jit(solution)/shard_map/ppermute | solution.py:402
  46.7 1.4 %collective-permute-start.17 = (bf16[176,128]{1,0:T(8,128)(2,1)S(1)}, bf16[176,128]{1,0:T(8,128)(2,1)S(1)}, u32[]{:S(2)}, u32[]{:S(2)}) collective-permute-start(bf16[176,128]{1,0:T(8,128)(2,1)S(1)} %get-tuple-element.73), channel_id=1, source_target_pairs={{0,12},{1,13},{2,14},{3,15},{4,8},{5,9},{6,10},{7,11},{8,4},{9,5},... | collective-permute-start | bytes 135176 | tf_op jit(solution)/shard_map/ppermute | solution.py:402
  48.0 0.0 collective-permute-done.13.refs_0_
  48.0 0.3 collective-permute-start.18
  48.3 0.0 collective-permute-done.14.refs_1_
  48.3 1.3 %collective-permute-start.19 = (bf16[176,128]{1,0:T(8,128)(2,1)S(1)}, bf16[176,128]{1,0:T(8,128)(2,1)S(1)}, u32[]{:S(2)}, u32[]{:S(2)}) collective-permute-start(bf16[176,128]{1,0:T(8,128)(2,1)S(1)} %get-tuple-element.75), channel_id=1, source_target_pairs={{0,2},{1,3},{2,0},{3,1},{4,6},{5,7},{6,4},{7,5},{8,10},{9,11},{10,... | collective-permute-start | bytes 135176 | tf_op jit(solution)/shard_map/ppermute | solution.py:402
  49.6 1.5 %collective-permute-done.15.refs_2_ = bf16[176,128]{1,0:T(8,128)(2,1)S(1)} collective-permute-done((bf16[176,128]{1,0:T(8,128)(2,1)S(1)}, bf16[176,128]{1,0:T(8,128)(2,1)S(1)}, u32[]{:S(2)}, u32[]{:S(2)}) %collective-permute-start.15) | collective-permute-done | bytes 45088 | tf_op jit(solution)/shard_map/ppermute | solution.py:402
  51.1 1.5 %collective-permute-done.17.refs_4_ = bf16[176,128]{1,0:T(8,128)(2,1)S(1)} collective-permute-done((bf16[176,128]{1,0:T(8,128)(2,1)S(1)}, bf16[176,128]{1,0:T(8,128)(2,1)S(1)}, u32[]{:S(2)}, u32[]{:S(2)}) %collective-permute-start.17) | collective-permute-done | bytes 45088 | tf_op jit(solution)/shard_map/ppermute | solution.py:402
  52.6 0.4 collective-permute-done.18.refs_5_
  53.0 0.0 collective-permute-done.19.refs_6_
  53.0 0.9 %finish.1 = (f32[32,512]{1,0:T(8,128)}, f32[32,128]{1,0:T(8,128)}, f32[1,32]{1,0:T(1,128)}) custom-call(f32[176,128]{1,0:T(8,128)S(1)} %get-tuple-element.68.mine, bf16[176,128]{1,0:T(8,128)(2,1)S(1)} %collective-permute-done.13.refs_0_, bf16[176,128]{1,0:T(8,128)(2,1)S(1)} %collective-permute-done.14.refs_1_, ...), custom_call_target="tpu_custom_call" | custom-call | tf_op jit(solution)/shard_map/finish/pallas_call | solution.py:355
  (10 shorter events, 0.1 us)
Async XLA Ops:
  4.4 10.8 %collective-permute-start.4 = (bf16[4,288,128]{2,1,0:T(8,128)(2,1)S(1)}, bf16[4,288,128]{2,1,0:T(8,128)(2,1)S(1)}, u32[]{:S(2)}, u32[]{:S(2)}) collective-permute-start(bf16[4,288,128]{2,1,0:T(8,128)(2,1)S(1)} %get-tuple-element.41.refs_0_), channel_id=1, source_target_pairs={{0,2},{1,3},{2,0},{3,1},{4,6},{5,7},{6,4},{7,5},{8,10},{9,11},{10,... | collective-permute-start | bytes 884744 | tf_op jit(solution)/shard_map/ppermute | solution.py:392
  7.5 13.2 %collective-permute-start.5 = (bf16[4,288,128]{2,1,0:T(8,128)(2,1)S(1)}, bf16[4,288,128]{2,1,0:T(8,128)(2,1)S(1)}, u32[]{:S(2)}, u32[]{:S(2)}) collective-permute-start(bf16[4,288,128]{2,1,0:T(8,128)(2,1)S(1)} %get-tuple-element.41.refs_0_), channel_id=1, source_target_pairs={{0,1},{1,0},{2,3},{3,2},{4,5},{5,4},{6,7},{7,6},{8,9},{9,8},{10,11... | collective-permute-start | bytes 884744 | tf_op jit(solution)/shard_map/ppermute | solution.py:392
  9.3 11.8 %collective-permute-start.1 = (bf16[4,288,128]{2,1,0:T(8,128)(2,1)S(1)}, bf16[4,288,128]{2,1,0:T(8,128)(2,1)S(1)}, u32[]{:S(2)}, u32[]{:S(2)}) collective-permute-start(bf16[4,288,128]{2,1,0:T(8,128)(2,1)S(1)} %get-tuple-element.46.refs_0_), channel_id=1, source_target_pairs={{0,2},{1,3},{2,0},{3,1},{4,6},{5,7},{6,4},{7,5},{8,10},{9,11},{10,... | collective-permute-start | bytes 884744 | tf_op jit(solution)/shard_map/ppermute | solution.py:392
  9.5 17.5 %collective-permute-start.2 = (bf16[4,288,128]{2,1,0:T(8,128)(2,1)S(1)}, bf16[4,288,128]{2,1,0:T(8,128)(2,1)S(1)}, u32[]{:S(2)}, u32[]{:S(2)}) collective-permute-start(bf16[4,288,128]{2,1,0:T(8,128)(2,1)S(1)} %get-tuple-element.46.refs_0_), channel_id=1, source_target_pairs={{0,1},{1,0},{2,3},{3,2},{4,5},{5,4},{6,7},{7,6},{8,9},{9,8},{10,11... | collective-permute-start | bytes 884744 | tf_op jit(solution)/shard_map/ppermute | solution.py:392
  15.3 7.6 %collective-permute-start.6 = (bf16[4,288,128]{2,1,0:T(8,128)(2,1)S(1)}, bf16[4,288,128]{2,1,0:T(8,128)(2,1)S(1)}, u32[]{:S(2)}, u32[]{:S(2)}) collective-permute-start(bf16[4,288,128]{2,1,0:T(8,128)(2,1)S(1)} %collective-permute-done.4.refs_1_), channel_id=1, source_target_pairs={{0,1},{1,0},{2,3},{3,2},{4,5},{5,4},{6,7},{7,6},{8,9},{9,8},{10,11... | collective-permute-start | bytes 884744 | tf_op jit(solution)/shard_map/ppermute | solution.py:392
  16.8 3.7 %copy-start.1 = (s32[1024]{0:T(1024)S(1)}, s32[1024]{0:T(1024)}, u32[]{:S(2)}) copy-start(s32[1024]{0:T(1024)} %param.10) | copy-start | bytes 12292
  16.9 6.2 %copy-start = (f32[1024,128]{1,0:T(8,128)S(1)}, f32[1024,128]{1,0:T(8,128)}, u32[]{:S(2)}) copy-start(f32[1024,128]{1,0:T(8,128)} %refs_4_.9) | copy-start | bytes 1572868
  16.9 9.5 %collective-permute-start.9 = (bf16[4,224,128]{2,1,0:T(8,128)(2,1)S(1)}, bf16[4,224,128]{2,1,0:T(8,128)(2,1)S(1)}, u32[]{:S(2)}, u32[]{:S(2)}) collective-permute-start(bf16[4,224,128]{2,1,0:T(8,128)(2,1)S(1)} %get-tuple-element.47.refs_0_), channel_id=1, source_target_pairs={{0,2},{1,3},{2,0},{3,1},{4,6},{5,7},{6,4},{7,5},{8,10},{9,11},{10,... | collective-permute-start | bytes 688136 | tf_op jit(solution)/shard_map/ppermute | solution.py:392
  20.6 10.0 %collective-permute-start.10 = (bf16[4,224,128]{2,1,0:T(8,128)(2,1)S(1)}, bf16[4,224,128]{2,1,0:T(8,128)(2,1)S(1)}, u32[]{:S(2)}, u32[]{:S(2)}) collective-permute-start(bf16[4,224,128]{2,1,0:T(8,128)(2,1)S(1)} %get-tuple-element.47.refs_0_), channel_id=1, source_target_pairs={{0,1},{1,0},{2,3},{3,2},{4,5},{5,4},{6,7},{7,6},{8,9},{9,8},{10,11... | collective-permute-start | bytes 688136 | tf_op jit(solution)/shard_map/ppermute | solution.py:392
  21.1 9.5 %collective-permute-start = (bf16[4,224,128]{2,1,0:T(8,128)(2,1)S(1)}, bf16[4,224,128]{2,1,0:T(8,128)(2,1)S(1)}, u32[]{:S(2)}, u32[]{:S(2)}) collective-permute-start(bf16[4,224,128]{2,1,0:T(8,128)(2,1)S(1)} %get-tuple-element.48.refs_10_.refs_0_), channel_id=1, source_target_pairs={{0,2},{1,3},{2,0},{3,1},{4,6},{5,7},{6,4},{7,5},{8,10},{9,11},{10,... | collective-permute-start | bytes 688136 | tf_op jit(solution)/shard_map/ppermute | solution.py:392
  22.9 4.2 %collective-permute-start.3 = (bf16[4,288,128]{2,1,0:T(8,128)(2,1)S(1)}, bf16[4,288,128]{2,1,0:T(8,128)(2,1)S(1)}, u32[]{:S(2)}, u32[]{:S(2)}) collective-permute-start(bf16[4,288,128]{2,1,0:T(8,128)(2,1)S(1)} %collective-permute-done.1.refs_1_), channel_id=1, source_target_pairs={{0,1},{1,0},{2,3},{3,2},{4,5},{5,4},{6,7},{7,6},{8,9},{9,8},{10,11... | collective-permute-start | bytes 884744 | tf_op jit(solution)/shard_map/ppermute | solution.py:392
  26.4 6.9 %collective-permute-start.7 = (bf16[4,224,128]{2,1,0:T(8,128)(2,1)S(1)}, bf16[4,224,128]{2,1,0:T(8,128)(2,1)S(1)}, u32[]{:S(2)}, u32[]{:S(2)}) collective-permute-start(bf16[4,224,128]{2,1,0:T(8,128)(2,1)S(1)} %get-tuple-element.48.refs_10_.refs_0_), channel_id=1, source_target_pairs={{0,1},{1,0},{2,3},{3,2},{4,5},{5,4},{6,7},{7,6},{8,9},{9,8},{10,11... | collective-permute-start | bytes 688136 | tf_op jit(solution)/shard_map/ppermute | solution.py:392
  27.0 3.7 %collective-permute-start.11 = (bf16[4,224,128]{2,1,0:T(8,128)(2,1)S(1)}, bf16[4,224,128]{2,1,0:T(8,128)(2,1)S(1)}, u32[]{:S(2)}, u32[]{:S(2)}) collective-permute-start(bf16[4,224,128]{2,1,0:T(8,128)(2,1)S(1)} %tie.3.refs_1_), channel_id=1, source_target_pairs={{0,1},{1,0},{2,3},{3,2},{4,5},{5,4},{6,7},{7,6},{8,9},{9,8},{10,11... | collective-permute-start | bytes 688136 | tf_op jit(solution)/shard_map/ppermute | solution.py:392
  30.6 2.6 %collective-permute-start.8 = (bf16[4,224,128]{2,1,0:T(8,128)(2,1)S(1)}, bf16[4,224,128]{2,1,0:T(8,128)(2,1)S(1)}, u32[]{:S(2)}, u32[]{:S(2)}) collective-permute-start(bf16[4,224,128]{2,1,0:T(8,128)(2,1)S(1)} %tie.2.refs_1_), channel_id=1, source_target_pairs={{0,1},{1,0},{2,3},{3,2},{4,5},{5,4},{6,7},{7,6},{8,9},{9,8},{10,11... | collective-permute-start | bytes 688136 | tf_op jit(solution)/shard_map/ppermute | solution.py:392
  36.0 2.4 %collective-permute-start.12 = (f32[8,176,128]{2,1,0:T(8,128)S(1)}, f32[8,176,128]{2,1,0:T(8,128)S(1)}, u32[]{:S(2)}, u32[]{:S(2)}) collective-permute-start(f32[8,176,128]{2,1,0:T(8,128)S(1)} %get-tuple-element.67), channel_id=1, source_target_pairs={{0,1},{1,0},{2,3},{3,2},{4,5},{5,4},{6,7},{7,6},{8,9},{9,8},{10,11... | collective-permute-start | bytes 2162696 | tf_op jit(solution)/shard_map/ppermute | solution.py:392
  38.5 9.6 %collective-permute-start.13 = (bf16[176,128]{1,0:T(8,128)(2,1)S(1)}, bf16[176,128]{1,0:T(8,128)(2,1)S(1)}, u32[]{:S(2)}, u32[]{:S(2)}) collective-permute-start(bf16[176,128]{1,0:T(8,128)(2,1)S(1)} %get-tuple-element.69), channel_id=1, source_target_pairs={{0,4},{1,5},{2,6},{3,7},{4,0},{5,1},{6,2},{7,3},{8,12},{9,13},{10,... | collective-permute-start | bytes 135176 | tf_op jit(solution)/shard_map/ppermute | solution.py:402
  40.4 7.9 %collective-permute-start.14 = (bf16[176,128]{1,0:T(8,128)(2,1)S(1)}, bf16[176,128]{1,0:T(8,128)(2,1)S(1)}, u32[]{:S(2)}, u32[]{:S(2)}) collective-permute-start(bf16[176,128]{1,0:T(8,128)(2,1)S(1)} %get-tuple-element.70), channel_id=1, source_target_pairs={{0,10},{1,11},{2,8},{3,9},{4,14},{5,15},{6,12},{7,13},{8,2},{9,3},... | collective-permute-start | bytes 135176 | tf_op jit(solution)/shard_map/ppermute | solution.py:402
  43.9 7.2 %collective-permute-start.15 = (bf16[176,128]{1,0:T(8,128)(2,1)S(1)}, bf16[176,128]{1,0:T(8,128)(2,1)S(1)}, u32[]{:S(2)}, u32[]{:S(2)}) collective-permute-start(bf16[176,128]{1,0:T(8,128)(2,1)S(1)} %get-tuple-element.71), channel_id=1, source_target_pairs={{0,8},{1,9},{2,10},{3,11},{4,12},{5,13},{6,14},{7,15},{8,0},{9,1},... | collective-permute-start | bytes 135176 | tf_op jit(solution)/shard_map/ppermute | solution.py:402
  44.2 6.9 %collective-permute-start.16 = (bf16[176,128]{1,0:T(8,128)(2,1)S(1)}, bf16[176,128]{1,0:T(8,128)(2,1)S(1)}, u32[]{:S(2)}, u32[]{:S(2)}) collective-permute-start(bf16[176,128]{1,0:T(8,128)(2,1)S(1)} %get-tuple-element.72), channel_id=1, source_target_pairs={{0,14},{1,15},{2,12},{3,13},{4,10},{5,11},{6,8},{7,9},{8,6},{9,7},... | collective-permute-start | bytes 135176 | tf_op jit(solution)/shard_map/ppermute | solution.py:402
  46.7 6.0 %collective-permute-start.17 = (bf16[176,128]{1,0:T(8,128)(2,1)S(1)}, bf16[176,128]{1,0:T(8,128)(2,1)S(1)}, u32[]{:S(2)}, u32[]{:S(2)}) collective-permute-start(bf16[176,128]{1,0:T(8,128)(2,1)S(1)} %get-tuple-element.73), channel_id=1, source_target_pairs={{0,12},{1,13},{2,14},{3,15},{4,8},{5,9},{6,10},{7,11},{8,4},{9,5},... | collective-permute-start | bytes 135176 | tf_op jit(solution)/shard_map/ppermute | solution.py:402
  48.0 5.0 %collective-permute-start.18 = (bf16[176,128]{1,0:T(8,128)(2,1)S(1)}, bf16[176,128]{1,0:T(8,128)(2,1)S(1)}, u32[]{:S(2)}, u32[]{:S(2)}) collective-permute-start(bf16[176,128]{1,0:T(8,128)(2,1)S(1)} %get-tuple-element.74), channel_id=1, source_target_pairs={{0,6},{1,7},{2,4},{3,5},{4,2},{5,3},{6,0},{7,1},{8,14},{9,15},{10,... | collective-permute-start | bytes 135176 | tf_op jit(solution)/shard_map/ppermute | solution.py:402
  48.3 4.7 %collective-permute-start.19 = (bf16[176,128]{1,0:T(8,128)(2,1)S(1)}, bf16[176,128]{1,0:T(8,128)(2,1)S(1)}, u32[]{:S(2)}, u32[]{:S(2)}) collective-permute-start(bf16[176,128]{1,0:T(8,128)(2,1)S(1)} %get-tuple-element.75), channel_id=1, source_target_pairs={{0,2},{1,3},{2,0},{3,1},{4,6},{5,7},{6,4},{7,5},{8,10},{9,11},{10,... | collective-permute-start | bytes 135176 | tf_op jit(solution)/shard_map/ppermute | solution.py:402

commit v7 on v6

--- a/solution.py
+++ b/solution.py
@@ -268,7 +268,7 @@
                 send[place] = block
 
 
-def backward(own, others, targets, area, hidden, slope, latents, weight_out, prior, first, loss_coef, dests=0, after=None, unroll=10, sub=256):
+def backward(own, others, targets, area, hidden, slope, latents, weight_out, prior, first, loss_coef, dests=0, after=None, unroll=18, sub=256):
     members, size, variables = own.shape
     depth = latents.shape[2]
     width = weight_out.shape[0]

time: 54 us -> 53.7 us (level)
  Pallas kernels: 21.4 us -> 20.6 us
  waiting for transfers between devices: 11.2 us -> 11.8 us
    pallas_call x4, Pallas kernels: 11.7 us -> 10.9 us  [backward(): pl.pallas_call(partial(backward_body, len(others), 0 if after is None els...]
  transfers between devices with their start and end apart: 20 -> 20, of which waited for: 7 -> 8; matrix products, arithmetic and copies ran while one was open for 0% -> 0% of each run, Pallas kernels for 26% -> 25%
where the time goes in v7:
time: 53.7 us; the launch traced here: 53.5 us
  Pallas kernels  20.6 us (38%)
  starting transfers between devices  20.1 us (37%)
  waiting for transfers between devices  11.8 us (22%)
  between operations  0.77 us (1%)
    ppermute x7, starting transfers between devices, swap_points(): return lax.ppermute(block, ('pts', 'mem'), pairs)  11.1 us
    pallas_call x4, Pallas kernels, backward(): pl.pallas_call(partial(backward_body, len(others), 0 if after is None els...  10.9 us
    ppermute x13, starting transfers between devices, swap_members(): return lax.ppermute(block, 'mem', [(i, i ^ bit) for i in range(size)])  8.95 us
    pallas_call x4, Pallas kernels, forward(): pl.pallas_call(partial(forward_body, first, size, piece_of(size, sub), st...  8.76 us
    ppermute x13, waiting for transfers between devices, swap_members(): return lax.ppermute(block, 'mem', [(i, i ^ bit) for i in range(size)])  8.36 us
    ppermute x7, waiting for transfers between devices, swap_points(): return lax.ppermute(block, ('pts', 'mem'), pairs)  3.4 us
  transfers between devices with their start and end apart: 20, of which 8 were waited for; matrix products, arithmetic and copies ran while one was open for 0% of the time, Pallas kernels for 25%

profile of v7, /device:TPU:0, one launch (start us, length us, event | category | flops | bytes accessed | tf_op | source)
XLA Modules:
  0.0 53.5 jit_solution(5903580761741443343)
XLA Ops:
  0.6 3.8 %forward.4 = (bf16[4,288,128]{2,1,0:T(8,128)(2,1)S(1)}, bf16[4,288,512]{2,1,0:T(8,128)(2,1)S(1)}, f32[4,288,512]{2,1,0:T(8,128)S(1)}, f32[4,512]{1,0:T(4,128)S(1...) custom-call(s32[4]{0:T(128)} %refs_0_.1, f32[1,512]{1,0:T(1,128)} %bitcast.2, ...), custom_call_target="tpu_custom_call" | custom-call | flops 754974720 | tf_op jit(solution)/shard_map/forward/pallas_call | solution.py:141
  4.4 3.0 %collective-permute-start.4 = (bf16[4,288,128]{2,1,0:T(8,128)(2,1)S(1)}, bf16[4,288,128]{2,1,0:T(8,128)(2,1)S(1)}, u32[]{:S(2)}, u32[]{:S(2)}) collective-permute-start(bf16[4,288,128]{2,1,0:T(8,128)(2,1)S(1)} %get-tuple-element.41.refs_0_), channel_id=1, source_target_pairs={{0,2},{1,3},{2,0},{3,1},{4,6},{5,7},{6,4},{7,5},{8,10},{9,11},{10,... | collective-permute-start | bytes 884744 | tf_op jit(solution)/shard_map/ppermute | solution.py:392
  7.5 0.0 collective-permute-start.5
  7.5 1.9 %forward.5 = (bf16[4,288,128]{2,1,0:T(8,128)(2,1)S(1)}, bf16[4,288,512]{2,1,0:T(8,128)(2,1)S(1)}, f32[4,288,512]{2,1,0:T(8,128)S(1)}) custom-call(bf16[4,288,128]{2,1,0:T(8,128)(2,1)S(1)} %get-tuple-element.41.refs_0_, f32[4,512]{1,0:T(4,128)S(1)} %get-tuple-element.42.refs_1_, bf16[4,1024,512]{2,1,0:T(8,128)(2,1)S(1)} %get-tuple-element.43.refs_2_.refs_8_, ...), custom_call_target="tpu_custom_call" | custom-call | flops 754974720 | tf_op jit(solution)/shard_map/forward/pallas_call | solution.py:141
  9.3 0.2 collective-permute-start.1
  9.5 0.5 collective-permute-start.2
  10.0 5.3 %collective-permute-done.4.refs_1_ = bf16[4,288,128]{2,1,0:T(8,128)(2,1)S(1)} collective-permute-done((bf16[4,288,128]{2,1,0:T(8,128)(2,1)S(1)}, bf16[4,288,128]{2,1,0:T(8,128)(2,1)S(1)}, u32[]{:S(2)}, u32[]{:S(2)}) %collective-permute-start.4) | collective-permute-done | bytes 294944 | tf_op jit(solution)/shard_map/ppermute | solution.py:392
  15.3 0.0 collective-permute-start.6
  15.3 1.5 %forward.6 = (bf16[4,224,128]{2,1,0:T(8,128)(2,1)S(1)}, bf16[4,224,512]{2,1,0:T(8,128)(2,1)S(1)}, f32[4,224,512]{2,1,0:T(8,128)S(1)}) custom-call(bf16[4,288,128]{2,1,0:T(8,128)(2,1)S(1)} %get-tuple-element.46.refs_0_, f32[4,512]{1,0:T(4,128)S(1)} %get-tuple-element.42.refs_1_, bf16[4,1024,512]{2,1,0:T(8,128)(2,1)S(1)} %get-tuple-element.43.refs_2_.refs_8_, ...), custom_call_target="tpu_custom_call" | custom-call | flops 587202560 | tf_op jit(solution)/shard_map/forward/pallas_call | solution.py:141
  16.8 0.0 copy-start.1
  16.9 0.0 copy-start
  16.9 2.1 %collective-permute-start.9 = (bf16[4,224,128]{2,1,0:T(8,128)(2,1)S(1)}, bf16[4,224,128]{2,1,0:T(8,128)(2,1)S(1)}, u32[]{:S(2)}, u32[]{:S(2)}) collective-permute-start(bf16[4,224,128]{2,1,0:T(8,128)(2,1)S(1)} %get-tuple-element.47.refs_0_), channel_id=1, source_target_pairs={{0,2},{1,3},{2,0},{3,1},{4,6},{5,7},{6,4},{7,5},{8,10},{9,11},{10,... | collective-permute-start | bytes 688136 | tf_op jit(solution)/shard_map/ppermute | solution.py:392
  19.0 1.5 %forward.7 = (bf16[4,224,128]{2,1,0:T(8,128)(2,1)S(1)}, bf16[4,224,512]{2,1,0:T(8,128)(2,1)S(1)}, f32[4,224,512]{2,1,0:T(8,128)S(1)}) custom-call(bf16[4,224,128]{2,1,0:T(8,128)(2,1)S(1)} %get-tuple-element.47.refs_0_, f32[4,512]{1,0:T(4,128)S(1)} %get-tuple-element.42.refs_1_, bf16[4,1024,512]{2,1,0:T(8,128)(2,1)S(1)} %get-tuple-element.43.refs_2_.refs_8_, ...), custom_call_target="tpu_custom_call" | custom-call | flops 587202560 | tf_op jit(solution)/shard_map/forward/pallas_call | solution.py:141
  20.6 0.0 collective-permute-done.5.refs_2_
  20.6 0.3 collective-permute-start.10
  20.9 0.2 collective-permute-done.1.refs_1_
  21.1 1.7 %collective-permute-start = (bf16[4,224,128]{2,1,0:T(8,128)(2,1)S(1)}, bf16[4,224,128]{2,1,0:T(8,128)(2,1)S(1)}, u32[]{:S(2)}, u32[]{:S(2)}) collective-permute-start(bf16[4,224,128]{2,1,0:T(8,128)(2,1)S(1)} %get-tuple-element.48.refs_10_.refs_0_), channel_id=1, source_target_pairs={{0,2},{1,3},{2,0},{3,1},{4,6},{5,7},{6,4},{7,5},{8,10},{9,11},{10,... | collective-permute-start | bytes 688136 | tf_op jit(solution)/shard_map/ppermute | solution.py:392
  22.9 0.0 collective-permute-done.6.refs_3_
  22.9 0.2 broadcast_in_dim.10.refs_5_
  23.1 2.9 %backward.4 = (f32[512,512]{1,0:T(8,128)S(1)}, f32[512,128]{1,0:T(8,128)S(1)}, f32[16,512]{1,0:T(8,128)S(1)}) custom-call(bf16[4,288,128]{2,1,0:T(8,128)(2,1)S(1)} %get-tuple-element.41.refs_0_, bf16[4,288,128]{2,1,0:T(8,128)(2,1)S(1)} %collective-permute-done.4.refs_1_, bf16[4,288,128]{2,1,0:T(8,128)(2,1)S(1)} %collective-permute-done.5.refs_2_, ...), custom_call_target="tpu_custom_call" | custom-call | flops 4529848320 | tf_op jit(solution)/shard_map/backward/pallas_call | solution.py:286
  26.0 0.1 collective-permute-done.9.value
  26.1 0.5 collective-permute-start.7
  26.5 0.0 collective-permute-done.2.refs_2_
  26.5 0.1 collective-permute-start.11
  26.6 0.0 collective-permute-done.3.refs_3_
  26.6 3.1 %backward.5 = (f32[512,512]{1,0:T(8,128)S(1)}, f32[512,128]{1,0:T(8,128)S(1)}, f32[16,512]{1,0:T(8,128)S(1)}) custom-call(bf16[4,288,128]{2,1,0:T(8,128)(2,1)S(1)} %get-tuple-element.46.refs_0_, bf16[4,288,128]{2,1,0:T(8,128)(2,1)S(1)} %collective-permute-done.1.refs_1_, bf16[4,288,128]{2,1,0:T(8,128)(2,1)S(1)} %collective-permute-done.2.refs_2_, ...), custom_call_target="tpu_custom_call" | custom-call | flops 4529848320 | tf_op jit(solution)/shard_map/backward/pallas_call | solution.py:286
  29.7 0.9 %collective-permute-done.value = bf16[4,224,128]{2,1,0:T(8,128)(2,1)S(1)} collective-permute-done((bf16[4,224,128]{2,1,0:T(8,128)(2,1)S(1)}, bf16[4,224,128]{2,1,0:T(8,128)(2,1)S(1)}, u32[]{:S(2)}, u32[]{:S(2)}) %collective-permute-start) | collective-permute-done | bytes 229408 | tf_op jit(solution)/shard_map/ppermute | solution.py:392
  30.6 0.0 collective-permute-done.11.refs_3_
  30.6 2.4 %backward.6 = (f32[512,512]{1,0:T(8,128)S(1)}, f32[512,128]{1,0:T(8,128)S(1)}, f32[16,512]{1,0:T(8,128)S(1)}) custom-call(bf16[4,224,128]{2,1,0:T(8,128)(2,1)S(1)} %get-tuple-element.47.refs_0_, bf16[4,224,128]{2,1,0:T(8,128)(2,1)S(1)} %tie.3.refs_1_, bf16[4,224,128]{2,1,0:T(8,128)(2,1)S(1)} %collective-permute-done.10.refs_2_, ...), custom_call_target="tpu_custom_call" | custom-call | flops 3523215360 | tf_op jit(solution)/shard_map/backward/pallas_call | solution.py:286
  33.1 0.0 collective-permute-done.8.refs_3_
  33.1 2.6 %backward.7 = (f32[8,176,128]{2,1,0:T(8,128)S(1)}, f32[8,176,128]{2,1,0:T(8,128)S(1)}) custom-call(bf16[4,224,128]{2,1,0:T(8,128)(2,1)S(1)} %get-tuple-element.48.refs_10_.refs_0_, bf16[4,224,128]{2,1,0:T(8,128)(2,1)S(1)} %tie.2.refs_1_, bf16[4,224,128]{2,1,0:T(8,128)(2,1)S(1)} %collective-permute-done.7.refs_2_, ...), custom_call_target="tpu_custom_call" | custom-call | flops 3523215360 | tf_op jit(solution)/shard_map/backward/pallas_call | solution.py:286
  35.6 0.6 %collective-permute-start.12 = (f32[8,176,128]{2,1,0:T(8,128)S(1)}, f32[8,176,128]{2,1,0:T(8,128)S(1)}, u32[]{:S(2)}, u32[]{:S(2)}) collective-permute-start(f32[8,176,128]{2,1,0:T(8,128)S(1)} %get-tuple-element.67), channel_id=1, source_target_pairs={{0,1},{1,0},{2,3},{3,2},{4,5},{5,4},{6,7},{7,6},{8,9},{9,8},{10,11... | collective-permute-start | bytes 2162696 | tf_op jit(solution)/shard_map/ppermute | solution.py:392
  36.2 1.8 %collective-permute-done.12.arrived = f32[8,176,128]{2,1,0:T(8,128)S(1)} collective-permute-done((f32[8,176,128]{2,1,0:T(8,128)S(1)}, f32[8,176,128]{2,1,0:T(8,128)S(1)}, u32[]{:S(2)}, u32[]{:S(2)}) %collective-permute-start.12) | collective-permute-done | bytes 720928 | tf_op jit(solution)/shard_map/ppermute | solution.py:392
  38.0 0.1 spread_out.1
  38.1 1.9 %collective-permute-start.13 = (bf16[176,128]{1,0:T(8,128)(2,1)S(1)}, bf16[176,128]{1,0:T(8,128)(2,1)S(1)}, u32[]{:S(2)}, u32[]{:S(2)}) collective-permute-start(bf16[176,128]{1,0:T(8,128)(2,1)S(1)} %get-tuple-element.69), channel_id=1, source_target_pairs={{0,4},{1,5},{2,6},{3,7},{4,0},{5,1},{6,2},{7,3},{8,12},{9,13},{10,... | collective-permute-start | bytes 135176 | tf_op jit(solution)/shard_map/ppermute | solution.py:402
  40.0 3.5 %collective-permute-start.14 = (bf16[176,128]{1,0:T(8,128)(2,1)S(1)}, bf16[176,128]{1,0:T(8,128)(2,1)S(1)}, u32[]{:S(2)}, u32[]{:S(2)}) collective-permute-start(bf16[176,128]{1,0:T(8,128)(2,1)S(1)} %get-tuple-element.70), channel_id=1, source_target_pairs={{0,10},{1,11},{2,8},{3,9},{4,14},{5,15},{6,12},{7,13},{8,2},{9,3},... | collective-permute-start | bytes 135176 | tf_op jit(solution)/shard_map/ppermute | solution.py:402
  43.5 0.3 collective-permute-start.15
  43.9 2.4 %collective-permute-start.16 = (bf16[176,128]{1,0:T(8,128)(2,1)S(1)}, bf16[176,128]{1,0:T(8,128)(2,1)S(1)}, u32[]{:S(2)}, u32[]{:S(2)}) collective-permute-start(bf16[176,128]{1,0:T(8,128)(2,1)S(1)} %get-tuple-element.72), channel_id=1, source_target_pairs={{0,14},{1,15},{2,12},{3,13},{4,10},{5,11},{6,8},{7,9},{8,6},{9,7},... | collective-permute-start | bytes 135176 | tf_op jit(solution)/shard_map/ppermute | solution.py:402
  46.3 1.4 %collective-permute-start.17 = (bf16[176,128]{1,0:T(8,128)(2,1)S(1)}, bf16[176,128]{1,0:T(8,128)(2,1)S(1)}, u32[]{:S(2)}, u32[]{:S(2)}) collective-permute-start(bf16[176,128]{1,0:T(8,128)(2,1)S(1)} %get-tuple-element.73), channel_id=1, source_target_pairs={{0,12},{1,13},{2,14},{3,15},{4,8},{5,9},{6,10},{7,11},{8,4},{9,5},... | collective-permute-start | bytes 135176 | tf_op jit(solution)/shard_map/ppermute | solution.py:402
  47.7 0.0 collective-permute-done.13.refs_0_
  47.7 0.3 collective-permute-start.18
  47.9 0.0 collective-permute-done.14.refs_1_
  47.9 1.3 %collective-permute-start.19 = (bf16[176,128]{1,0:T(8,128)(2,1)S(1)}, bf16[176,128]{1,0:T(8,128)(2,1)S(1)}, u32[]{:S(2)}, u32[]{:S(2)}) collective-permute-start(bf16[176,128]{1,0:T(8,128)(2,1)S(1)} %get-tuple-element.75), channel_id=1, source_target_pairs={{0,2},{1,3},{2,0},{3,1},{4,6},{5,7},{6,4},{7,5},{8,10},{9,11},{10,... | collective-permute-start | bytes 135176 | tf_op jit(solution)/shard_map/ppermute | solution.py:402
  49.2 1.5 %collective-permute-done.15.refs_2_ = bf16[176,128]{1,0:T(8,128)(2,1)S(1)} collective-permute-done((bf16[176,128]{1,0:T(8,128)(2,1)S(1)}, bf16[176,128]{1,0:T(8,128)(2,1)S(1)}, u32[]{:S(2)}, u32[]{:S(2)}) %collective-permute-start.15) | collective-permute-done | bytes 45088 | tf_op jit(solution)/shard_map/ppermute | solution.py:402
  50.8 1.5 %collective-permute-done.17.refs_4_ = bf16[176,128]{1,0:T(8,128)(2,1)S(1)} collective-permute-done((bf16[176,128]{1,0:T(8,128)(2,1)S(1)}, bf16[176,128]{1,0:T(8,128)(2,1)S(1)}, u32[]{:S(2)}, u32[]{:S(2)}) %collective-permute-start.17) | collective-permute-done | bytes 45088 | tf_op jit(solution)/shard_map/ppermute | solution.py:402
  52.3 0.4 collective-permute-done.18.refs_5_
  52.6 0.0 collective-permute-done.19.refs_6_
  52.6 0.9 %finish.1 = (f32[32,512]{1,0:T(8,128)}, f32[32,128]{1,0:T(8,128)}, f32[1,32]{1,0:T(1,128)}) custom-call(f32[176,128]{1,0:T(8,128)S(1)} %get-tuple-element.68.mine, bf16[176,128]{1,0:T(8,128)(2,1)S(1)} %collective-permute-done.13.refs_0_, bf16[176,128]{1,0:T(8,128)(2,1)S(1)} %collective-permute-done.14.refs_1_, ...), custom_call_target="tpu_custom_call" | custom-call | tf_op jit(solution)/shard_map/finish/pallas_call | solution.py:355
  (10 shorter events, 0.1 us)
Async XLA Ops:
  4.4 10.8 %collective-permute-start.4 = (bf16[4,288,128]{2,1,0:T(8,128)(2,1)S(1)}, bf16[4,288,128]{2,1,0:T(8,128)(2,1)S(1)}, u32[]{:S(2)}, u32[]{:S(2)}) collective-permute-start(bf16[4,288,128]{2,1,0:T(8,128)(2,1)S(1)} %get-tuple-element.41.refs_0_), channel_id=1, source_target_pairs={{0,2},{1,3},{2,0},{3,1},{4,6},{5,7},{6,4},{7,5},{8,10},{9,11},{10,... | collective-permute-start | bytes 884744 | tf_op jit(solution)/shard_map/ppermute | solution.py:392
  7.5 13.2 %collective-permute-start.5 = (bf16[4,288,128]{2,1,0:T(8,128)(2,1)S(1)}, bf16[4,288,128]{2,1,0:T(8,128)(2,1)S(1)}, u32[]{:S(2)}, u32[]{:S(2)}) collective-permute-start(bf16[4,288,128]{2,1,0:T(8,128)(2,1)S(1)} %get-tuple-element.41.refs_0_), channel_id=1, source_target_pairs={{0,1},{1,0},{2,3},{3,2},{4,5},{5,4},{6,7},{7,6},{8,9},{9,8},{10,11... | collective-permute-start | bytes 884744 | tf_op jit(solution)/shard_map/ppermute | solution.py:392
  9.3 11.8 %collective-permute-start.1 = (bf16[4,288,128]{2,1,0:T(8,128)(2,1)S(1)}, bf16[4,288,128]{2,1,0:T(8,128)(2,1)S(1)}, u32[]{:S(2)}, u32[]{:S(2)}) collective-permute-start(bf16[4,288,128]{2,1,0:T(8,128)(2,1)S(1)} %get-tuple-element.46.refs_0_), channel_id=1, source_target_pairs={{0,2},{1,3},{2,0},{3,1},{4,6},{5,7},{6,4},{7,5},{8,10},{9,11},{10,... | collective-permute-start | bytes 884744 | tf_op jit(solution)/shard_map/ppermute | solution.py:392
  9.5 17.1 %collective-permute-start.2 = (bf16[4,288,128]{2,1,0:T(8,128)(2,1)S(1)}, bf16[4,288,128]{2,1,0:T(8,128)(2,1)S(1)}, u32[]{:S(2)}, u32[]{:S(2)}) collective-permute-start(bf16[4,288,128]{2,1,0:T(8,128)(2,1)S(1)} %get-tuple-element.46.refs_0_), channel_id=1, source_target_pairs={{0,1},{1,0},{2,3},{3,2},{4,5},{5,4},{6,7},{7,6},{8,9},{9,8},{10,11... | collective-permute-start | bytes 884744 | tf_op jit(solution)/shard_map/ppermute | solution.py:392
  15.3 7.6 %collective-permute-start.6 = (bf16[4,288,128]{2,1,0:T(8,128)(2,1)S(1)}, bf16[4,288,128]{2,1,0:T(8,128)(2,1)S(1)}, u32[]{:S(2)}, u32[]{:S(2)}) collective-permute-start(bf16[4,288,128]{2,1,0:T(8,128)(2,1)S(1)} %collective-permute-done.4.refs_1_), channel_id=1, source_target_pairs={{0,1},{1,0},{2,3},{3,2},{4,5},{5,4},{6,7},{7,6},{8,9},{9,8},{10,11... | collective-permute-start | bytes 884744 | tf_op jit(solution)/shard_map/ppermute | solution.py:392
  16.8 3.7 %copy-start.1 = (s32[1024]{0:T(1024)S(1)}, s32[1024]{0:T(1024)}, u32[]{:S(2)}) copy-start(s32[1024]{0:T(1024)} %param.10) | copy-start | bytes 12292
  16.9 6.2 %copy-start = (f32[1024,128]{1,0:T(8,128)S(1)}, f32[1024,128]{1,0:T(8,128)}, u32[]{:S(2)}) copy-start(f32[1024,128]{1,0:T(8,128)} %refs_4_.9) | copy-start | bytes 1572868
  16.9 9.2 %collective-permute-start.9 = (bf16[4,224,128]{2,1,0:T(8,128)(2,1)S(1)}, bf16[4,224,128]{2,1,0:T(8,128)(2,1)S(1)}, u32[]{:S(2)}, u32[]{:S(2)}) collective-permute-start(bf16[4,224,128]{2,1,0:T(8,128)(2,1)S(1)} %get-tuple-element.47.refs_0_), channel_id=1, source_target_pairs={{0,2},{1,3},{2,0},{3,1},{4,6},{5,7},{6,4},{7,5},{8,10},{9,11},{10,... | collective-permute-start | bytes 688136 | tf_op jit(solution)/shard_map/ppermute | solution.py:392
  20.6 10.0 %collective-permute-start.10 = (bf16[4,224,128]{2,1,0:T(8,128)(2,1)S(1)}, bf16[4,224,128]{2,1,0:T(8,128)(2,1)S(1)}, u32[]{:S(2)}, u32[]{:S(2)}) collective-permute-start(bf16[4,224,128]{2,1,0:T(8,128)(2,1)S(1)} %get-tuple-element.47.refs_0_), channel_id=1, source_target_pairs={{0,1},{1,0},{2,3},{3,2},{4,5},{5,4},{6,7},{7,6},{8,9},{9,8},{10,11... | collective-permute-start | bytes 688136 | tf_op jit(solution)/shard_map/ppermute | solution.py:392
  21.1 9.5 %collective-permute-start = (bf16[4,224,128]{2,1,0:T(8,128)(2,1)S(1)}, bf16[4,224,128]{2,1,0:T(8,128)(2,1)S(1)}, u32[]{:S(2)}, u32[]{:S(2)}) collective-permute-start(bf16[4,224,128]{2,1,0:T(8,128)(2,1)S(1)} %get-tuple-element.48.refs_10_.refs_0_), channel_id=1, source_target_pairs={{0,2},{1,3},{2,0},{3,1},{4,6},{5,7},{6,4},{7,5},{8,10},{9,11},{10,... | collective-permute-start | bytes 688136 | tf_op jit(solution)/shard_map/ppermute | solution.py:392
  22.9 3.8 %collective-permute-start.3 = (bf16[4,288,128]{2,1,0:T(8,128)(2,1)S(1)}, bf16[4,288,128]{2,1,0:T(8,128)(2,1)S(1)}, u32[]{:S(2)}, u32[]{:S(2)}) collective-permute-start(bf16[4,288,128]{2,1,0:T(8,128)(2,1)S(1)} %collective-permute-done.1.refs_1_), channel_id=1, source_target_pairs={{0,1},{1,0},{2,3},{3,2},{4,5},{5,4},{6,7},{7,6},{8,9},{9,8},{10,11... | collective-permute-start | bytes 884744 | tf_op jit(solution)/shard_map/ppermute | solution.py:392
  26.1 7.0 %collective-permute-start.7 = (bf16[4,224,128]{2,1,0:T(8,128)(2,1)S(1)}, bf16[4,224,128]{2,1,0:T(8,128)(2,1)S(1)}, u32[]{:S(2)}, u32[]{:S(2)}) collective-permute-start(bf16[4,224,128]{2,1,0:T(8,128)(2,1)S(1)} %get-tuple-element.48.refs_10_.refs_0_), channel_id=1, source_target_pairs={{0,1},{1,0},{2,3},{3,2},{4,5},{5,4},{6,7},{7,6},{8,9},{9,8},{10,11... | collective-permute-start | bytes 688136 | tf_op jit(solution)/shard_map/ppermute | solution.py:392
  26.5 4.1 %collective-permute-start.11 = (bf16[4,224,128]{2,1,0:T(8,128)(2,1)S(1)}, bf16[4,224,128]{2,1,0:T(8,128)(2,1)S(1)}, u32[]{:S(2)}, u32[]{:S(2)}) collective-permute-start(bf16[4,224,128]{2,1,0:T(8,128)(2,1)S(1)} %tie.3.refs_1_), channel_id=1, source_target_pairs={{0,1},{1,0},{2,3},{3,2},{4,5},{5,4},{6,7},{7,6},{8,9},{9,8},{10,11... | collective-permute-start | bytes 688136 | tf_op jit(solution)/shard_map/ppermute | solution.py:392
  30.6 2.5 %collective-permute-start.8 = (bf16[4,224,128]{2,1,0:T(8,128)(2,1)S(1)}, bf16[4,224,128]{2,1,0:T(8,128)(2,1)S(1)}, u32[]{:S(2)}, u32[]{:S(2)}) collective-permute-start(bf16[4,224,128]{2,1,0:T(8,128)(2,1)S(1)} %tie.2.refs_1_), channel_id=1, source_target_pairs={{0,1},{1,0},{2,3},{3,2},{4,5},{5,4},{6,7},{7,6},{8,9},{9,8},{10,11... | collective-permute-start | bytes 688136 | tf_op jit(solution)/shard_map/ppermute | solution.py:392
  35.6 2.4 %collective-permute-start.12 = (f32[8,176,128]{2,1,0:T(8,128)S(1)}, f32[8,176,128]{2,1,0:T(8,128)S(1)}, u32[]{:S(2)}, u32[]{:S(2)}) collective-permute-start(f32[8,176,128]{2,1,0:T(8,128)S(1)} %get-tuple-element.67), channel_id=1, source_target_pairs={{0,1},{1,0},{2,3},{3,2},{4,5},{5,4},{6,7},{7,6},{8,9},{9,8},{10,11... | collective-permute-start | bytes 2162696 | tf_op jit(solution)/shard_map/ppermute | solution.py:392
  38.1 9.6 %collective-permute-start.13 = (bf16[176,128]{1,0:T(8,128)(2,1)S(1)}, bf16[176,128]{1,0:T(8,128)(2,1)S(1)}, u32[]{:S(2)}, u32[]{:S(2)}) collective-permute-start(bf16[176,128]{1,0:T(8,128)(2,1)S(1)} %get-tuple-element.69), channel_id=1, source_target_pairs={{0,4},{1,5},{2,6},{3,7},{4,0},{5,1},{6,2},{7,3},{8,12},{9,13},{10,... | collective-permute-start | bytes 135176 | tf_op jit(solution)/shard_map/ppermute | solution.py:402
  40.0 7.9 %collective-permute-start.14 = (bf16[176,128]{1,0:T(8,128)(2,1)S(1)}, bf16[176,128]{1,0:T(8,128)(2,1)S(1)}, u32[]{:S(2)}, u32[]{:S(2)}) collective-permute-start(bf16[176,128]{1,0:T(8,128)(2,1)S(1)} %get-tuple-element.70), channel_id=1, source_target_pairs={{0,10},{1,11},{2,8},{3,9},{4,14},{5,15},{6,12},{7,13},{8,2},{9,3},... | collective-permute-start | bytes 135176 | tf_op jit(solution)/shard_map/ppermute | solution.py:402
  43.5 7.2 %collective-permute-start.15 = (bf16[176,128]{1,0:T(8,128)(2,1)S(1)}, bf16[176,128]{1,0:T(8,128)(2,1)S(1)}, u32[]{:S(2)}, u32[]{:S(2)}) collective-permute-start(bf16[176,128]{1,0:T(8,128)(2,1)S(1)} %get-tuple-element.71), channel_id=1, source_target_pairs={{0,8},{1,9},{2,10},{3,11},{4,12},{5,13},{6,14},{7,15},{8,0},{9,1},... | collective-permute-start | bytes 135176 | tf_op jit(solution)/shard_map/ppermute | solution.py:402
  43.9 6.9 %collective-permute-start.16 = (bf16[176,128]{1,0:T(8,128)(2,1)S(1)}, bf16[176,128]{1,0:T(8,128)(2,1)S(1)}, u32[]{:S(2)}, u32[]{:S(2)}) collective-permute-start(bf16[176,128]{1,0:T(8,128)(2,1)S(1)} %get-tuple-element.72), channel_id=1, source_target_pairs={{0,14},{1,15},{2,12},{3,13},{4,10},{5,11},{6,8},{7,9},{8,6},{9,7},... | collective-permute-start | bytes 135176 | tf_op jit(solution)/shard_map/ppermute | solution.py:402
  46.3 5.9 %collective-permute-start.17 = (bf16[176,128]{1,0:T(8,128)(2,1)S(1)}, bf16[176,128]{1,0:T(8,128)(2,1)S(1)}, u32[]{:S(2)}, u32[]{:S(2)}) collective-permute-start(bf16[176,128]{1,0:T(8,128)(2,1)S(1)} %get-tuple-element.73), channel_id=1, source_target_pairs={{0,12},{1,13},{2,14},{3,15},{4,8},{5,9},{6,10},{7,11},{8,4},{9,5},... | collective-permute-start | bytes 135176 | tf_op jit(solution)/shard_map/ppermute | solution.py:402
  47.7 5.0 %collective-permute-start.18 = (bf16[176,128]{1,0:T(8,128)(2,1)S(1)}, bf16[176,128]{1,0:T(8,128)(2,1)S(1)}, u32[]{:S(2)}, u32[]{:S(2)}) collective-permute-start(bf16[176,128]{1,0:T(8,128)(2,1)S(1)} %get-tuple-element.74), channel_id=1, source_target_pairs={{0,6},{1,7},{2,4},{3,5},{4,2},{5,3},{6,0},{7,1},{8,14},{9,15},{10,... | collective-permute-start | bytes 135176 | tf_op jit(solution)/shard_map/ppermute | solution.py:402
  47.9 4.7 %collective-permute-start.19 = (bf16[176,128]{1,0:T(8,128)(2,1)S(1)}, bf16[176,128]{1,0:T(8,128)(2,1)S(1)}, u32[]{:S(2)}, u32[]{:S(2)}) collective-permute-start(bf16[176,128]{1,0:T(8,128)(2,1)S(1)} %get-tuple-element.75), channel_id=1, source_target_pairs={{0,2},{1,3},{2,0},{3,1},{4,6},{5,7},{6,4},{7,5},{8,10},{9,11},{10,... | collective-permute-start | bytes 135176 | tf_op jit(solution)/shard_map/ppermute | solution.py:402

commit v8 on v7

--- a/solution.py
+++ b/solution.py
@@ -265,10 +265,10 @@
 
             @pl.when(core != half)
             def _():
-                send[place] = block
-
-
-def backward(own, others, targets, area, hidden, slope, latents, weight_out, prior, first, loss_coef, dests=0, after=None, unroll=18, sub=256):
+                send[place] = block.astype(send.dtype)
+
+
+def backward(own, others, targets, area, hidden, slope, latents, weight_out, prior, first, loss_coef, dests=0, send_dtype=F32, after=None, unroll=18, sub=256):
     members, size, variables = own.shape
     depth = latents.shape[2]
     width = weight_out.shape[0]
@@ -276,7 +276,9 @@
     count = members * (1 + len(others))
     if dests:
         rows = depth // dests * (width // variables + 1) + TILE
-        shapes = [jax.ShapeDtypeStruct((dests // 2, rows, variables), F32)] * 2
+        shapes = [
+            jax.ShapeDtypeStruct((dests // 2, rows, variables), dtype) for dtype in (F32, send_dtype)
+        ]
     else:
         shapes = [
             jax.ShapeDtypeStruct((depth, width), F32),
@@ -308,27 +310,29 @@
 OFFSETS = ((1, 0), (2, 1), (2, 0), (3, 1), (3, 0), (1, 1), (0, 1))
 
 
-def spread_body(keep, arrived, mine, *parts):
+def spread_body(n_sums, *refs):
+    sums, (mine, *parts) = refs[:n_sums], refs[n_sums:]
     z, x = lax.axis_index("pts"), lax.axis_index("mem") >> 1
     here = z * 2 + x
-    mine[...] = keep[here] + arrived[here]
+    total = lambda place: sum(ref[place].astype(F32) for ref in sums)
+    mine[...] = total(here)
     for part, (dz, dx) in zip(parts, OFFSETS):
         there = (z ^ dz) * 2 + (x ^ dx)
-        part[...] = (keep[there] + arrived[there]).astype(part.dtype)
-
-
-def spread_out(keep, arrived, dtype):
-    _, rows, lanes = keep.shape
+        part[...] = total(there).astype(part.dtype)
+
+
+def spread_out(sums, dtype):
+    _, rows, lanes = sums[0].shape
     whole = pl.BlockSpec(memory_space=pltpu.VMEM)
     return pl.pallas_call(
-        spread_body,
-        in_specs=[whole, whole],
+        partial(spread_body, len(sums)),
+        in_specs=[whole] * len(sums),
         out_specs=[whole] * (1 + len(OFFSETS)),
         out_shape=[jax.ShapeDtypeStruct((rows, lanes), F32)]
         + [jax.ShapeDtypeStruct((rows, lanes), dtype)] * len(OFFSETS),
         compiler_params=pltpu.CompilerParams(vmem_limit_bytes=SMALL_LIMIT),
         name="spread_out",
-    )(keep, arrived)
+    )(*sums)
 
 
 def finish_body(share, mine, *refs):
@@ -440,10 +444,15 @@
         for bit in bits[1:]:
             held = held + [swap_members(v, bit) for v in held]
         last = first + size == points
+        split = packed and last and k > 0
+        if split:
+            early = total[0], swap_members(total[1], 1)
+        after = saved[-1][0][0] if k == 0 else total[0] if split else None
         total = list(backward(
-            held[0], held[1:], targets, area, hidden, slope, arrays[1], arrays[3], total,
-            first, loss_coef, dests if last and packed else 0,
-            after=saved[-1][0][0] if k == 0 else None,
+            held[0], held[1:], targets, area, hidden, slope, arrays[1], arrays[3],
+            None if split else total, first, loss_coef,
+            dests if packed and k >= len(plan) - 2 else 0,
+            LINK if last else F32, after=after,
         ))
         sums.append(total[-1])
     if not packed:
@@ -451,7 +460,7 @@
         return scatter(total[0]), scatter(total[1]), scatter(jnp.sum(total[2], axis=0))
     keep, send = total
     arrived = swap_members(send, 1)
-    mine, *parts = spread_out(keep, arrived, LINK)
+    mine, *parts = spread_out([*early, keep, arrived], LINK)
     parts = [swap_points(part, dz, dx) for part, (dz, dx) in zip(parts, OFFSETS)]
     in_share, out_share, bias_share = finish(mine, parts, depth // dests, width)
     return in_share, out_share, bias_share.reshape(depth // dests)

time: 53.7 us -> 53.8 us (level)
    ppermute x13 -> x14, waiting for transfers between devices: 8.36 us -> 8.15 us  [swap_members(): return lax.ppermute(block, 'mem', [(i, i ^ bit) for i in range(size)])]
    ppermute x13 -> x14, starting transfers between devices: 8.95 us -> 9.08 us  [swap_members(): return lax.ppermute(block, 'mem', [(i, i ^ bit) for i in range(size)])]
  transfers between devices with their start and end apart: 20 -> 21, of which waited for: 8 -> 9; matrix products, arithmetic and copies ran while one was open for 0% -> 0% of each run, Pallas kernels for 25% -> 30%
where the time goes in v8:
time: 53.8 us; the launch traced here: 53.6 us
  Pallas kernels  20.9 us (39%)
  starting transfers between devices  20.2 us (38%)
  waiting for transfers between devices  11.5 us (21%)
  between operations  0.76 us (1%)
    pallas_call x4, Pallas kernels, backward(): pl.pallas_call(partial(backward_body, len(others), 0 if after is None els...  11.1 us
    ppermute x7, starting transfers between devices, swap_points(): return lax.ppermute(block, ('pts', 'mem'), pairs)  11.1 us
    ppermute x14, starting transfers between devices, swap_members(): return lax.ppermute(block, 'mem', [(i, i ^ bit) for i in range(size)])  9.08 us
    pallas_call x4, Pallas kernels, forward(): pl.pallas_call(partial(forward_body, first, size, piece_of(size, sub), st...  8.76 us
    ppermute x14, waiting for transfers between devices, swap_members(): return lax.ppermute(block, 'mem', [(i, i ^ bit) for i in range(size)])  8.15 us
    ppermute x7, waiting for transfers between devices, swap_points(): return lax.ppermute(block, ('pts', 'mem'), pairs)  3.4 us
  transfers between devices with their start and end apart: 21, of which 9 were waited for; matrix products, arithmetic and copies ran while one was open for 0% of the time, Pallas kernels for 30%

profile of v8, /device:TPU:0, one launch (start us, length us, event | category | flops | bytes accessed | tf_op | source)
XLA Modules:
  0.0 53.6 jit_solution(1318566671099953528)
XLA Ops:
  0.6 3.8 %forward.4 = (bf16[4,288,128]{2,1,0:T(8,128)(2,1)S(1)}, bf16[4,288,512]{2,1,0:T(8,128)(2,1)S(1)}, f32[4,288,512]{2,1,0:T(8,128)S(1)}, f32[4,512]{1,0:T(4,128)S(1...) custom-call(s32[4]{0:T(128)} %refs_0_.1, f32[1,512]{1,0:T(1,128)} %bitcast.2, ...), custom_call_target="tpu_custom_call" | custom-call | flops 754974720 | tf_op jit(solution)/shard_map/forward/pallas_call | solution.py:141
  4.4 3.0 %collective-permute-start.1 = (bf16[4,288,128]{2,1,0:T(8,128)(2,1)S(1)}, bf16[4,288,128]{2,1,0:T(8,128)(2,1)S(1)}, u32[]{:S(2)}, u32[]{:S(2)}) collective-permute-start(bf16[4,288,128]{2,1,0:T(8,128)(2,1)S(1)} %get-tuple-element.40.refs_0_), channel_id=1, source_target_pairs={{0,2},{1,3},{2,0},{3,1},{4,6},{5,7},{6,4},{7,5},{8,10},{9,11},{10,... | collective-permute-start | bytes 884744 | tf_op jit(solution)/shard_map/ppermute | solution.py:396
  7.5 1.9 %forward.5 = (bf16[4,288,128]{2,1,0:T(8,128)(2,1)S(1)}, bf16[4,288,512]{2,1,0:T(8,128)(2,1)S(1)}, f32[4,288,512]{2,1,0:T(8,128)S(1)}) custom-call(bf16[4,288,128]{2,1,0:T(8,128)(2,1)S(1)} %get-tuple-element.40.refs_0_, f32[4,512]{1,0:T(4,128)S(1)} %get-tuple-element.41.refs_1_, bf16[4,1024,512]{2,1,0:T(8,128)(2,1)S(1)} %get-tuple-element.42.refs_2_.refs_8_, ...), custom_call_target="tpu_custom_call" | custom-call | flops 754974720 | tf_op jit(solution)/shard_map/forward/pallas_call | solution.py:141
  9.3 0.2 collective-permute-start.6
  9.5 0.5 collective-permute-start.7
  10.0 5.3 %collective-permute-done.1.refs_1_ = bf16[4,288,128]{2,1,0:T(8,128)(2,1)S(1)} collective-permute-done((bf16[4,288,128]{2,1,0:T(8,128)(2,1)S(1)}, bf16[4,288,128]{2,1,0:T(8,128)(2,1)S(1)}, u32[]{:S(2)}, u32[]{:S(2)}) %collective-permute-start.1) | collective-permute-done | bytes 294944 | tf_op jit(solution)/shard_map/ppermute | solution.py:396
  15.3 0.0 collective-permute-start.3
  15.3 1.5 %forward.6 = (bf16[4,224,128]{2,1,0:T(8,128)(2,1)S(1)}, bf16[4,224,512]{2,1,0:T(8,128)(2,1)S(1)}, f32[4,224,512]{2,1,0:T(8,128)S(1)}) custom-call(bf16[4,288,128]{2,1,0:T(8,128)(2,1)S(1)} %get-tuple-element.45.refs_0_, f32[4,512]{1,0:T(4,128)S(1)} %get-tuple-element.41.refs_1_, bf16[4,1024,512]{2,1,0:T(8,128)(2,1)S(1)} %get-tuple-element.42.refs_2_.refs_8_, ...), custom_call_target="tpu_custom_call" | custom-call | flops 587202560 | tf_op jit(solution)/shard_map/forward/pallas_call | solution.py:141
  16.8 0.0 copy-start.1
  16.9 0.0 copy-start
  16.9 2.1 %collective-permute-start = (bf16[4,224,128]{2,1,0:T(8,128)(2,1)S(1)}, bf16[4,224,128]{2,1,0:T(8,128)(2,1)S(1)}, u32[]{:S(2)}, u32[]{:S(2)}) collective-permute-start(bf16[4,224,128]{2,1,0:T(8,128)(2,1)S(1)} %get-tuple-element.46.refs_0_), channel_id=1, source_target_pairs={{0,2},{1,3},{2,0},{3,1},{4,6},{5,7},{6,4},{7,5},{8,10},{9,11},{10,... | collective-permute-start | bytes 688136 | tf_op jit(solution)/shard_map/ppermute | solution.py:396
  19.0 1.5 %forward.7 = (bf16[4,224,128]{2,1,0:T(8,128)(2,1)S(1)}, bf16[4,224,512]{2,1,0:T(8,128)(2,1)S(1)}, f32[4,224,512]{2,1,0:T(8,128)S(1)}) custom-call(bf16[4,224,128]{2,1,0:T(8,128)(2,1)S(1)} %get-tuple-element.46.refs_0_, f32[4,512]{1,0:T(4,128)S(1)} %get-tuple-element.41.refs_1_, bf16[4,1024,512]{2,1,0:T(8,128)(2,1)S(1)} %get-tuple-element.42.refs_2_.refs_8_, ...), custom_call_target="tpu_custom_call" | custom-call | flops 587202560 | tf_op jit(solution)/shard_map/forward/pallas_call | solution.py:141
  20.6 0.0 collective-permute-done.2.refs_2_
  20.6 0.3 collective-permute-start.4
  20.9 0.2 collective-permute-done.6.refs_1_
  21.1 1.7 %collective-permute-start.10 = (bf16[4,224,128]{2,1,0:T(8,128)(2,1)S(1)}, bf16[4,224,128]{2,1,0:T(8,128)(2,1)S(1)}, u32[]{:S(2)}, u32[]{:S(2)}) collective-permute-start(bf16[4,224,128]{2,1,0:T(8,128)(2,1)S(1)} %get-tuple-element.49.refs_10_.refs_0_), channel_id=1, source_target_pairs={{0,2},{1,3},{2,0},{3,1},{4,6},{5,7},{6,4},{7,5},{8,10},{9,11},{10,... | collective-permute-start | bytes 688136 | tf_op jit(solution)/shard_map/ppermute | solution.py:396
  22.9 0.0 collective-permute-done.3.refs_3_
  22.9 0.0 collective-permute-start.8
  22.9 0.2 broadcast_in_dim.10.refs_5_
  23.1 2.9 %backward.4 = (f32[512,512]{1,0:T(8,128)S(1)}, f32[512,128]{1,0:T(8,128)S(1)}, f32[16,512]{1,0:T(8,128)S(1)}) custom-call(bf16[4,288,128]{2,1,0:T(8,128)(2,1)S(1)} %get-tuple-element.40.refs_0_, bf16[4,288,128]{2,1,0:T(8,128)(2,1)S(1)} %collective-permute-done.1.refs_1_, bf16[4,288,128]{2,1,0:T(8,128)(2,1)S(1)} %collective-permute-done.2.refs_2_, ...), custom_call_target="tpu_custom_call" | custom-call | flops 4529848320 | tf_op jit(solution)/shard_map/backward/pallas_call | solution.py:288
  26.0 0.1 collective-permute-done.value
  26.1 0.5 collective-permute-start.11
  26.6 0.0 collective-permute-done.7.refs_2_
  26.6 0.1 collective-permute-start.5
  26.7 0.0 collective-permute-done.8.refs_3_
  26.7 3.1 %backward.5 = (f32[512,512]{1,0:T(8,128)S(1)}, f32[512,128]{1,0:T(8,128)S(1)}, f32[16,512]{1,0:T(8,128)S(1)}) custom-call(bf16[4,288,128]{2,1,0:T(8,128)(2,1)S(1)} %get-tuple-element.45.refs_0_, bf16[4,288,128]{2,1,0:T(8,128)(2,1)S(1)} %collective-permute-done.6.refs_1_, bf16[4,288,128]{2,1,0:T(8,128)(2,1)S(1)} %collective-permute-done.7.refs_2_, ...), custom_call_target="tpu_custom_call" | custom-call | flops 4529848320 | tf_op jit(solution)/shard_map/backward/pallas_call | solution.py:288
  29.8 0.8 %collective-permute-done.10.value = bf16[4,224,128]{2,1,0:T(8,128)(2,1)S(1)} collective-permute-done((bf16[4,224,128]{2,1,0:T(8,128)(2,1)S(1)}, bf16[4,224,128]{2,1,0:T(8,128)(2,1)S(1)}, u32[]{:S(2)}, u32[]{:S(2)}) %collective-permute-start.10) | collective-permute-done | bytes 229408 | tf_op jit(solution)/shard_map/ppermute | solution.py:396
  30.6 0.0 collective-permute-start.12
  30.6 0.0 collective-permute-done.4.refs_2_
  30.6 0.0 collective-permute-done.5.refs_3_
  30.6 2.6 %backward.6 = (f32[8,176,128]{2,1,0:T(8,128)S(1)}, f32[8,176,128]{2,1,0:T(8,128)S(1)}) custom-call(bf16[4,224,128]{2,1,0:T(8,128)(2,1)S(1)} %get-tuple-element.46.refs_0_, bf16[4,224,128]{2,1,0:T(8,128)(2,1)S(1)} %tie.2.refs_1_, bf16[4,224,128]{2,1,0:T(8,128)(2,1)S(1)} %collective-permute-done.4.refs_2_, ...), custom_call_target="tpu_custom_call" | custom-call | flops 3523215360 | tf_op jit(solution)/shard_map/backward/pallas_call | solution.py:288
  33.2 0.6 %collective-permute-start.9 = (f32[8,176,128]{2,1,0:T(8,128)S(1)}, f32[8,176,128]{2,1,0:T(8,128)S(1)}, u32[]{:S(2)}, u32[]{:S(2)}) collective-permute-start(f32[8,176,128]{2,1,0:T(8,128)S(1)} %get-tuple-element.61), channel_id=1, source_target_pairs={{0,1},{1,0},{2,3},{3,2},{4,5},{5,4},{6,7},{7,6},{8,9},{9,8},{10,11... | collective-permute-start | bytes 2162696 | tf_op jit(solution)/shard_map/ppermute | solution.py:396
  33.8 2.6 %backward.7 = (f32[8,176,128]{2,1,0:T(8,128)S(1)}, bf16[8,176,128]{2,1,0:T(8,128)(2,1)S(1)}) custom-call(bf16[4,224,128]{2,1,0:T(8,128)(2,1)S(1)} %get-tuple-element.49.refs_10_.refs_0_, bf16[4,224,128]{2,1,0:T(8,128)(2,1)S(1)} %tie.3.refs_1_, bf16[4,224,128]{2,1,0:T(8,128)(2,1)S(1)} %collective-permute-done.11.refs_2_, ...), custom_call_target="tpu_custom_call" | custom-call | flops 3523215360 | tf_op jit(solution)/shard_map/backward/pallas_call | solution.py:288
  36.3 0.1 collective-permute-start.13
  36.4 1.7 %collective-permute-done.13.refs_3_ = bf16[8,176,128]{2,1,0:T(8,128)(2,1)S(1)} collective-permute-done((bf16[8,176,128]{2,1,0:T(8,128)(2,1)S(1)}, bf16[8,176,128]{2,1,0:T(8,128)(2,1)S(1)}, u32[]{:S(2)}, u32[]{:S(2)}) %collective-permute-start.13) | collective-permute-done | bytes 360480 | tf_op jit(solution)/shard_map/ppermute | solution.py:396
  38.1 0.1 spread_out.1
  38.2 1.9 %collective-permute-start.14 = (bf16[176,128]{1,0:T(8,128)(2,1)S(1)}, bf16[176,128]{1,0:T(8,128)(2,1)S(1)}, u32[]{:S(2)}, u32[]{:S(2)}) collective-permute-start(bf16[176,128]{1,0:T(8,128)(2,1)S(1)} %get-tuple-element.67), channel_id=1, source_target_pairs={{0,4},{1,5},{2,6},{3,7},{4,0},{5,1},{6,2},{7,3},{8,12},{9,13},{10,... | collective-permute-start | bytes 135176 | tf_op jit(solution)/shard_map/ppermute | solution.py:406
  40.1 3.5 %collective-permute-start.15 = (bf16[176,128]{1,0:T(8,128)(2,1)S(1)}, bf16[176,128]{1,0:T(8,128)(2,1)S(1)}, u32[]{:S(2)}, u32[]{:S(2)}) collective-permute-start(bf16[176,128]{1,0:T(8,128)(2,1)S(1)} %get-tuple-element.68), channel_id=1, source_target_pairs={{0,10},{1,11},{2,8},{3,9},{4,14},{5,15},{6,12},{7,13},{8,2},{9,3},... | collective-permute-start | bytes 135176 | tf_op jit(solution)/shard_map/ppermute | solution.py:406
  43.6 0.3 collective-permute-start.16
  44.0 2.5 %collective-permute-start.17 = (bf16[176,128]{1,0:T(8,128)(2,1)S(1)}, bf16[176,128]{1,0:T(8,128)(2,1)S(1)}, u32[]{:S(2)}, u32[]{:S(2)}) collective-permute-start(bf16[176,128]{1,0:T(8,128)(2,1)S(1)} %get-tuple-element.70), channel_id=1, source_target_pairs={{0,14},{1,15},{2,12},{3,13},{4,10},{5,11},{6,8},{7,9},{8,6},{9,7},... | collective-permute-start | bytes 135176 | tf_op jit(solution)/shard_map/ppermute | solution.py:406
  46.4 1.3 %collective-permute-start.18 = (bf16[176,128]{1,0:T(8,128)(2,1)S(1)}, bf16[176,128]{1,0:T(8,128)(2,1)S(1)}, u32[]{:S(2)}, u32[]{:S(2)}) collective-permute-start(bf16[176,128]{1,0:T(8,128)(2,1)S(1)} %get-tuple-element.71), channel_id=1, source_target_pairs={{0,12},{1,13},{2,14},{3,15},{4,8},{5,9},{6,10},{7,11},{8,4},{9,5},... | collective-permute-start | bytes 135176 | tf_op jit(solution)/shard_map/ppermute | solution.py:406
  47.8 0.3 collective-permute-start.19
  48.0 1.3 %collective-permute-start.20 = (bf16[176,128]{1,0:T(8,128)(2,1)S(1)}, bf16[176,128]{1,0:T(8,128)(2,1)S(1)}, u32[]{:S(2)}, u32[]{:S(2)}) collective-permute-start(bf16[176,128]{1,0:T(8,128)(2,1)S(1)} %get-tuple-element.73), channel_id=1, source_target_pairs={{0,2},{1,3},{2,0},{3,1},{4,6},{5,7},{6,4},{7,5},{8,10},{9,11},{10,... | collective-permute-start | bytes 135176 | tf_op jit(solution)/shard_map/ppermute | solution.py:406
  49.3 1.3 %collective-permute-done.16.refs_2_ = bf16[176,128]{1,0:T(8,128)(2,1)S(1)} collective-permute-done((bf16[176,128]{1,0:T(8,128)(2,1)S(1)}, bf16[176,128]{1,0:T(8,128)(2,1)S(1)}, u32[]{:S(2)}, u32[]{:S(2)}) %collective-permute-start.16) | collective-permute-done | bytes 45088 | tf_op jit(solution)/shard_map/ppermute | solution.py:406
  50.7 0.1 collective-permute-done.17.refs_3_
  50.8 1.6 %collective-permute-done.18.refs_4_ = bf16[176,128]{1,0:T(8,128)(2,1)S(1)} collective-permute-done((bf16[176,128]{1,0:T(8,128)(2,1)S(1)}, bf16[176,128]{1,0:T(8,128)(2,1)S(1)}, u32[]{:S(2)}, u32[]{:S(2)}) %collective-permute-start.18) | collective-permute-done | bytes 45088 | tf_op jit(solution)/shard_map/ppermute | solution.py:406
  52.4 0.3 collective-permute-done.19.refs_5_
  52.7 0.9 %finish.1 = (f32[32,512]{1,0:T(8,128)}, f32[32,128]{1,0:T(8,128)}, f32[1,32]{1,0:T(1,128)}) custom-call(f32[176,128]{1,0:T(8,128)S(1)} %get-tuple-element.66.mine, bf16[176,128]{1,0:T(8,128)(2,1)S(1)} %collective-permute-done.14.refs_0_, bf16[176,128]{1,0:T(8,128)(2,1)S(1)} %collective-permute-done.15.refs_1_, ...), custom_call_target="tpu_custom_call" | custom-call | tf_op jit(solution)/shard_map/finish/pallas_call | solution.py:359
  (12 shorter events, 0.1 us)
Async XLA Ops:
  4.4 10.8 %collective-permute-start.1 = (bf16[4,288,128]{2,1,0:T(8,128)(2,1)S(1)}, bf16[4,288,128]{2,1,0:T(8,128)(2,1)S(1)}, u32[]{:S(2)}, u32[]{:S(2)}) collective-permute-start(bf16[4,288,128]{2,1,0:T(8,128)(2,1)S(1)} %get-tuple-element.40.refs_0_), channel_id=1, source_target_pairs={{0,2},{1,3},{2,0},{3,1},{4,6},{5,7},{6,4},{7,5},{8,10},{9,11},{10,... | collective-permute-start | bytes 884744 | tf_op jit(solution)/shard_map/ppermute | solution.py:396
  7.5 13.2 %collective-permute-start.2 = (bf16[4,288,128]{2,1,0:T(8,128)(2,1)S(1)}, bf16[4,288,128]{2,1,0:T(8,128)(2,1)S(1)}, u32[]{:S(2)}, u32[]{:S(2)}) collective-permute-start(bf16[4,288,128]{2,1,0:T(8,128)(2,1)S(1)} %get-tuple-element.40.refs_0_), channel_id=1, source_target_pairs={{0,1},{1,0},{2,3},{3,2},{4,5},{5,4},{6,7},{7,6},{8,9},{9,8},{10,11... | collective-permute-start | bytes 884744 | tf_op jit(solution)/shard_map/ppermute | solution.py:396
  9.3 11.8 %collective-permute-start.6 = (bf16[4,288,128]{2,1,0:T(8,128)(2,1)S(1)}, bf16[4,288,128]{2,1,0:T(8,128)(2,1)S(1)}, u32[]{:S(2)}, u32[]{:S(2)}) collective-permute-start(bf16[4,288,128]{2,1,0:T(8,128)(2,1)S(1)} %get-tuple-element.45.refs_0_), channel_id=1, source_target_pairs={{0,2},{1,3},{2,0},{3,1},{4,6},{5,7},{6,4},{7,5},{8,10},{9,11},{10,... | collective-permute-start | bytes 884744 | tf_op jit(solution)/shard_map/ppermute | solution.py:396
  9.5 17.1 %collective-permute-start.7 = (bf16[4,288,128]{2,1,0:T(8,128)(2,1)S(1)}, bf16[4,288,128]{2,1,0:T(8,128)(2,1)S(1)}, u32[]{:S(2)}, u32[]{:S(2)}) collective-permute-start(bf16[4,288,128]{2,1,0:T(8,128)(2,1)S(1)} %get-tuple-element.45.refs_0_), channel_id=1, source_target_pairs={{0,1},{1,0},{2,3},{3,2},{4,5},{5,4},{6,7},{7,6},{8,9},{9,8},{10,11... | collective-permute-start | bytes 884744 | tf_op jit(solution)/shard_map/ppermute | solution.py:396
  15.3 7.6 %collective-permute-start.3 = (bf16[4,288,128]{2,1,0:T(8,128)(2,1)S(1)}, bf16[4,288,128]{2,1,0:T(8,128)(2,1)S(1)}, u32[]{:S(2)}, u32[]{:S(2)}) collective-permute-start(bf16[4,288,128]{2,1,0:T(8,128)(2,1)S(1)} %collective-permute-done.1.refs_1_), channel_id=1, source_target_pairs={{0,1},{1,0},{2,3},{3,2},{4,5},{5,4},{6,7},{7,6},{8,9},{9,8},{10,11... | collective-permute-start | bytes 884744 | tf_op jit(solution)/shard_map/ppermute | solution.py:396
  16.8 3.7 %copy-start.1 = (s32[1024]{0:T(1024)S(1)}, s32[1024]{0:T(1024)}, u32[]{:S(2)}) copy-start(s32[1024]{0:T(1024)} %param.10) | copy-start | bytes 12292
  16.9 6.2 %copy-start = (f32[1024,128]{1,0:T(8,128)S(1)}, f32[1024,128]{1,0:T(8,128)}, u32[]{:S(2)}) copy-start(f32[1024,128]{1,0:T(8,128)} %refs_4_.9) | copy-start | bytes 1572868
  16.9 9.2 %collective-permute-start = (bf16[4,224,128]{2,1,0:T(8,128)(2,1)S(1)}, bf16[4,224,128]{2,1,0:T(8,128)(2,1)S(1)}, u32[]{:S(2)}, u32[]{:S(2)}) collective-permute-start(bf16[4,224,128]{2,1,0:T(8,128)(2,1)S(1)} %get-tuple-element.46.refs_0_), channel_id=1, source_target_pairs={{0,2},{1,3},{2,0},{3,1},{4,6},{5,7},{6,4},{7,5},{8,10},{9,11},{10,... | collective-permute-start | bytes 688136 | tf_op jit(solution)/shard_map/ppermute | solution.py:396
  20.6 10.0 %collective-permute-start.4 = (bf16[4,224,128]{2,1,0:T(8,128)(2,1)S(1)}, bf16[4,224,128]{2,1,0:T(8,128)(2,1)S(1)}, u32[]{:S(2)}, u32[]{:S(2)}) collective-permute-start(bf16[4,224,128]{2,1,0:T(8,128)(2,1)S(1)} %get-tuple-element.46.refs_0_), channel_id=1, source_target_pairs={{0,1},{1,0},{2,3},{3,2},{4,5},{5,4},{6,7},{7,6},{8,9},{9,8},{10,11... | collective-permute-start | bytes 688136 | tf_op jit(solution)/shard_map/ppermute | solution.py:396
  21.1 9.5 %collective-permute-start.10 = (bf16[4,224,128]{2,1,0:T(8,128)(2,1)S(1)}, bf16[4,224,128]{2,1,0:T(8,128)(2,1)S(1)}, u32[]{:S(2)}, u32[]{:S(2)}) collective-permute-start(bf16[4,224,128]{2,1,0:T(8,128)(2,1)S(1)} %get-tuple-element.49.refs_10_.refs_0_), channel_id=1, source_target_pairs={{0,2},{1,3},{2,0},{3,1},{4,6},{5,7},{6,4},{7,5},{8,10},{9,11},{10,... | collective-permute-start | bytes 688136 | tf_op jit(solution)/shard_map/ppermute | solution.py:396
  22.9 3.8 %collective-permute-start.8 = (bf16[4,288,128]{2,1,0:T(8,128)(2,1)S(1)}, bf16[4,288,128]{2,1,0:T(8,128)(2,1)S(1)}, u32[]{:S(2)}, u32[]{:S(2)}) collective-permute-start(bf16[4,288,128]{2,1,0:T(8,128)(2,1)S(1)} %collective-permute-done.6.refs_1_), channel_id=1, source_target_pairs={{0,1},{1,0},{2,3},{3,2},{4,5},{5,4},{6,7},{7,6},{8,9},{9,8},{10,11... | collective-permute-start | bytes 884744 | tf_op jit(solution)/shard_map/ppermute | solution.py:396
  26.1 7.7 %collective-permute-start.11 = (bf16[4,224,128]{2,1,0:T(8,128)(2,1)S(1)}, bf16[4,224,128]{2,1,0:T(8,128)(2,1)S(1)}, u32[]{:S(2)}, u32[]{:S(2)}) collective-permute-start(bf16[4,224,128]{2,1,0:T(8,128)(2,1)S(1)} %get-tuple-element.49.refs_10_.refs_0_), channel_id=1, source_target_pairs={{0,1},{1,0},{2,3},{3,2},{4,5},{5,4},{6,7},{7,6},{8,9},{9,8},{10,11... | collective-permute-start | bytes 688136 | tf_op jit(solution)/shard_map/ppermute | solution.py:396
  26.6 4.1 %collective-permute-start.5 = (bf16[4,224,128]{2,1,0:T(8,128)(2,1)S(1)}, bf16[4,224,128]{2,1,0:T(8,128)(2,1)S(1)}, u32[]{:S(2)}, u32[]{:S(2)}) collective-permute-start(bf16[4,224,128]{2,1,0:T(8,128)(2,1)S(1)} %tie.2.refs_1_), channel_id=1, source_target_pairs={{0,1},{1,0},{2,3},{3,2},{4,5},{5,4},{6,7},{7,6},{8,9},{9,8},{10,11... | collective-permute-start | bytes 688136 | tf_op jit(solution)/shard_map/ppermute | solution.py:396
  30.6 3.2 %collective-permute-start.12 = (bf16[4,224,128]{2,1,0:T(8,128)(2,1)S(1)}, bf16[4,224,128]{2,1,0:T(8,128)(2,1)S(1)}, u32[]{:S(2)}, u32[]{:S(2)}) collective-permute-start(bf16[4,224,128]{2,1,0:T(8,128)(2,1)S(1)} %tie.3.refs_1_), channel_id=1, source_target_pairs={{0,1},{1,0},{2,3},{3,2},{4,5},{5,4},{6,7},{7,6},{8,9},{9,8},{10,11... | collective-permute-start | bytes 688136 | tf_op jit(solution)/shard_map/ppermute | solution.py:396
  33.2 4.9 %collective-permute-start.9 = (f32[8,176,128]{2,1,0:T(8,128)S(1)}, f32[8,176,128]{2,1,0:T(8,128)S(1)}, u32[]{:S(2)}, u32[]{:S(2)}) collective-permute-start(f32[8,176,128]{2,1,0:T(8,128)S(1)} %get-tuple-element.61), channel_id=1, source_target_pairs={{0,1},{1,0},{2,3},{3,2},{4,5},{5,4},{6,7},{7,6},{8,9},{9,8},{10,11... | collective-permute-start | bytes 2162696 | tf_op jit(solution)/shard_map/ppermute | solution.py:396
  36.3 1.7 %collective-permute-start.13 = (bf16[8,176,128]{2,1,0:T(8,128)(2,1)S(1)}, bf16[8,176,128]{2,1,0:T(8,128)(2,1)S(1)}, u32[]{:S(2)}, u32[]{:S(2)}) collective-permute-start(bf16[8,176,128]{2,1,0:T(8,128)(2,1)S(1)} %get-tuple-element.65), channel_id=1, source_target_pairs={{0,1},{1,0},{2,3},{3,2},{4,5},{5,4},{6,7},{7,6},{8,9},{9,8},{10,11... | collective-permute-start | bytes 1081352 | tf_op jit(solution)/shard_map/ppermute | solution.py:396
  38.2 9.5 %collective-permute-start.14 = (bf16[176,128]{1,0:T(8,128)(2,1)S(1)}, bf16[176,128]{1,0:T(8,128)(2,1)S(1)}, u32[]{:S(2)}, u32[]{:S(2)}) collective-permute-start(bf16[176,128]{1,0:T(8,128)(2,1)S(1)} %get-tuple-element.67), channel_id=1, source_target_pairs={{0,4},{1,5},{2,6},{3,7},{4,0},{5,1},{6,2},{7,3},{8,12},{9,13},{10,... | collective-permute-start | bytes 135176 | tf_op jit(solution)/shard_map/ppermute | solution.py:406
  40.1 7.9 %collective-permute-start.15 = (bf16[176,128]{1,0:T(8,128)(2,1)S(1)}, bf16[176,128]{1,0:T(8,128)(2,1)S(1)}, u32[]{:S(2)}, u32[]{:S(2)}) collective-permute-start(bf16[176,128]{1,0:T(8,128)(2,1)S(1)} %get-tuple-element.68), channel_id=1, source_target_pairs={{0,10},{1,11},{2,8},{3,9},{4,14},{5,15},{6,12},{7,13},{8,2},{9,3},... | collective-permute-start | bytes 135176 | tf_op jit(solution)/shard_map/ppermute | solution.py:406
  43.6 7.0 %collective-permute-start.16 = (bf16[176,128]{1,0:T(8,128)(2,1)S(1)}, bf16[176,128]{1,0:T(8,128)(2,1)S(1)}, u32[]{:S(2)}, u32[]{:S(2)}) collective-permute-start(bf16[176,128]{1,0:T(8,128)(2,1)S(1)} %get-tuple-element.69), channel_id=1, source_target_pairs={{0,8},{1,9},{2,10},{3,11},{4,12},{5,13},{6,14},{7,15},{8,0},{9,1},... | collective-permute-start | bytes 135176 | tf_op jit(solution)/shard_map/ppermute | solution.py:406
  44.0 6.8 %collective-permute-start.17 = (bf16[176,128]{1,0:T(8,128)(2,1)S(1)}, bf16[176,128]{1,0:T(8,128)(2,1)S(1)}, u32[]{:S(2)}, u32[]{:S(2)}) collective-permute-start(bf16[176,128]{1,0:T(8,128)(2,1)S(1)} %get-tuple-element.70), channel_id=1, source_target_pairs={{0,14},{1,15},{2,12},{3,13},{4,10},{5,11},{6,8},{7,9},{8,6},{9,7},... | collective-permute-start | bytes 135176 | tf_op jit(solution)/shard_map/ppermute | solution.py:406
  46.4 6.0 %collective-permute-start.18 = (bf16[176,128]{1,0:T(8,128)(2,1)S(1)}, bf16[176,128]{1,0:T(8,128)(2,1)S(1)}, u32[]{:S(2)}, u32[]{:S(2)}) collective-permute-start(bf16[176,128]{1,0:T(8,128)(2,1)S(1)} %get-tuple-element.71), channel_id=1, source_target_pairs={{0,12},{1,13},{2,14},{3,15},{4,8},{5,9},{6,10},{7,11},{8,4},{9,5},... | collective-permute-start | bytes 135176 | tf_op jit(solution)/shard_map/ppermute | solution.py:406
  47.8 5.0 %collective-permute-start.19 = (bf16[176,128]{1,0:T(8,128)(2,1)S(1)}, bf16[176,128]{1,0:T(8,128)(2,1)S(1)}, u32[]{:S(2)}, u32[]{:S(2)}) collective-permute-start(bf16[176,128]{1,0:T(8,128)(2,1)S(1)} %get-tuple-element.72), channel_id=1, source_target_pairs={{0,6},{1,7},{2,4},{3,5},{4,2},{5,3},{6,0},{7,1},{8,14},{9,15},{10,... | collective-permute-start | bytes 135176 | tf_op jit(solution)/shard_map/ppermute | solution.py:406
  48.0 4.7 %collective-permute-start.20 = (bf16[176,128]{1,0:T(8,128)(2,1)S(1)}, bf16[176,128]{1,0:T(8,128)(2,1)S(1)}, u32[]{:S(2)}, u32[]{:S(2)}) collective-permute-start(bf16[176,128]{1,0:T(8,128)(2,1)S(1)} %get-tuple-element.73), channel_id=1, source_target_pairs={{0,2},{1,3},{2,0},{3,1},{4,6},{5,7},{6,4},{7,5},{8,10},{9,11},{10,... | collective-permute-start | bytes 135176 | tf_op jit(solution)/shard_map/ppermute | solution.py:406

commit v9 on v7

--- a/solution.py
+++ b/solution.py
@@ -402,7 +402,7 @@
     return lax.ppermute(block, ("pts", "mem"), pairs)
 
 
-CHUNKS = (288, 288, 224, 224)
+CHUNKS = (288, 288, 256, 192)
 
 
 def chunks_of(points):

time: 53.7 us -> 53.4 us (level)
  no operation moved by 1% of the time
where the time goes in v9:
time: 53.4 us; the launch traced here: 53.3 us
  Pallas kernels  20.5 us (38%)
  starting transfers between devices  20 us (37%)
  waiting for transfers between devices  11.8 us (22%)
  between operations  0.77 us (1%)
    ppermute x7, starting transfers between devices, swap_points(): return lax.ppermute(block, ('pts', 'mem'), pairs)  11.1 us
    pallas_call x4, Pallas kernels, backward(): pl.pallas_call(partial(backward_body, len(others), 0 if after is None els...  10.8 us
    ppermute x13, starting transfers between devices, swap_members(): return lax.ppermute(block, 'mem', [(i, i ^ bit) for i in range(size)])  8.9 us
    pallas_call x4, Pallas kernels, forward(): pl.pallas_call(partial(forward_body, first, size, piece_of(size, sub), st...  8.74 us
    ppermute x13, waiting for transfers between devices, swap_members(): return lax.ppermute(block, 'mem', [(i, i ^ bit) for i in range(size)])  8.38 us
    ppermute x7, waiting for transfers between devices, swap_points(): return lax.ppermute(block, ('pts', 'mem'), pairs)  3.39 us
  transfers between devices with their start and end apart: 20, of which 8 were waited for; matrix products, arithmetic and copies ran while one was open for 0% of the time, Pallas kernels for 25%

profile of v9, /device:TPU:0, one launch (start us, length us, event | category | flops | bytes accessed | tf_op | source)
XLA Modules:
  0.0 53.3 jit_solution(4743651164989246831)
XLA Ops:
  0.6 3.8 %forward.4 = (bf16[4,288,128]{2,1,0:T(8,128)(2,1)S(1)}, bf16[4,288,512]{2,1,0:T(8,128)(2,1)S(1)}, f32[4,288,512]{2,1,0:T(8,128)S(1)}, f32[4,512]{1,0:T(4,128)S(1...) custom-call(s32[4]{0:T(128)} %refs_0_.1, f32[1,512]{1,0:T(1,128)} %bitcast.2, ...), custom_call_target="tpu_custom_call" | custom-call | flops 754974720 | tf_op jit(solution)/shard_map/forward/pallas_call | solution.py:141
  4.4 3.0 %collective-permute-start.4 = (bf16[4,288,128]{2,1,0:T(8,128)(2,1)S(1)}, bf16[4,288,128]{2,1,0:T(8,128)(2,1)S(1)}, u32[]{:S(2)}, u32[]{:S(2)}) collective-permute-start(bf16[4,288,128]{2,1,0:T(8,128)(2,1)S(1)} %get-tuple-element.41.refs_0_), channel_id=1, source_target_pairs={{0,2},{1,3},{2,0},{3,1},{4,6},{5,7},{6,4},{7,5},{8,10},{9,11},{10,... | collective-permute-start | bytes 884744 | tf_op jit(solution)/shard_map/ppermute | solution.py:392
  7.5 0.0 collective-permute-start.5
  7.5 1.9 %forward.5 = (bf16[4,288,128]{2,1,0:T(8,128)(2,1)S(1)}, bf16[4,288,512]{2,1,0:T(8,128)(2,1)S(1)}, f32[4,288,512]{2,1,0:T(8,128)S(1)}) custom-call(bf16[4,288,128]{2,1,0:T(8,128)(2,1)S(1)} %get-tuple-element.41.refs_0_, f32[4,512]{1,0:T(4,128)S(1)} %get-tuple-element.42.refs_1_, bf16[4,1024,512]{2,1,0:T(8,128)(2,1)S(1)} %get-tuple-element.43.refs_2_.refs_8_, ...), custom_call_target="tpu_custom_call" | custom-call | flops 754974720 | tf_op jit(solution)/shard_map/forward/pallas_call | solution.py:141
  9.3 0.2 collective-permute-start.1
  9.5 0.5 collective-permute-start.2
  10.0 5.3 %collective-permute-done.4.refs_1_ = bf16[4,288,128]{2,1,0:T(8,128)(2,1)S(1)} collective-permute-done((bf16[4,288,128]{2,1,0:T(8,128)(2,1)S(1)}, bf16[4,288,128]{2,1,0:T(8,128)(2,1)S(1)}, u32[]{:S(2)}, u32[]{:S(2)}) %collective-permute-start.4) | collective-permute-done | bytes 294944 | tf_op jit(solution)/shard_map/ppermute | solution.py:392
  15.3 0.0 collective-permute-start.6
  15.3 1.7 %forward.6 = (bf16[4,256,128]{2,1,0:T(8,128)(2,1)S(1)}, bf16[4,256,512]{2,1,0:T(8,128)(2,1)S(1)}, f32[4,256,512]{2,1,0:T(8,128)S(1)}) custom-call(bf16[4,288,128]{2,1,0:T(8,128)(2,1)S(1)} %get-tuple-element.46.refs_0_, f32[4,512]{1,0:T(4,128)S(1)} %get-tuple-element.42.refs_1_, bf16[4,1024,512]{2,1,0:T(8,128)(2,1)S(1)} %get-tuple-element.43.refs_2_.refs_8_, ...), custom_call_target="tpu_custom_call" | custom-call | flops 671088640 | tf_op jit(solution)/shard_map/forward/pallas_call | solution.py:141
  17.0 0.0 copy-start.1
  17.0 0.0 copy-start
  17.1 2.1 %collective-permute-start.9 = (bf16[4,256,128]{2,1,0:T(8,128)(2,1)S(1)}, bf16[4,256,128]{2,1,0:T(8,128)(2,1)S(1)}, u32[]{:S(2)}, u32[]{:S(2)}) collective-permute-start(bf16[4,256,128]{2,1,0:T(8,128)(2,1)S(1)} %get-tuple-element.47.refs_0_), channel_id=1, source_target_pairs={{0,2},{1,3},{2,0},{3,1},{4,6},{5,7},{6,4},{7,5},{8,10},{9,11},{10,... | collective-permute-start | bytes 786440 | tf_op jit(solution)/shard_map/ppermute | solution.py:392
  19.2 1.4 %forward.7 = (bf16[4,192,128]{2,1,0:T(8,128)(2,1)S(1)}, bf16[4,192,512]{2,1,0:T(8,128)(2,1)S(1)}, f32[4,192,512]{2,1,0:T(8,128)S(1)}) custom-call(bf16[4,256,128]{2,1,0:T(8,128)(2,1)S(1)} %get-tuple-element.47.refs_0_, f32[4,512]{1,0:T(4,128)S(1)} %get-tuple-element.42.refs_1_, bf16[4,1024,512]{2,1,0:T(8,128)(2,1)S(1)} %get-tuple-element.43.refs_2_.refs_8_, ...), custom_call_target="tpu_custom_call" | custom-call | flops 503316480 | tf_op jit(solution)/shard_map/forward/pallas_call | solution.py:141
  20.6 0.0 collective-permute-done.5.refs_2_
  20.6 0.3 collective-permute-start.10
  20.9 0.1 collective-permute-done.1.refs_1_
  21.0 1.7 %collective-permute-start = (bf16[4,192,128]{2,1,0:T(8,128)(2,1)S(1)}, bf16[4,192,128]{2,1,0:T(8,128)(2,1)S(1)}, u32[]{:S(2)}, u32[]{:S(2)}) collective-permute-start(bf16[4,192,128]{2,1,0:T(8,128)(2,1)S(1)} %get-tuple-element.48.refs_10_.refs_0_), channel_id=1, source_target_pairs={{0,2},{1,3},{2,0},{3,1},{4,6},{5,7},{6,4},{7,5},{8,10},{9,11},{10,... | collective-permute-start | bytes 589832 | tf_op jit(solution)/shard_map/ppermute | solution.py:392
  22.7 0.0 collective-permute-done.6.refs_3_
  22.7 0.0 collective-permute-start.3
  22.7 0.2 broadcast_in_dim.10.refs_5_
  22.9 2.9 %backward.4 = (f32[512,512]{1,0:T(8,128)S(1)}, f32[512,128]{1,0:T(8,128)S(1)}, f32[16,512]{1,0:T(8,128)S(1)}) custom-call(bf16[4,288,128]{2,1,0:T(8,128)(2,1)S(1)} %get-tuple-element.41.refs_0_, bf16[4,288,128]{2,1,0:T(8,128)(2,1)S(1)} %collective-permute-done.4.refs_1_, bf16[4,288,128]{2,1,0:T(8,128)(2,1)S(1)} %collective-permute-done.5.refs_2_, ...), custom_call_target="tpu_custom_call" | custom-call | flops 4529848320 | tf_op jit(solution)/shard_map/backward/pallas_call | solution.py:286
  25.8 0.8 %collective-permute-done.9.value = bf16[4,256,128]{2,1,0:T(8,128)(2,1)S(1)} collective-permute-done((bf16[4,256,128]{2,1,0:T(8,128)(2,1)S(1)}, bf16[4,256,128]{2,1,0:T(8,128)(2,1)S(1)}, u32[]{:S(2)}, u32[]{:S(2)}) %collective-permute-start.9) | collective-permute-done | bytes 262176 | tf_op jit(solution)/shard_map/ppermute | solution.py:392
  26.6 0.0 collective-permute-start.7
  26.6 0.5 collective-permute-start.11
  27.1 3.1 %backward.5 = (f32[512,512]{1,0:T(8,128)S(1)}, f32[512,128]{1,0:T(8,128)S(1)}, f32[16,512]{1,0:T(8,128)S(1)}) custom-call(bf16[4,288,128]{2,1,0:T(8,128)(2,1)S(1)} %get-tuple-element.46.refs_0_, bf16[4,288,128]{2,1,0:T(8,128)(2,1)S(1)} %collective-permute-done.1.refs_1_, bf16[4,288,128]{2,1,0:T(8,128)(2,1)S(1)} %collective-permute-done.2.refs_2_, ...), custom_call_target="tpu_custom_call" | custom-call | flops 4529848320 | tf_op jit(solution)/shard_map/backward/pallas_call | solution.py:286
  30.2 0.4 collective-permute-done.value
  30.6 0.0 collective-permute-done.10.refs_2_
  30.6 0.0 collective-permute-done.11.refs_3_
  30.6 2.5 %backward.6 = (f32[512,512]{1,0:T(8,128)S(1)}, f32[512,128]{1,0:T(8,128)S(1)}, f32[16,512]{1,0:T(8,128)S(1)}) custom-call(bf16[4,256,128]{2,1,0:T(8,128)(2,1)S(1)} %get-tuple-element.47.refs_0_, bf16[4,256,128]{2,1,0:T(8,128)(2,1)S(1)} %tie.3.refs_1_, bf16[4,256,128]{2,1,0:T(8,128)(2,1)S(1)} %collective-permute-done.10.refs_2_, ...), custom_call_target="tpu_custom_call" | custom-call | flops 4026531840 | tf_op jit(solution)/shard_map/backward/pallas_call | solution.py:286
  33.2 2.2 %backward.7 = (f32[8,176,128]{2,1,0:T(8,128)S(1)}, f32[8,176,128]{2,1,0:T(8,128)S(1)}) custom-call(bf16[4,192,128]{2,1,0:T(8,128)(2,1)S(1)} %get-tuple-element.48.refs_10_.refs_0_, bf16[4,192,128]{2,1,0:T(8,128)(2,1)S(1)} %tie.2.refs_1_, bf16[4,192,128]{2,1,0:T(8,128)(2,1)S(1)} %collective-permute-done.7.refs_2_, ...), custom_call_target="tpu_custom_call" | custom-call | flops 3019898880 | tf_op jit(solution)/shard_map/backward/pallas_call | solution.py:286
  35.4 0.6 %collective-permute-start.12 = (f32[8,176,128]{2,1,0:T(8,128)S(1)}, f32[8,176,128]{2,1,0:T(8,128)S(1)}, u32[]{:S(2)}, u32[]{:S(2)}) collective-permute-start(f32[8,176,128]{2,1,0:T(8,128)S(1)} %get-tuple-element.67), channel_id=1, source_target_pairs={{0,1},{1,0},{2,3},{3,2},{4,5},{5,4},{6,7},{7,6},{8,9},{9,8},{10,11... | collective-permute-start | bytes 2162696 | tf_op jit(solution)/shard_map/ppermute | solution.py:392
  36.0 1.8 %collective-permute-done.12.arrived = f32[8,176,128]{2,1,0:T(8,128)S(1)} collective-permute-done((f32[8,176,128]{2,1,0:T(8,128)S(1)}, f32[8,176,128]{2,1,0:T(8,128)S(1)}, u32[]{:S(2)}, u32[]{:S(2)}) %collective-permute-start.12) | collective-permute-done | bytes 720928 | tf_op jit(solution)/shard_map/ppermute | solution.py:392
  37.8 0.1 spread_out.1
  37.9 1.9 %collective-permute-start.13 = (bf16[176,128]{1,0:T(8,128)(2,1)S(1)}, bf16[176,128]{1,0:T(8,128)(2,1)S(1)}, u32[]{:S(2)}, u32[]{:S(2)}) collective-permute-start(bf16[176,128]{1,0:T(8,128)(2,1)S(1)} %get-tuple-element.69), channel_id=1, source_target_pairs={{0,4},{1,5},{2,6},{3,7},{4,0},{5,1},{6,2},{7,3},{8,12},{9,13},{10,... | collective-permute-start | bytes 135176 | tf_op jit(solution)/shard_map/ppermute | solution.py:402
  39.8 3.5 %collective-permute-start.14 = (bf16[176,128]{1,0:T(8,128)(2,1)S(1)}, bf16[176,128]{1,0:T(8,128)(2,1)S(1)}, u32[]{:S(2)}, u32[]{:S(2)}) collective-permute-start(bf16[176,128]{1,0:T(8,128)(2,1)S(1)} %get-tuple-element.70), channel_id=1, source_target_pairs={{0,10},{1,11},{2,8},{3,9},{4,14},{5,15},{6,12},{7,13},{8,2},{9,3},... | collective-permute-start | bytes 135176 | tf_op jit(solution)/shard_map/ppermute | solution.py:402
  43.3 0.3 collective-permute-start.15
  43.7 2.4 %collective-permute-start.16 = (bf16[176,128]{1,0:T(8,128)(2,1)S(1)}, bf16[176,128]{1,0:T(8,128)(2,1)S(1)}, u32[]{:S(2)}, u32[]{:S(2)}) collective-permute-start(bf16[176,128]{1,0:T(8,128)(2,1)S(1)} %get-tuple-element.72), channel_id=1, source_target_pairs={{0,14},{1,15},{2,12},{3,13},{4,10},{5,11},{6,8},{7,9},{8,6},{9,7},... | collective-permute-start | bytes 135176 | tf_op jit(solution)/shard_map/ppermute | solution.py:402
  46.1 1.3 %collective-permute-start.17 = (bf16[176,128]{1,0:T(8,128)(2,1)S(1)}, bf16[176,128]{1,0:T(8,128)(2,1)S(1)}, u32[]{:S(2)}, u32[]{:S(2)}) collective-permute-start(bf16[176,128]{1,0:T(8,128)(2,1)S(1)} %get-tuple-element.73), channel_id=1, source_target_pairs={{0,12},{1,13},{2,14},{3,15},{4,8},{5,9},{6,10},{7,11},{8,4},{9,5},... | collective-permute-start | bytes 135176 | tf_op jit(solution)/shard_map/ppermute | solution.py:402
  47.4 0.0 collective-permute-done.13.refs_0_
  47.4 0.3 collective-permute-start.18
  47.7 0.0 collective-permute-done.14.refs_1_
  47.7 1.3 %collective-permute-start.19 = (bf16[176,128]{1,0:T(8,128)(2,1)S(1)}, bf16[176,128]{1,0:T(8,128)(2,1)S(1)}, u32[]{:S(2)}, u32[]{:S(2)}) collective-permute-start(bf16[176,128]{1,0:T(8,128)(2,1)S(1)} %get-tuple-element.75), channel_id=1, source_target_pairs={{0,2},{1,3},{2,0},{3,1},{4,6},{5,7},{6,4},{7,5},{8,10},{9,11},{10,... | collective-permute-start | bytes 135176 | tf_op jit(solution)/shard_map/ppermute | solution.py:402
  49.0 1.5 %collective-permute-done.15.refs_2_ = bf16[176,128]{1,0:T(8,128)(2,1)S(1)} collective-permute-done((bf16[176,128]{1,0:T(8,128)(2,1)S(1)}, bf16[176,128]{1,0:T(8,128)(2,1)S(1)}, u32[]{:S(2)}, u32[]{:S(2)}) %collective-permute-start.15) | collective-permute-done | bytes 45088 | tf_op jit(solution)/shard_map/ppermute | solution.py:402
  50.5 0.0 collective-permute-done.16.refs_3_
  50.5 1.5 %collective-permute-done.17.refs_4_ = bf16[176,128]{1,0:T(8,128)(2,1)S(1)} collective-permute-done((bf16[176,128]{1,0:T(8,128)(2,1)S(1)}, bf16[176,128]{1,0:T(8,128)(2,1)S(1)}, u32[]{:S(2)}, u32[]{:S(2)}) %collective-permute-start.17) | collective-permute-done | bytes 45088 | tf_op jit(solution)/shard_map/ppermute | solution.py:402
  52.0 0.4 collective-permute-done.18.refs_5_
  52.4 0.0 collective-permute-done.19.refs_6_
  52.4 0.9 %finish.1 = (f32[32,512]{1,0:T(8,128)}, f32[32,128]{1,0:T(8,128)}, f32[1,32]{1,0:T(1,128)}) custom-call(f32[176,128]{1,0:T(8,128)S(1)} %get-tuple-element.68.mine, bf16[176,128]{1,0:T(8,128)(2,1)S(1)} %collective-permute-done.13.refs_0_, bf16[176,128]{1,0:T(8,128)(2,1)S(1)} %collective-permute-done.14.refs_1_, ...), custom_call_target="tpu_custom_call" | custom-call | tf_op jit(solution)/shard_map/finish/pallas_call | solution.py:355
  (10 shorter events, 0.1 us)
Async XLA Ops:
  4.4 10.8 %collective-permute-start.4 = (bf16[4,288,128]{2,1,0:T(8,128)(2,1)S(1)}, bf16[4,288,128]{2,1,0:T(8,128)(2,1)S(1)}, u32[]{:S(2)}, u32[]{:S(2)}) collective-permute-start(bf16[4,288,128]{2,1,0:T(8,128)(2,1)S(1)} %get-tuple-element.41.refs_0_), channel_id=1, source_target_pairs={{0,2},{1,3},{2,0},{3,1},{4,6},{5,7},{6,4},{7,5},{8,10},{9,11},{10,... | collective-permute-start | bytes 884744 | tf_op jit(solution)/shard_map/ppermute | solution.py:392
  7.5 13.1 %collective-permute-start.5 = (bf16[4,288,128]{2,1,0:T(8,128)(2,1)S(1)}, bf16[4,288,128]{2,1,0:T(8,128)(2,1)S(1)}, u32[]{:S(2)}, u32[]{:S(2)}) collective-permute-start(bf16[4,288,128]{2,1,0:T(8,128)(2,1)S(1)} %get-tuple-element.41.refs_0_), channel_id=1, source_target_pairs={{0,1},{1,0},{2,3},{3,2},{4,5},{5,4},{6,7},{7,6},{8,9},{9,8},{10,11... | collective-permute-start | bytes 884744 | tf_op jit(solution)/shard_map/ppermute | solution.py:392
  9.3 11.6 %collective-permute-start.1 = (bf16[4,288,128]{2,1,0:T(8,128)(2,1)S(1)}, bf16[4,288,128]{2,1,0:T(8,128)(2,1)S(1)}, u32[]{:S(2)}, u32[]{:S(2)}) collective-permute-start(bf16[4,288,128]{2,1,0:T(8,128)(2,1)S(1)} %get-tuple-element.46.refs_0_), channel_id=1, source_target_pairs={{0,2},{1,3},{2,0},{3,1},{4,6},{5,7},{6,4},{7,5},{8,10},{9,11},{10,... | collective-permute-start | bytes 884744 | tf_op jit(solution)/shard_map/ppermute | solution.py:392
  9.5 17.1 %collective-permute-start.2 = (bf16[4,288,128]{2,1,0:T(8,128)(2,1)S(1)}, bf16[4,288,128]{2,1,0:T(8,128)(2,1)S(1)}, u32[]{:S(2)}, u32[]{:S(2)}) collective-permute-start(bf16[4,288,128]{2,1,0:T(8,128)(2,1)S(1)} %get-tuple-element.46.refs_0_), channel_id=1, source_target_pairs={{0,1},{1,0},{2,3},{3,2},{4,5},{5,4},{6,7},{7,6},{8,9},{9,8},{10,11... | collective-permute-start | bytes 884744 | tf_op jit(solution)/shard_map/ppermute | solution.py:392
  15.3 7.4 %collective-permute-start.6 = (bf16[4,288,128]{2,1,0:T(8,128)(2,1)S(1)}, bf16[4,288,128]{2,1,0:T(8,128)(2,1)S(1)}, u32[]{:S(2)}, u32[]{:S(2)}) collective-permute-start(bf16[4,288,128]{2,1,0:T(8,128)(2,1)S(1)} %collective-permute-done.4.refs_1_), channel_id=1, source_target_pairs={{0,1},{1,0},{2,3},{3,2},{4,5},{5,4},{6,7},{7,6},{8,9},{9,8},{10,11... | collective-permute-start | bytes 884744 | tf_op jit(solution)/shard_map/ppermute | solution.py:392
  17.0 3.5 %copy-start.1 = (s32[1024]{0:T(1024)S(1)}, s32[1024]{0:T(1024)}, u32[]{:S(2)}) copy-start(s32[1024]{0:T(1024)} %param.10) | copy-start | bytes 12292
  17.0 5.9 %copy-start = (f32[1024,128]{1,0:T(8,128)S(1)}, f32[1024,128]{1,0:T(8,128)}, u32[]{:S(2)}) copy-start(f32[1024,128]{1,0:T(8,128)} %refs_4_.9) | copy-start | bytes 1572868
  17.1 9.5 %collective-permute-start.9 = (bf16[4,256,128]{2,1,0:T(8,128)(2,1)S(1)}, bf16[4,256,128]{2,1,0:T(8,128)(2,1)S(1)}, u32[]{:S(2)}, u32[]{:S(2)}) collective-permute-start(bf16[4,256,128]{2,1,0:T(8,128)(2,1)S(1)} %get-tuple-element.47.refs_0_), channel_id=1, source_target_pairs={{0,2},{1,3},{2,0},{3,1},{4,6},{5,7},{6,4},{7,5},{8,10},{9,11},{10,... | collective-permute-start | bytes 786440 | tf_op jit(solution)/shard_map/ppermute | solution.py:392
  20.6 10.0 %collective-permute-start.10 = (bf16[4,256,128]{2,1,0:T(8,128)(2,1)S(1)}, bf16[4,256,128]{2,1,0:T(8,128)(2,1)S(1)}, u32[]{:S(2)}, u32[]{:S(2)}) collective-permute-start(bf16[4,256,128]{2,1,0:T(8,128)(2,1)S(1)} %get-tuple-element.47.refs_0_), channel_id=1, source_target_pairs={{0,1},{1,0},{2,3},{3,2},{4,5},{5,4},{6,7},{7,6},{8,9},{9,8},{10,11... | collective-permute-start | bytes 786440 | tf_op jit(solution)/shard_map/ppermute | solution.py:392
  21.0 9.7 %collective-permute-start = (bf16[4,192,128]{2,1,0:T(8,128)(2,1)S(1)}, bf16[4,192,128]{2,1,0:T(8,128)(2,1)S(1)}, u32[]{:S(2)}, u32[]{:S(2)}) collective-permute-start(bf16[4,192,128]{2,1,0:T(8,128)(2,1)S(1)} %get-tuple-element.48.refs_10_.refs_0_), channel_id=1, source_target_pairs={{0,2},{1,3},{2,0},{3,1},{4,6},{5,7},{6,4},{7,5},{8,10},{9,11},{10,... | collective-permute-start | bytes 589832 | tf_op jit(solution)/shard_map/ppermute | solution.py:392
  22.7 4.4 %collective-permute-start.3 = (bf16[4,288,128]{2,1,0:T(8,128)(2,1)S(1)}, bf16[4,288,128]{2,1,0:T(8,128)(2,1)S(1)}, u32[]{:S(2)}, u32[]{:S(2)}) collective-permute-start(bf16[4,288,128]{2,1,0:T(8,128)(2,1)S(1)} %collective-permute-done.1.refs_1_), channel_id=1, source_target_pairs={{0,1},{1,0},{2,3},{3,2},{4,5},{5,4},{6,7},{7,6},{8,9},{9,8},{10,11... | collective-permute-start | bytes 884744 | tf_op jit(solution)/shard_map/ppermute | solution.py:392
  26.6 6.6 %collective-permute-start.7 = (bf16[4,192,128]{2,1,0:T(8,128)(2,1)S(1)}, bf16[4,192,128]{2,1,0:T(8,128)(2,1)S(1)}, u32[]{:S(2)}, u32[]{:S(2)}) collective-permute-start(bf16[4,192,128]{2,1,0:T(8,128)(2,1)S(1)} %get-tuple-element.48.refs_10_.refs_0_), channel_id=1, source_target_pairs={{0,1},{1,0},{2,3},{3,2},{4,5},{5,4},{6,7},{7,6},{8,9},{9,8},{10,11... | collective-permute-start | bytes 589832 | tf_op jit(solution)/shard_map/ppermute | solution.py:392
  26.6 4.0 %collective-permute-start.11 = (bf16[4,256,128]{2,1,0:T(8,128)(2,1)S(1)}, bf16[4,256,128]{2,1,0:T(8,128)(2,1)S(1)}, u32[]{:S(2)}, u32[]{:S(2)}) collective-permute-start(bf16[4,256,128]{2,1,0:T(8,128)(2,1)S(1)} %tie.3.refs_1_), channel_id=1, source_target_pairs={{0,1},{1,0},{2,3},{3,2},{4,5},{5,4},{6,7},{7,6},{8,9},{9,8},{10,11... | collective-permute-start | bytes 786440 | tf_op jit(solution)/shard_map/ppermute | solution.py:392
  30.6 2.6 %collective-permute-start.8 = (bf16[4,192,128]{2,1,0:T(8,128)(2,1)S(1)}, bf16[4,192,128]{2,1,0:T(8,128)(2,1)S(1)}, u32[]{:S(2)}, u32[]{:S(2)}) collective-permute-start(bf16[4,192,128]{2,1,0:T(8,128)(2,1)S(1)} %tie.2.refs_1_), channel_id=1, source_target_pairs={{0,1},{1,0},{2,3},{3,2},{4,5},{5,4},{6,7},{7,6},{8,9},{9,8},{10,11... | collective-permute-start | bytes 589832 | tf_op jit(solution)/shard_map/ppermute | solution.py:392
  35.4 2.4 %collective-permute-start.12 = (f32[8,176,128]{2,1,0:T(8,128)S(1)}, f32[8,176,128]{2,1,0:T(8,128)S(1)}, u32[]{:S(2)}, u32[]{:S(2)}) collective-permute-start(f32[8,176,128]{2,1,0:T(8,128)S(1)} %get-tuple-element.67), channel_id=1, source_target_pairs={{0,1},{1,0},{2,3},{3,2},{4,5},{5,4},{6,7},{7,6},{8,9},{9,8},{10,11... | collective-permute-start | bytes 2162696 | tf_op jit(solution)/shard_map/ppermute | solution.py:392
  37.9 9.6 %collective-permute-start.13 = (bf16[176,128]{1,0:T(8,128)(2,1)S(1)}, bf16[176,128]{1,0:T(8,128)(2,1)S(1)}, u32[]{:S(2)}, u32[]{:S(2)}) collective-permute-start(bf16[176,128]{1,0:T(8,128)(2,1)S(1)} %get-tuple-element.69), channel_id=1, source_target_pairs={{0,4},{1,5},{2,6},{3,7},{4,0},{5,1},{6,2},{7,3},{8,12},{9,13},{10,... | collective-permute-start | bytes 135176 | tf_op jit(solution)/shard_map/ppermute | solution.py:402
  39.8 7.9 %collective-permute-start.14 = (bf16[176,128]{1,0:T(8,128)(2,1)S(1)}, bf16[176,128]{1,0:T(8,128)(2,1)S(1)}, u32[]{:S(2)}, u32[]{:S(2)}) collective-permute-start(bf16[176,128]{1,0:T(8,128)(2,1)S(1)} %get-tuple-element.70), channel_id=1, source_target_pairs={{0,10},{1,11},{2,8},{3,9},{4,14},{5,15},{6,12},{7,13},{8,2},{9,3},... | collective-permute-start | bytes 135176 | tf_op jit(solution)/shard_map/ppermute | solution.py:402
  43.3 7.2 %collective-permute-start.15 = (bf16[176,128]{1,0:T(8,128)(2,1)S(1)}, bf16[176,128]{1,0:T(8,128)(2,1)S(1)}, u32[]{:S(2)}, u32[]{:S(2)}) collective-permute-start(bf16[176,128]{1,0:T(8,128)(2,1)S(1)} %get-tuple-element.71), channel_id=1, source_target_pairs={{0,8},{1,9},{2,10},{3,11},{4,12},{5,13},{6,14},{7,15},{8,0},{9,1},... | collective-permute-start | bytes 135176 | tf_op jit(solution)/shard_map/ppermute | solution.py:402
  43.7 6.9 %collective-permute-start.16 = (bf16[176,128]{1,0:T(8,128)(2,1)S(1)}, bf16[176,128]{1,0:T(8,128)(2,1)S(1)}, u32[]{:S(2)}, u32[]{:S(2)}) collective-permute-start(bf16[176,128]{1,0:T(8,128)(2,1)S(1)} %get-tuple-element.72), channel_id=1, source_target_pairs={{0,14},{1,15},{2,12},{3,13},{4,10},{5,11},{6,8},{7,9},{8,6},{9,7},... | collective-permute-start | bytes 135176 | tf_op jit(solution)/shard_map/ppermute | solution.py:402
  46.1 6.0 %collective-permute-start.17 = (bf16[176,128]{1,0:T(8,128)(2,1)S(1)}, bf16[176,128]{1,0:T(8,128)(2,1)S(1)}, u32[]{:S(2)}, u32[]{:S(2)}) collective-permute-start(bf16[176,128]{1,0:T(8,128)(2,1)S(1)} %get-tuple-element.73), channel_id=1, source_target_pairs={{0,12},{1,13},{2,14},{3,15},{4,8},{5,9},{6,10},{7,11},{8,4},{9,5},... | collective-permute-start | bytes 135176 | tf_op jit(solution)/shard_map/ppermute | solution.py:402
  47.4 5.0 %collective-permute-start.18 = (bf16[176,128]{1,0:T(8,128)(2,1)S(1)}, bf16[176,128]{1,0:T(8,128)(2,1)S(1)}, u32[]{:S(2)}, u32[]{:S(2)}) collective-permute-start(bf16[176,128]{1,0:T(8,128)(2,1)S(1)} %get-tuple-element.74), channel_id=1, source_target_pairs={{0,6},{1,7},{2,4},{3,5},{4,2},{5,3},{6,0},{7,1},{8,14},{9,15},{10,... | collective-permute-start | bytes 135176 | tf_op jit(solution)/shard_map/ppermute | solution.py:402
  47.7 4.7 %collective-permute-start.19 = (bf16[176,128]{1,0:T(8,128)(2,1)S(1)}, bf16[176,128]{1,0:T(8,128)(2,1)S(1)}, u32[]{:S(2)}, u32[]{:S(2)}) collective-permute-start(bf16[176,128]{1,0:T(8,128)(2,1)S(1)} %get-tuple-element.75), channel_id=1, source_target_pairs={{0,2},{1,3},{2,0},{3,1},{4,6},{5,7},{6,4},{7,5},{8,10},{9,11},{10,... | collective-permute-start | bytes 135176 | tf_op jit(solution)/shard_map/ppermute | solution.py:402
